TPU v7x, 32 devices: a whole 2x2x4 slice. The times are simulated.
32 devices in a mesh: groups: 2 (over x), obs: 16 (over z, y, core).
Axes of the slice: x: 2, y: 2, z: 4, core: 2. Of those that a mesh axis runs over, the one named last changes fastest.
Arguments:
- footprints: float32 [512, 4, 128, 256], P(('groups', 'obs')), parts along dimension 0, may hold values from -0.1875 to 0.1875
- tile_index: int32 [512, 4], P(('groups', 'obs')), parts along dimension 0, may hold values from 0 to 511, as said below
- observed: float32 [512, 128], P(('groups', 'obs')), parts along dimension 0, may hold values from -6 to 6
- week_ids: int32 [512, 128], P(('groups', 'obs')), parts along dimension 0, may hold values from 0 to 7
- week_weight: float32 [16], P('groups'), parts along dimension 0, may hold values from 0.25 to 4
- counts: int32 [32], P(('groups', 'obs')), parts along dimension 0, may hold values from 1 to 2048, 16384 in all
- flux_start: float32 [1024, 256], P(('groups', 'obs')), parts along dimension 0, may hold values from -6 to 6
- flux_prior: float32 [1024, 256], P(('groups', 'obs')), parts along dimension 0, may hold values from -6 to 6
- prior_precision: float32 [1024, 256], P(('groups', 'obs')), parts along dimension 0, may hold values from 0.3 to 3
Outputs:
- flux: float32 [1024, 256], P(('groups', 'obs')), parts along dimension 0
- departure: float32 [512, 128], P(('groups', 'obs')), parts along dimension 0
There are 2 independent parts, one for each index of `groups`. A program takes and returns all parts, laid end to end along the dimension named above; each array names one. Nothing has to cross between parts.
Inputs may be any that keep to these rules, and one draw needn't show every extreme that they name: `tile_index`: for every device, the 64 tiles of its sounding blocks name flux blocks of any one device's share (blocks j * 32 to (j + 1) * 32 - 1) at most 8 times, and some share exactly 8 times. In each part of groups the counts sum to 16384, and the largest is 2048.
All inputs are finite; a program needn't handle non-finite values.
Results may differ from a plain program's by a relative error of at most 0.0001.
Values sent between devices are 32-bit elements; how exact they have to be, the bound alone decides.
No kernel may reach another device: no remote copies, remote signals or barrier semaphores. Data moves between devices by JAX's collectives and lax.ppermute only.
A program may use at most 64 MiB of HBM per device.

v0:
```python
import jax
import jax.numpy as jnp
from jax import lax
from jax.sharding import PartitionSpec as P

ITERS = 2


def body(
    footprints,
    tile_index,
    observed,
    week_ids,
    week_weight,
    counts,
    flux_start,
    flux_prior,
    prior_precision,
):
    shares = lax.axis_size("obs")
    my_index = lax.axis_index("obs")
    sound_blocks, tiles_each, tile_rows, tile_cols = footprints.shape
    flux_rows = flux_start.shape[0]
    positions = lax.broadcasted_iota(
        jnp.int32, (sound_blocks, tile_rows), 0
    ) * tile_rows + lax.broadcasted_iota(jnp.int32, (sound_blocks, tile_rows), 1)
    live_rows = (positions < counts[0]).astype(jnp.float32)
    week_table = (
        week_ids[:, :, None] == jnp.arange(week_weight.shape[0], dtype=jnp.int32)[None, None, :]
    ).astype(jnp.float32)
    weights = live_rows * jnp.sum(week_table * week_weight, axis=2)
    flat_ids = tile_index.reshape(-1)

    def forward(blocks):
        return jnp.einsum("bkrc,bkc->br", footprints, blocks, precision=lax.Precision.HIGHEST)

    def fetch_blocks(owned):
        gathered = lax.all_gather(owned, "obs", axis=0, tiled=True)
        return gathered[tile_index]

    flux = flux_start
    departure = forward(fetch_blocks(flux_start)) - observed
    for sweep in range(ITERS):
        adjoint_terms = jnp.einsum(
            "bkrc,br->bkc", footprints, weights * departure, precision=lax.Precision.HIGHEST
        ).reshape(-1, tile_cols)
        spread = (
            jnp.zeros((flux_rows * shares, tile_cols), jnp.float32).at[flat_ids].add(adjoint_terms)
        )
        summed = lax.psum(spread, "obs")
        gradient = lax.dynamic_slice_in_dim(
            summed, my_index * flux_rows, flux_rows, 0
        ) + prior_precision * (flux - flux_prior)
        grad_local = jnp.sum(gradient * gradient)
        prior_local = jnp.sum(prior_precision * gradient * gradient)
        grad_square, grad_prior = lax.psum((grad_local, prior_local), "obs")
        image = forward(fetch_blocks(gradient))
        fit_curve = lax.psum(jnp.sum(weights * image * image), "obs")
        step_size = grad_square / (fit_curve + grad_prior)
        flux = flux - step_size * gradient
        departure = departure - step_size * image
    return (flux, departure)


def solution(mesh):
    return jax.shard_map(
        body,
        mesh=mesh,
        in_specs=(
            P(("groups", "obs"), None, None, None),
            P(("groups", "obs"), None),
            P(("groups", "obs"), None),
            P(("groups", "obs"), None),
            P("groups"),
            P(("groups", "obs")),
            P(("groups", "obs"), None),
            P(("groups", "obs"), None),
            P(("groups", "obs"), None),
        ),
        out_specs=(P(("groups", "obs"), None), P(("groups", "obs"), None)),
        check_vma=False,
    )
```

profile of v0, /device:TPU:0, one launch (start us, length us, event | category | flops | bytes accessed | tf_op | source)
XLA Modules:
  0.0 378.7 jit_solution(17387452520989431928)
XLA Ops:
  7.2 0.7 compare_select_fusion
  7.9 0.8 copy.15
  9.6 24.8 %all_gather.9 = f32[512,256]{1,0:T(8,128)S(1)} all-gather(f32[32,256]{1,0:T(8,128)} %param.15), channel_id=1, replica_groups=mesh['groups'=2,'obs'=16] {'obs'}, dimensions={0}, use_global_device_ids=true | all-gather | bytes 557056 | tf_op jit(solution)/shard_map/all_gather | solution.py:38
  34.4 0.7 gather_fusion
  35.2 1.0 select_reduce_fusion
  36.1 10.1 %fusion.12 = f32[16,1,128,1]{2,1,3,0:T(1,128)S(1)} fusion(f32[16,4,256,1]{2,3,1,0:T(1,128)S(1)} %reshape.103, f32[16,4,128,256]{3,2,1,0:T(8,128)} %param.9), kind=kOutput, calls=%fused_computation.38 | convolution fusion | flops 25165824 | bytes 8462336 | tf_op jit(solution)/shard_map/bkrc,bkc->br/dot_general | solution.py:35
  46.3 4.0 %fusion.13 = f32[16,1,4,256]{3,1,2,0:T(1,128)S(1)} fusion(f32[16,128,1,1]{1,2,3,0:T(1,128)S(1)} %bitcast.46, f32[16,4,128,256]{3,2,1,0:T(8,128)S(1)} %copy-done), kind=kOutput, calls=%fused_computation.39 | convolution fusion | flops 25165824 | bytes 8462336 | tf_op jit(solution)/shard_map/bkrc,br->bkc/dot_general | solution.py:44
  50.4 1.7 scatter_custom_fusion
  52.2 87.5 %all-reduce.5.cloned.1.call-done = f32[512,256]{1,0:T(8,128)} async-done(((f32[512,256]{1,0:T(8,128)}), f32[512,256]{1,0:T(8,128)}) %all-reduce.5.cloned.1.call-update) | async-done | bytes 524304 | tf_op jit(solution)/shard_map/psum | solution.py:50
  139.7 1.5 fusion.4
  141.2 22.3 %all_gather.10 = f32[512,256]{1,0:T(8,128)S(1)} all-gather(f32[32,256]{1,0:T(8,128)S(1)} %get-tuple-element.11), channel_id=1, replica_groups=mesh['groups'=2,'obs'=16] {'obs'}, dimensions={0}, use_global_device_ids=true | all-gather | bytes 557056 | tf_op jit(solution)/shard_map/all_gather | solution.py:38
  163.4 0.7 gather_fusion.1
  164.2 9.2 %fusion.14 = f32[16,1,128,1]{2,1,3,0:T(1,128)S(1)} fusion(f32[16,4,256,1]{2,3,1,0:T(1,128)S(1)} %reshape.105, f32[16,4,128,256]{3,2,1,0:T(8,128)} %param.9), kind=kOutput, calls=%fused_computation.40 | convolution fusion | flops 25165824 | bytes 8462336 | tf_op jit(solution)/shard_map/bkrc,bkc->br/dot_general | solution.py:35
  173.4 0.8 fusion.6
  175.5 30.6 %all-reduce.1 = (f32[]{:T(128)}, f32[]{:T(128)}) all-reduce(f32[]{:T(128)} %get-tuple-element.5, f32[]{:T(128)S(6)} %add.60), channel_id=1, replica_groups=mesh['groups'=2,'obs'=16] {'obs'}, use_global_device_ids=true, to_apply=%region_4.0 | all-reduce | flops 2 | bytes 16 | tf_op jit(solution)/shard_map/psum | solution.py:56
  207.6 6.3 %fusion.15 = f32[16,1,4,256]{3,1,2,0:T(1,128)S(1)} fusion(f32[16,128,1,1]{1,2,3,0:T(1,128)S(1)} %bitcast.47, f32[16,4,128,256]{3,2,1,0:T(8,128)} %param.9), kind=kOutput, calls=%fused_computation.41 | convolution fusion | flops 25165824 | bytes 8462336 | tf_op jit(solution)/shard_map/bkrc,br->bkc/dot_general | solution.py:44
  214.0 1.7 scatter_custom_fusion.1
  215.7 87.4 %all-reduce.7.cloned.1.call-done = f32[512,256]{1,0:T(8,128)} async-done(((f32[512,256]{1,0:T(8,128)}), f32[512,256]{1,0:T(8,128)}) %all-reduce.7.cloned.1.call-update) | async-done | bytes 524304 | tf_op jit(solution)/shard_map/psum | solution.py:50
  303.1 1.5 fusion.5
  304.6 22.3 %all_gather.11 = f32[512,256]{1,0:T(8,128)S(1)} all-gather(f32[32,256]{1,0:T(8,128)S(1)} %get-tuple-element.10), channel_id=1, replica_groups=mesh['groups'=2,'obs'=16] {'obs'}, dimensions={0}, use_global_device_ids=true | all-gather | bytes 557056 | tf_op jit(solution)/shard_map/all_gather | solution.py:38
  326.9 0.7 gather_fusion.2
  327.6 9.2 %fusion.16 = f32[16,1,128,1]{2,1,3,0:T(1,128)S(1)} fusion(f32[16,4,256,1]{2,3,1,0:T(1,128)S(1)} %reshape.107, f32[16,4,128,256]{3,2,1,0:T(8,128)} %param.9), kind=kOutput, calls=%fused_computation.42 | convolution fusion | flops 25165824 | bytes 8462336 | tf_op jit(solution)/shard_map/bkrc,bkc->br/dot_general | solution.py:35
  336.8 0.8 fusion.7
  338.9 30.3 %all-reduce = (f32[]{:T(128)}, f32[]{:T(128)}) all-reduce(f32[]{:T(128)} %get-tuple-element.3, f32[]{:T(128)S(6)} %add.62), channel_id=1, replica_groups=mesh['groups'=2,'obs'=16] {'obs'}, use_global_device_ids=true, to_apply=%region_12.0 | all-reduce | flops 2 | bytes 16 | tf_op jit(solution)/shard_map/psum | solution.py:56
  (31 shorter events, 2.1 us)
Async XLA Ops:
  7.2 39.1 %copy-start.4 = (f32[16,128]{1,0:T(8,128)S(1)}, f32[16,128]{1,0:T(8,128)}, u32[]{:S(2)}) copy-start(f32[16,128]{1,0:T(8,128)} %param.11) | copy-start | bytes 24580
  7.2 132.5 %all-reduce.5.cloned.1.call-start = ((), (), s32[]{:S(2)}) async-start(), calls=%async_computation | async-start | bytes 1048576 | tf_op jit(solution)/shard_map/psum | solution.py:50
  35.1 11.2 %copy-start = (f32[16,4,128,256]{3,2,1,0:T(8,128)S(1)}, f32[16,4,128,256]{3,2,1,0:T(8,128)}, u32[]{:S(2)}) copy-start(f32[16,4,128,256]{3,2,1,0:T(8,128)} %param.9) | copy-start | bytes 25165828
  36.1 103.6 %copy-start.1 = (f32[32,256]{1,0:T(8,128)S(1)}, f32[32,256]{1,0:T(8,128)}, u32[]{:S(2)}) copy-start(f32[32,256]{1,0:T(8,128)} %param.15) | copy-start | bytes 98308
  36.1 103.6 %copy-start.2 = (f32[32,256]{1,0:T(8,128)S(1)}, f32[32,256]{1,0:T(8,128)}, u32[]{:S(2)}) copy-start(f32[32,256]{1,0:T(8,128)} %param.17) | copy-start | bytes 98308
  36.1 103.6 %copy-start.3 = (f32[32,256]{1,0:T(8,128)S(1)}, f32[32,256]{1,0:T(8,128)}, u32[]{:S(2)}) copy-start(f32[32,256]{1,0:T(8,128)} %param.16) | copy-start | bytes 98308
  52.2 251.0 %all-reduce.7.cloned.1.call-start = ((), (), s32[]{:S(2)}) async-start(), calls=%async_computation.1 | async-start | bytes 1048576 | tf_op jit(solution)/shard_map/psum | solution.py:50
Sparse Core Ops, SparseCore 0:
  52.3 87.3 all-reduce.4
  215.8 87.2 all-reduce.6
where the time goes:
time: 379 us
  waiting for transfers between devices  175 us (46%)
  blocking collectives  130 us (34%)
  matrix products  38.9 us (10%)
  between operations  20.2 us (5%)
  other arithmetic  11 us (3%)
    psum x2, waiting for transfers between devices, body(): summed = lax.psum(spread, 'obs')  175 us
    all_gather x3, blocking collectives, fetch_blocks(): gathered = lax.all_gather(owned, 'obs', axis=0, tiled=True)  69.3 us
    psum x2, blocking collectives, body(): grad_square, grad_prior = lax.psum((grad_local, prior_local), 'obs')  60.9 us
    dot_general x3, matrix products, forward(): jnp.einsum('bkrc,bkc->br', footprints, blocks, precision=lax.Precision.HI...  28.5 us
    dot_general x2, matrix products, body(): jnp.einsum('bkrc,br->bkc', footprints, weights * departure, precision=lax...  10.4 us
  transfers between devices with their start and end apart: 2, of which 2 were waited for; matrix products, arithmetic and copies ran while one was open for 0% of the time, Pallas kernels for 0%

commit v1 on v0

v1 whole, which is shorter than its diff:
```python
import functools

import jax
import jax.numpy as jnp
from jax import lax
from jax.experimental import pallas as pl
from jax.experimental.pallas import tpu as pltpu
from jax.sharding import PartitionSpec as P

VMEM = pl.BlockSpec(memory_space=pltpu.VMEM)
SMEM = pl.BlockSpec(memory_space=pltpu.SMEM)
ANY = pl.BlockSpec(memory_space=pl.ANY)
LIMIT = 40 * 1024 * 1024


def stage_masks(n):
    stages, low = [], 1
    while low < n:
        if low < 4 or low * 4 > n:
            stages.append([low])
            low *= 2
        else:
            stages.append([low, 2 * low, 3 * low])
            low *= 4
    return stages[::-1]


def piece_order(n):
    order = [0]
    for masks in stage_masks(n):
        order = order + [m ^ o for m in masks for o in order]
    return order


def swap(x, mask):
    n = lax.axis_size("obs")
    return lax.ppermute(x, "obs", [(i, i ^ mask) for i in range(n)])


def spread(x):
    stages = stage_masks(lax.axis_size("obs"))
    for masks in stages[:-1]:
        x = jnp.concatenate([x] + [swap(x, m) for m in masks], axis=0)
    return x, swap(x, stages[-1][0])


def prepare_kernel(week_weight, counts, week_ids, observed, w_out, y_out):
    blocks, rows = week_ids.shape
    ids = week_ids[...]
    table = jnp.zeros(ids.shape, jnp.float32)
    for week in range(week_weight.shape[0]):
        table = jnp.where(ids == week, week_weight[week], table)
    position = lax.broadcasted_iota(jnp.int32, ids.shape, 0) * rows + lax.broadcasted_iota(jnp.int32, ids.shape, 1)
    weights = jnp.where(position < counts[0], table, 0.0)
    fill = jnp.zeros((rows - blocks, rows), jnp.float32)
    w_out[...] = jnp.concatenate([weights, fill], axis=0).T
    y_out[...] = jnp.concatenate([observed[...], fill], axis=0).T


def forward_block(tiles, values, lane, b, minus):
    total = None
    for k, v in enumerate(values):
        part = tiles[b, k] * v
        total = part if total is None else total + part
    half = total.shape[1] // 2
    total = total[:, :half] + total[:, half:]
    if minus is not None:
        total = total - jnp.where(lane == b, minus, 0.0)
    return jnp.sum(total, axis=1, keepdims=True)


def start_tiles(footprints, tiles, sem):
    @pl.loop(0, tiles.shape[0])
    def _(b):
        pltpu.make_async_copy(footprints.at[b], tiles.at[b], sem.at[b]).start()


def first_kernel(rows, low, high, footprints, weights, observed, terms_out, departure_out, tiles, sem):
    start_tiles(footprints, tiles, sem)
    blocks, each, tile_rows, _ = tiles.shape
    lane = lax.broadcasted_iota(jnp.int32, (tile_rows, tile_rows), 1)
    departure_out[...] = jnp.zeros_like(departure_out)
    half = low.shape[0]

    @pl.loop(0, blocks)
    def _(b):
        pltpu.make_async_copy(footprints.at[b], tiles.at[b], sem.at[b]).wait()
        values = []
        for k in range(each):
            row = rows[b * each + k]
            a = low[pl.ds(jnp.minimum(row, half - 1), 1), :]
            z = high[pl.ds(jnp.maximum(row - half, 0), 1), :]
            values.append(jnp.where(row < half, a, z))
        depart = forward_block(tiles, values, lane, b, observed[...])
        departure_out[...] = jnp.where(lane == b, depart, departure_out[...])
        w = jnp.sum(jnp.where(lane == b, weights[...], 0.0), axis=1, keepdims=True)
        scaled = w * depart
        for k in range(each):
            terms_out[pl.ds(b * each + k, 1), :] = jnp.sum(tiles[b, k] * scaled, axis=0, keepdims=True)


def gather_terms(order, me, want, static, low, high, piece, hot):
    lane = lax.broadcasted_iota(jnp.int32, (1, 128), 1)
    wanted = want[...]
    ids_row = static.shape[1] - 8
    for q in range(len(order) // 2):
        first = static[me ^ order[2 * q], pl.ds(ids_row, 1), :128]
        second = static[me ^ order[2 * q + 1], pl.ds(ids_row, 1), :128]
        ids = jnp.where(lane < 64, first, second)
        hot[:, q * 128:(q + 1) * 128] = jnp.where(wanted == ids, 1.0, 0.0)
    each = len(order) // 2
    total = jnp.zeros((wanted.shape[0], low.shape[-1]), jnp.float32)
    for i, part in enumerate((low, high)):
        if part.shape[0] == each * piece:
            block = part[...]
        else:
            pitch = part.shape[0] // each
            block = jnp.concatenate([part[j * pitch:j * pitch + piece, :] for j in range(each)], axis=0)
        total = total + jnp.dot(
            hot[:, i * each * piece:(i + 1) * each * piece], block,
            precision=lax.Precision.HIGHEST, preferred_element_type=jnp.float32)
    return total


def second_kernel(order, tile_ids, me, want, static, low, high, footprints, weights, c_own, precision,
                  terms_out, gradient_out, image_out, tiles, sem, hot):
    start_tiles(footprints, tiles, sem)
    blocks, each, tile_rows, _ = tiles.shape
    count = blocks * each
    own = c_own.shape[0]
    lane = lax.broadcasted_iota(jnp.int32, (tile_rows, tile_rows), 1)
    image_out[...] = jnp.zeros_like(image_out)
    gradient_out[...] = gather_terms(order, me[0], want, static, low, high, count, hot)

    @pl.loop(0, count)
    def _(t):
        row = tile_ids[t]
        more = static[row // own, pl.ds(row % own, 1), :]
        gradient_out[pl.ds(t, 1), :] = gradient_out[pl.ds(t, 1), :] + more

    mine = gradient_out[count:, :] + c_own[...]
    gradient_out[count:, :] = mine

    @pl.loop(0, blocks)
    def _(b):
        pltpu.make_async_copy(footprints.at[b], tiles.at[b], sem.at[b]).wait()
        values = [gradient_out[pl.ds(b * each + k, 1), :] for k in range(each)]
        image = forward_block(tiles, values, lane, b, None)
        image_out[...] = jnp.where(lane == b, image, image_out[...])
        w = jnp.sum(jnp.where(lane == b, weights[...], 0.0), axis=1, keepdims=True)
        scaled = w * image
        for k in range(each):
            terms_out[pl.ds(b * each + k, 1), :] = jnp.sum(tiles[b, k] * scaled, axis=0, keepdims=True)

    image = image_out[...]
    terms_out[count:, :] = sums_row(mine, precision[...], weights[...], image, (8, terms_out.shape[1]))


def sums_row(gradient, precision, weights, image, shape):
    square = jnp.sum(gradient * gradient)
    below = jnp.sum(precision * gradient * gradient) + jnp.sum(weights * image * image)
    lane = lax.broadcasted_iota(jnp.int32, shape, 1)
    return jnp.where(lane == 0, square, jnp.where(lane == 1, below, 0.0))


def third_kernel(order, tile_ids, me, want, static, low, high, footprints, weights, precision, gradient,
                 departure, image, flux,
                 sums_out, flux_out, gradient_out, departure_out, image_out, tiles, sem, hot, second):
    start_tiles(footprints, tiles, sem)
    blocks, each, tile_rows, _ = tiles.shape
    count = blocks * each
    own = flux.shape[0]
    n = len(order)
    lane = lax.broadcasted_iota(jnp.int32, (tile_rows, tile_rows), 1)
    second[...] = gather_terms(order, me[0], want, static, low, high, count, hot)
    pitch = low.shape[0] // (n // 2)
    sums = jnp.zeros((1, 128), jnp.float32)
    for part in (low, high):
        for j in range(n // 2):
            sums = sums + part[j * pitch + count:j * pitch + count + 1, :128]
    step = sums[:, 0:1] / sums[:, 1:2]

    @pl.loop(0, count)
    def _(t):
        row = tile_ids[t]
        scale = static[row // own, pl.ds(own + row % own, 1), :]
        old = gradient[pl.ds(t, 1), :]
        second[pl.ds(t, 1), :] = old - step * (second[pl.ds(t, 1), :] + scale * old)

    old = gradient[count:, :]
    mine = old - step * (second[count:, :] + precision[...] * old)
    gradient_out[...] = mine
    flux_out[...] = flux[...] - step * old
    columns = jnp.zeros((tile_rows, tile_rows), jnp.float32)

    def block(b, columns):
        pltpu.make_async_copy(footprints.at[b], tiles.at[b], sem.at[b]).wait()
        values = [second[pl.ds(b * each + k, 1), :] for k in range(each)]
        return jnp.where(lane == b, forward_block(tiles, values, lane, b, None), columns)

    columns = lax.fori_loop(0, blocks, block, columns)
    row = sums_row(mine, precision[...], weights[...], columns, (1, 128))
    sums_out[...] = jnp.broadcast_to(row[None], sums_out.shape)
    departure_out[...] = (departure[...] - step * image[...]).T[:blocks]
    image_out[...] = columns.T[:blocks]


def last_kernel(sums, flux, gradient, departure, image, flux_out, departure_out):
    total = jnp.sum(sums[...], axis=0)
    step = total[:, 0:1] / total[:, 1:2]
    flux_out[...] = flux[...] - step * gradient[...]
    departure_out[...] = departure[...] - step * image[...]


def call(kernel, ins, outs, scratch=(), flops=0, moved=0):
    return pl.pallas_call(
        kernel,
        out_shape=[jax.ShapeDtypeStruct(s, jnp.float32) for s in outs],
        in_specs=ins,
        out_specs=[VMEM] * len(outs),
        scratch_shapes=list(scratch),
        compiler_params=pltpu.CompilerParams(vmem_limit_bytes=LIMIT),
        cost_estimate=pl.CostEstimate(flops=flops, bytes_accessed=moved, transcendentals=0),
    )


def body(footprints, tile_index, observed, week_ids, week_weight, counts, flux_start, flux_prior, prior_precision):
    n = lax.axis_size("obs")
    me = lax.axis_index("obs").astype(jnp.int32)
    blocks, each, tile_rows, cols = footprints.shape
    own = flux_start.shape[0]
    count = blocks * each
    order = piece_order(n)

    low, high = spread(flux_start)

    flat = tile_index.reshape(-1)
    c_own = prior_precision * (flux_start - flux_prior)
    ids = jnp.tile(flat.astype(jnp.float32), cols // count)
    mine = jnp.concatenate([c_own, prior_precision, jnp.broadcast_to(ids[None], (8, cols))], axis=0)
    static = lax.all_gather(mine, "obs", axis=0)
    want = jnp.concatenate([flat, me * own + jnp.arange(own, dtype=jnp.int32)]).astype(jnp.float32)[:, None]
    distance = jnp.bitwise_xor(flat // own, me)
    place = jnp.zeros_like(flat)
    for at, o in enumerate(order):
        place = jnp.where(distance == o, at, place)
    rows = place * own + flat % own
    me_s = me[None]

    weights, observed_t = call(
        prepare_kernel, [SMEM, SMEM, VMEM, VMEM], [(tile_rows, tile_rows)] * 2, flops=10000, moved=200000,
    )(week_weight, counts, week_ids, observed)

    tiles = [pltpu.VMEM(footprints.shape, jnp.float32), pltpu.SemaphoreType.DMA((blocks,))]
    hot = pltpu.VMEM((count + own, n * count), jnp.float32)
    work = dict(flops=4 * footprints.size, moved=4 * footprints.size)

    terms, departure = call(
        first_kernel, [SMEM, VMEM, VMEM, ANY, VMEM, VMEM],
        [(count, cols), (tile_rows, tile_rows)], tiles, **work,
    )(rows, low, high, footprints, weights, observed_t)

    low, high = spread(terms)
    terms, gradient, image = call(
        functools.partial(second_kernel, order),
        [SMEM, SMEM, VMEM, VMEM, VMEM, VMEM, ANY, VMEM, VMEM, VMEM],
        [(count + 8, cols), (count + own, cols), (tile_rows, tile_rows)], tiles + [hot], **work,
    )(flat, me_s, want, static, low, high, footprints, weights, c_own, prior_precision)

    low, high = spread(terms)
    sums, flux, gradient, departure, image = call(
        functools.partial(third_kernel, order),
        [SMEM, SMEM, VMEM, VMEM, VMEM, VMEM, ANY] + [VMEM] * 6,
        [(n, 1, 128), (own, cols), (own, cols), (blocks, tile_rows), (blocks, tile_rows)],
        tiles + [hot, pltpu.VMEM((count + own, cols), jnp.float32)], **work,
    )(flat, me_s, want, static, low, high, footprints, weights, prior_precision, gradient, departure, image,
      flux_start)

    sums = lax.all_to_all(sums, "obs", 0, 0)
    flux, departure = call(
        last_kernel, [VMEM] * 5, [(own, cols), (blocks, tile_rows)], flops=20000, moved=200000,
    )(sums, flux, gradient, departure, image)
    return flux, departure


def solution(mesh):
    rows = P(("groups", "obs"), None)
    return jax.shard_map(
        body,
        mesh=mesh,
        in_specs=(
            P(("groups", "obs"), None, None, None), rows, rows, rows,
            P("groups"), P(("groups", "obs")), rows, rows, rows,
        ),
        out_specs=(rows, rows),
        check_vma=False,
    )
```

time: 379 us -> 119 us (0.31)
  waiting for transfers between devices: 175 us -> 37.7 us
  blocking collectives: 130 us -> 10.9 us
  matrix products: 38.9 us -> 0 us
  starting transfers between devices: 0.08 us -> 21.2 us
  Pallas kernels: 0 us -> 19.6 us
  local copies, waits for them, and re-layouts: 3.28 us -> 11.3 us
  other arithmetic: 11 us -> 3.11 us
  between operations: 20.2 us -> 14.9 us
    psum x2 -> x0, waiting for transfers between devices: 175 us -> none  [body(): summed = lax.psum(spread, 'obs')]
    all_gather x3 -> x0, blocking collectives: 69.3 us -> none  [fetch_blocks(): gathered = lax.all_gather(owned, 'obs', axis=0, tiled=True)]
    psum x2 -> x0, blocking collectives: 60.9 us -> none  [body(): grad_square, grad_prior = lax.psum((grad_local, prior_local), 'obs')]
    dot_general x5 -> x0, matrix products: 38.9 us -> none  [the longest x3 28.5 us: forward(): jnp.einsum('bkrc,bkc->br', footprints, blocks, precision=lax.Precision.HI...]
    ppermute x0 -> x15, waiting for transfers between devices: none -> 37.7 us  [swap(): return lax.ppermute(x, 'obs', [(i, i ^ mask) for i in range(n)])]
    ppermute x0 -> x15, starting transfers between devices: none -> 21.1 us  [swap(): return lax.ppermute(x, 'obs', [(i, i ^ mask) for i in range(n)])]
    pallas_call x0 -> x5, Pallas kernels: none -> 19.6 us  [the longest x1 8.9 us: body(): call(functools.partial(third_kernel, order), [SMEM, SMEM, VMEM, VMEM, VME...]
    all_to_all x0 -> x1, blocking collectives: none -> 10.9 us  [body(): sums = lax.all_to_all(sums, 'obs', 0, 0)]
  transfers between devices with their start and end apart: 2 -> 16, of which waited for: 2 -> 11; matrix products, arithmetic and copies ran while one was open for 0% -> 1% of each run, Pallas kernels for 0% -> 4%
where the time goes in v1:
time: 119 us
  waiting for transfers between devices  37.7 us (32%)
  starting transfers between devices  21.2 us (18%)
  Pallas kernels  19.6 us (16%)
  between operations  14.9 us (13%)
  local copies, waits for them, and re-layouts  11.3 us (9%)
  blocking collectives  10.9 us (9%)
  other arithmetic  3.11 us (3%)
    ppermute x15, waiting for transfers between devices, swap(): return lax.ppermute(x, 'obs', [(i, i ^ mask) for i in range(n)])  37.7 us
    ppermute x15, starting transfers between devices, swap(): return lax.ppermute(x, 'obs', [(i, i ^ mask) for i in range(n)])  21.1 us
    unnamed x30, local copies, waits for them, and re-layouts  10.9 us
    all_to_all x1, blocking collectives, body(): sums = lax.all_to_all(sums, 'obs', 0, 0)  10.9 us
    pallas_call x1, Pallas kernels, body(): call(functools.partial(third_kernel, order), [SMEM, SMEM, VMEM, VMEM, VME...  8.9 us
    pallas_call x1, Pallas kernels, body(): call(functools.partial(second_kernel, order), [SMEM, SMEM, VMEM, VMEM, VM...  5.4 us
    pallas_call x1, Pallas kernels, body(): call(first_kernel, [SMEM, VMEM, VMEM, ANY, VMEM, VMEM], [(count, cols), (...  3.93 us
  transfers between devices with their start and end apart: 16, of which 11 were waited for; matrix products, arithmetic and copies ran while one was open for 1% of the time, Pallas kernels for 4%

profile of v1, /device:TPU:0, one launch (start us, length us, event | category | flops | bytes accessed | tf_op | source)
XLA Modules:
  0.0 118.8 jit_solution(16855777122534429527)
XLA Ops:
  10.4 3.1 %collective-permute-start = (f32[32,256]{1,0:T(8,128)}, f32[32,256]{1,0:T(8,128)S(1)}, u32[]{:S(2)}, u32[]{:S(2)}) collective-permute-start(f32[32,256]{1,0:T(8,128)} %flux.1), channel_id=1, source_target_pairs={{0,4},{1,5},{2,6},{3,7},{4,0},{5,1},{6,2},{7,3},{8,12},{9,13},{10,... | collective-permute-start | bytes 98312 | tf_op jit(solution)/shard_map/ppermute | solution.py:37
  13.5 2.6 %collective-permute-start.1 = (f32[32,256]{1,0:T(8,128)}, f32[32,256]{1,0:T(8,128)S(1)}, u32[]{:S(2)}, u32[]{:S(2)}) collective-permute-start(f32[32,256]{1,0:T(8,128)} %flux.1), channel_id=1, source_target_pairs={{0,8},{1,9},{2,10},{3,11},{4,12},{5,13},{6,14},{7,15},{8,0},{9,1},... | collective-permute-start | bytes 98312 | tf_op jit(solution)/shard_map/ppermute | solution.py:37
  16.1 3.0 %collective-permute-done.1 = f32[32,256]{1,0:T(8,128)S(1)} collective-permute-done((f32[32,256]{1,0:T(8,128)}, f32[32,256]{1,0:T(8,128)S(1)}, u32[]{:S(2)}, u32[]{:S(2)}) %collective-permute-start.1) | collective-permute-done | bytes 32800 | tf_op jit(solution)/shard_map/ppermute | solution.py:37
  19.1 2.9 %collective-permute-done.2 = f32[32,256]{1,0:T(8,128)S(1)} collective-permute-done((f32[32,256]{1,0:T(8,128)}, f32[32,256]{1,0:T(8,128)S(1)}, u32[]{:S(2)}, u32[]{:S(2)}) %collective-permute-start.2) | collective-permute-done | bytes 32800 | tf_op jit(solution)/shard_map/ppermute | solution.py:37
  22.8 1.6 %collective-permute-start.3 = (f32[128,256]{1,0:T(8,128)S(1)}, f32[128,256]{1,0:T(8,128)S(1)}, u32[]{:S(2)}, u32[]{:S(2)}) collective-permute-start(f32[128,256]{1,0:T(8,128)S(1)} %pad_maximum_fusion.2), channel_id=1, source_target_pairs={{0,2},{1,3},{2,0},{3,1},{4,6},{5,7},{6,4},{7,5},{8,10},{9,11},{10,... | collective-permute-start | bytes 393224 | tf_op jit(solution)/shard_map/ppermute | solution.py:37
  24.4 3.4 %collective-permute-done.3 = f32[128,256]{1,0:T(8,128)S(1)} collective-permute-done((f32[128,256]{1,0:T(8,128)S(1)}, f32[128,256]{1,0:T(8,128)S(1)}, u32[]{:S(2)}, u32[]{:S(2)}) %collective-permute-start.3) | collective-permute-done | bytes 131104 | tf_op jit(solution)/shard_map/ppermute | solution.py:37
  31.3 3.4 %copy-done = f32[16,4,128,256]{3,2,1,0:T(8,128)S(1)} copy-done((f32[16,4,128,256]{3,2,1,0:T(8,128)S(1)}, f32[16,4,128,256]{3,2,1,0:T(8,128)}, u32[]{:S(2)}) %copy-start) | copy-done | bytes 8388632
  34.7 3.9 %shard_map.105 = (f32[64,256]{1,0:T(8,128)S(1)}, f32[128,128]{1,0:T(8,128)S(1)}) custom-call(s32[64]{0:T(128)S(1)} %get-tuple-element.28.rows, f32[256,256]{1,0:T(8,128)S(1)} %constant_dynamic-update-slice_fusion.low, f32[256,256]{1,0:T(8,128)S(1)} %collective-permute-done.4.high, f32[16,4,128,256]{3,2,1,0:T(8,128)S(1)} %copy-done, ...), custom_call_target="tpu_custom_call" | custom-call | flops 8388608 | bytes 8388608 | tf_op jit(solution)/shard_map/pallas_call | solution.py:258
  38.7 1.7 %collective-permute-start.6 = (f32[64,256]{1,0:T(8,128)S(1)}, f32[64,256]{1,0:T(8,128)S(1)}, u32[]{:S(2)}, u32[]{:S(2)}) collective-permute-start(f32[64,256]{1,0:T(8,128)S(1)} %get-tuple-element.16), channel_id=1, source_target_pairs={{0,8},{1,9},{2,10},{3,11},{4,12},{5,13},{6,14},{7,15},{8,0},{9,1},... | collective-permute-start | bytes 196616 | tf_op jit(solution)/shard_map/ppermute | solution.py:37
  40.4 2.7 %collective-permute-start.7 = (f32[64,256]{1,0:T(8,128)S(1)}, f32[64,256]{1,0:T(8,128)S(1)}, u32[]{:S(2)}, u32[]{:S(2)}) collective-permute-start(f32[64,256]{1,0:T(8,128)S(1)} %get-tuple-element.16), channel_id=1, source_target_pairs={{0,12},{1,13},{2,14},{3,15},{4,8},{5,9},{6,10},{7,11},{8,4},{9,5},... | collective-permute-start | bytes 196616 | tf_op jit(solution)/shard_map/ppermute | solution.py:37
  44.2 5.4 %collective-permute-done.6 = f32[64,256]{1,0:T(8,128)S(1)} collective-permute-done((f32[64,256]{1,0:T(8,128)S(1)}, f32[64,256]{1,0:T(8,128)S(1)}, u32[]{:S(2)}, u32[]{:S(2)}) %collective-permute-start.6) | collective-permute-done | bytes 65568 | tf_op jit(solution)/shard_map/ppermute | solution.py:37
  49.7 1.7 %collective-permute-start.8 = (f32[256,256]{1,0:T(8,128)S(1)}, f32[256,256]{1,0:T(8,128)S(1)}, u32[]{:S(2)}, u32[]{:S(2)}) collective-permute-start(f32[256,256]{1,0:T(8,128)S(1)} %pad_maximum_fusion.1), channel_id=1, source_target_pairs={{0,2},{1,3},{2,0},{3,1},{4,6},{5,7},{6,4},{7,5},{8,10},{9,11},{10,... | collective-permute-start | bytes 786440 | tf_op jit(solution)/shard_map/ppermute | solution.py:37
  51.4 5.6 %collective-permute-done.8 = f32[256,256]{1,0:T(8,128)S(1)} collective-permute-done((f32[256,256]{1,0:T(8,128)S(1)}, f32[256,256]{1,0:T(8,128)S(1)}, u32[]{:S(2)}, u32[]{:S(2)}) %collective-permute-start.8) | collective-permute-done | bytes 262176 | tf_op jit(solution)/shard_map/ppermute | solution.py:37
  57.4 1.6 %collective-permute-done.9.high = f32[512,256]{1,0:T(8,128)S(1)} collective-permute-done((f32[512,256]{1,0:T(8,128)S(1)}, f32[512,256]{1,0:T(8,128)S(1)}, u32[]{:S(2)}, u32[]{:S(2)}) %collective-permute-start.9) | collective-permute-done | bytes 524320 | tf_op jit(solution)/shard_map/ppermute | solution.py:37
  59.0 3.4 %copy-done.1 = f32[16,4,128,256]{3,2,1,0:T(8,128)S(1)} copy-done((f32[16,4,128,256]{3,2,1,0:T(8,128)S(1)}, f32[16,4,128,256]{3,2,1,0:T(8,128)}, u32[]{:S(2)}) %copy-start.1) | copy-done | bytes 8388632
  63.6 5.4 %shard_map.106 = (f32[72,256]{1,0:T(8,128)S(1)}, f32[96,256]{1,0:T(8,128)S(1)}, f32[128,128]{1,0:T(8,128)S(1)}) custom-call(s32[64]{0:T(128)S(1)} %reshape.40.tile_ids, s32[1]{0:T(128)} %bitcast.me, f32[96,1]{1,0:T(8,128)S(1)} %convert_element_type.17.want, f32[16,72,256]{2,1,0:T(8,128)S(1)} %bitcast.4, ...), custom_call_target="tpu_custom_call" | custom-call | flops 8388608 | bytes 8388608 | tf_op jit(solution)/shard_map/pallas_call | solution.py:264
  69.1 3.3 %collective-permute-start.10 = (f32[72,256]{1,0:T(8,128)S(1)}, f32[72,256]{1,0:T(8,128)S(1)}, u32[]{:S(2)}, u32[]{:S(2)}) collective-permute-start(f32[72,256]{1,0:T(8,128)S(1)} %get-tuple-element.17), channel_id=1, source_target_pairs={{0,4},{1,5},{2,6},{3,7},{4,0},{5,1},{6,2},{7,3},{8,12},{9,13},{10,... | collective-permute-start | bytes 221192 | tf_op jit(solution)/shard_map/ppermute | solution.py:37
  72.3 2.4 %collective-permute-start.12 = (f32[72,256]{1,0:T(8,128)S(1)}, f32[72,256]{1,0:T(8,128)S(1)}, u32[]{:S(2)}, u32[]{:S(2)}) collective-permute-start(f32[72,256]{1,0:T(8,128)S(1)} %get-tuple-element.17), channel_id=1, source_target_pairs={{0,12},{1,13},{2,14},{3,15},{4,8},{5,9},{6,10},{7,11},{8,4},{9,5},... | collective-permute-start | bytes 221192 | tf_op jit(solution)/shard_map/ppermute | solution.py:37
  75.0 5.3 %collective-permute-done.11 = f32[72,256]{1,0:T(8,128)S(1)} collective-permute-done((f32[72,256]{1,0:T(8,128)S(1)}, f32[72,256]{1,0:T(8,128)S(1)}, u32[]{:S(2)}, u32[]{:S(2)}) %collective-permute-start.11) | collective-permute-done | bytes 73760 | tf_op jit(solution)/shard_map/ppermute | solution.py:37
  80.4 1.8 %collective-permute-start.13 = (f32[288,256]{1,0:T(8,128)S(1)}, f32[288,256]{1,0:T(8,128)S(1)}, u32[]{:S(2)}, u32[]{:S(2)}) collective-permute-start(f32[288,256]{1,0:T(8,128)S(1)} %pad_maximum_fusion), channel_id=1, source_target_pairs={{0,2},{1,3},{2,0},{3,1},{4,6},{5,7},{6,4},{7,5},{8,10},{9,11},{10,... | collective-permute-start | bytes 884744 | tf_op jit(solution)/shard_map/ppermute | solution.py:37
  82.2 7.1 %collective-permute-done.13 = f32[288,256]{1,0:T(8,128)S(1)} collective-permute-done((f32[288,256]{1,0:T(8,128)S(1)}, f32[288,256]{1,0:T(8,128)S(1)}, u32[]{:S(2)}, u32[]{:S(2)}) %collective-permute-start.13) | collective-permute-done | bytes 294944 | tf_op jit(solution)/shard_map/ppermute | solution.py:37
  89.4 2.0 %collective-permute-done.14.high = f32[576,256]{1,0:T(8,128)S(1)} collective-permute-done((f32[576,256]{1,0:T(8,128)S(1)}, f32[576,256]{1,0:T(8,128)S(1)}, u32[]{:S(2)}, u32[]{:S(2)}) %collective-permute-start.14) | collective-permute-done | bytes 589856 | tf_op jit(solution)/shard_map/ppermute | solution.py:37
  91.4 8.9 %shard_map.107 = (f32[16,1,128]{2,1,0:T(1,128)S(1)}, f32[32,256]{1,0:T(8,128)S(1)}, f32[32,256]{1,0:T(8,128)S(1)}, f32[16,128]{1,0:T(8,128)S(1)}, f32[16,128]{1,0:T(8,128)S(1)}) custom-call(s32[64]{0:T(128)S(1)} %reshape.40.tile_ids, s32[1]{0:T(128)} %bitcast.me, f32[96,1]{1,0:T(8,128)S(1)} %convert_element_type.17.want, f32[16,72,256]{2,1,0:T(8,128)S(1)} %bitcast.5, ...), custom_call_target="tpu_custom_call" | custom-call | flops 8388608 | bytes 8388608 | tf_op jit(solution)/shard_map/pallas_call | solution.py:271
  100.3 10.9 %all_to_all.5.sums = f32[16,1,128]{2,1,0:T(1,128)S(1)} all-to-all(f32[16,1,128]{2,1,0:T(1,128)S(1)} %get-tuple-element.21), channel_id=1, replica_groups=mesh['groups'=2,'obs'=16] {'obs'}, dimensions={0} | all-to-all | bytes 16384 | tf_op jit(solution)/shard_map/all_to_all | solution.py:279
  (63 shorter events, 10.8 us)
Async XLA Ops:
  7.2 51.8 %copy-start.4 = (f32[32,256]{1,0:T(8,128)S(1)}, f32[32,256]{1,0:T(8,128)}, u32[]{:S(2)}) copy-start(f32[32,256]{1,0:T(8,128)} %precision.3) | copy-start | bytes 98308
  7.2 51.8 %all-gather.3.cloned.1.call-start = ((), (), s32[]{:S(2)}) async-start(), calls=%async_computation.1 | async-start | bytes 1253376 | tf_op jit(solution)/shard_map/all_gather | solution.py:241
  10.4 5.7 %collective-permute-start = (f32[32,256]{1,0:T(8,128)}, f32[32,256]{1,0:T(8,128)S(1)}, u32[]{:S(2)}, u32[]{:S(2)}) collective-permute-start(f32[32,256]{1,0:T(8,128)} %flux.1), channel_id=1, source_target_pairs={{0,4},{1,5},{2,6},{3,7},{4,0},{5,1},{6,2},{7,3},{8,12},{9,13},{10,... | collective-permute-start | bytes 98312 | tf_op jit(solution)/shard_map/ppermute | solution.py:37
  13.5 5.6 %collective-permute-start.1 = (f32[32,256]{1,0:T(8,128)}, f32[32,256]{1,0:T(8,128)S(1)}, u32[]{:S(2)}, u32[]{:S(2)}) collective-permute-start(f32[32,256]{1,0:T(8,128)} %flux.1), channel_id=1, source_target_pairs={{0,8},{1,9},{2,10},{3,11},{4,12},{5,13},{6,14},{7,15},{8,0},{9,1},... | collective-permute-start | bytes 98312 | tf_op jit(solution)/shard_map/ppermute | solution.py:37
  16.1 5.9 %collective-permute-start.2 = (f32[32,256]{1,0:T(8,128)}, f32[32,256]{1,0:T(8,128)S(1)}, u32[]{:S(2)}, u32[]{:S(2)}) collective-permute-start(f32[32,256]{1,0:T(8,128)} %flux.1), channel_id=1, source_target_pairs={{0,12},{1,13},{2,14},{3,15},{4,8},{5,9},{6,10},{7,11},{8,4},{9,5},... | collective-permute-start | bytes 98312 | tf_op jit(solution)/shard_map/ppermute | solution.py:37
  22.8 5.0 %collective-permute-start.3 = (f32[128,256]{1,0:T(8,128)S(1)}, f32[128,256]{1,0:T(8,128)S(1)}, u32[]{:S(2)}, u32[]{:S(2)}) collective-permute-start(f32[128,256]{1,0:T(8,128)S(1)} %pad_maximum_fusion.2), channel_id=1, source_target_pairs={{0,2},{1,3},{2,0},{3,1},{4,6},{5,7},{6,4},{7,5},{8,10},{9,11},{10,... | collective-permute-start | bytes 393224 | tf_op jit(solution)/shard_map/ppermute | solution.py:37
  27.8 3.4 %collective-permute-start.4 = (f32[256,256]{1,0:T(8,128)S(1)}, f32[256,256]{1,0:T(8,128)S(1)}, u32[]{:S(2)}, u32[]{:S(2)}) collective-permute-start(f32[256,256]{1,0:T(8,128)S(1)} %constant_dynamic-update-slice_fusion.low), channel_id=1, source_target_pairs={{0,1},{1,0},{2,3},{3,2},{4,5},{5,4},{6,7},{7,6},{8,9},{9,8},{10,11... | collective-permute-start | bytes 786440 | tf_op jit(solution)/shard_map/ppermute | solution.py:37
  28.6 0.7 copy-start.6
  29.3 0.7 copy-start.7
  31.3 3.4 %copy-start = (f32[16,4,128,256]{3,2,1,0:T(8,128)S(1)}, f32[16,4,128,256]{3,2,1,0:T(8,128)}, u32[]{:S(2)}) copy-start(f32[16,4,128,256]{3,2,1,0:T(8,128)} %footprints.5) | copy-start | bytes 25165828
  38.6 52.8 %copy-start.5 = (f32[32,256]{1,0:T(8,128)S(1)}, f32[32,256]{1,0:T(8,128)}, u32[]{:S(2)}) copy-start(f32[32,256]{1,0:T(8,128)} %flux.1) | copy-start | bytes 98308
  38.6 5.6 %collective-permute-start.5 = (f32[64,256]{1,0:T(8,128)S(1)}, f32[64,256]{1,0:T(8,128)S(1)}, u32[]{:S(2)}, u32[]{:S(2)}) collective-permute-start(f32[64,256]{1,0:T(8,128)S(1)} %get-tuple-element.16), channel_id=1, source_target_pairs={{0,4},{1,5},{2,6},{3,7},{4,0},{5,1},{6,2},{7,3},{8,12},{9,13},{10,... | collective-permute-start | bytes 196616 | tf_op jit(solution)/shard_map/ppermute | solution.py:37
  38.7 11.0 %collective-permute-start.6 = (f32[64,256]{1,0:T(8,128)S(1)}, f32[64,256]{1,0:T(8,128)S(1)}, u32[]{:S(2)}, u32[]{:S(2)}) collective-permute-start(f32[64,256]{1,0:T(8,128)S(1)} %get-tuple-element.16), channel_id=1, source_target_pairs={{0,8},{1,9},{2,10},{3,11},{4,12},{5,13},{6,14},{7,15},{8,0},{9,1},... | collective-permute-start | bytes 196616 | tf_op jit(solution)/shard_map/ppermute | solution.py:37
  40.4 9.3 %collective-permute-start.7 = (f32[64,256]{1,0:T(8,128)S(1)}, f32[64,256]{1,0:T(8,128)S(1)}, u32[]{:S(2)}, u32[]{:S(2)}) collective-permute-start(f32[64,256]{1,0:T(8,128)S(1)} %get-tuple-element.16), channel_id=1, source_target_pairs={{0,12},{1,13},{2,14},{3,15},{4,8},{5,9},{6,10},{7,11},{8,4},{9,5},... | collective-permute-start | bytes 196616 | tf_op jit(solution)/shard_map/ppermute | solution.py:37
  49.7 7.3 %collective-permute-start.8 = (f32[256,256]{1,0:T(8,128)S(1)}, f32[256,256]{1,0:T(8,128)S(1)}, u32[]{:S(2)}, u32[]{:S(2)}) collective-permute-start(f32[256,256]{1,0:T(8,128)S(1)} %pad_maximum_fusion.1), channel_id=1, source_target_pairs={{0,2},{1,3},{2,0},{3,1},{4,6},{5,7},{6,4},{7,5},{8,10},{9,11},{10,... | collective-permute-start | bytes 786440 | tf_op jit(solution)/shard_map/ppermute | solution.py:37
  57.0 2.0 %collective-permute-start.9 = (f32[512,256]{1,0:T(8,128)S(1)}, f32[512,256]{1,0:T(8,128)S(1)}, u32[]{:S(2)}, u32[]{:S(2)}) collective-permute-start(f32[512,256]{1,0:T(8,128)S(1)} %constant_dynamic-update-slice_fusion.5.low), channel_id=1, source_target_pairs={{0,1},{1,0},{2,3},{3,2},{4,5},{5,4},{6,7},{7,6},{8,9},{9,8},{10,11... | collective-permute-start | bytes 1572872 | tf_op jit(solution)/shard_map/ppermute | solution.py:37
  59.0 3.4 %copy-start.1 = (f32[16,4,128,256]{3,2,1,0:T(8,128)S(1)}, f32[16,4,128,256]{3,2,1,0:T(8,128)}, u32[]{:S(2)}) copy-start(f32[16,4,128,256]{3,2,1,0:T(8,128)} %footprints.5) | copy-start | bytes 25165828
  62.4 1.3 %copy-start.2 = (f32[1152,256]{1,0:T(8,128)S(1)}, f32[1152,256]{1,0:T(8,128)}, u32[]{:S(2)}) copy-start(f32[1152,256]{1,0:T(8,128)} %all-gather.3.cloned.1.call-done) | copy-start | bytes 3538948
  63.6 27.7 %copy-start.3 = (f32[1152,256]{1,0:T(8,128)S(1)}, f32[1152,256]{1,0:T(8,128)}, u32[]{:S(2)}) copy-start(f32[1152,256]{1,0:T(8,128)} %all-gather.3.cloned.1.call-done) | copy-start | bytes 3538948
  69.1 5.9 %collective-permute-start.10 = (f32[72,256]{1,0:T(8,128)S(1)}, f32[72,256]{1,0:T(8,128)S(1)}, u32[]{:S(2)}, u32[]{:S(2)}) collective-permute-start(f32[72,256]{1,0:T(8,128)S(1)} %get-tuple-element.17), channel_id=1, source_target_pairs={{0,4},{1,5},{2,6},{3,7},{4,0},{5,1},{6,2},{7,3},{8,12},{9,13},{10,... | collective-permute-start | bytes 221192 | tf_op jit(solution)/shard_map/ppermute | solution.py:37
  72.3 8.0 %collective-permute-start.11 = (f32[72,256]{1,0:T(8,128)S(1)}, f32[72,256]{1,0:T(8,128)S(1)}, u32[]{:S(2)}, u32[]{:S(2)}) collective-permute-start(f32[72,256]{1,0:T(8,128)S(1)} %get-tuple-element.17), channel_id=1, source_target_pairs={{0,8},{1,9},{2,10},{3,11},{4,12},{5,13},{6,14},{7,15},{8,0},{9,1},... | collective-permute-start | bytes 221192 | tf_op jit(solution)/shard_map/ppermute | solution.py:37
  72.3 8.0 %collective-permute-start.12 = (f32[72,256]{1,0:T(8,128)S(1)}, f32[72,256]{1,0:T(8,128)S(1)}, u32[]{:S(2)}, u32[]{:S(2)}) collective-permute-start(f32[72,256]{1,0:T(8,128)S(1)} %get-tuple-element.17), channel_id=1, source_target_pairs={{0,12},{1,13},{2,14},{3,15},{4,8},{5,9},{6,10},{7,11},{8,4},{9,5},... | collective-permute-start | bytes 221192 | tf_op jit(solution)/shard_map/ppermute | solution.py:37
  80.4 8.9 %collective-permute-start.13 = (f32[288,256]{1,0:T(8,128)S(1)}, f32[288,256]{1,0:T(8,128)S(1)}, u32[]{:S(2)}, u32[]{:S(2)}) collective-permute-start(f32[288,256]{1,0:T(8,128)S(1)} %pad_maximum_fusion), channel_id=1, source_target_pairs={{0,2},{1,3},{2,0},{3,1},{4,6},{5,7},{6,4},{7,5},{8,10},{9,11},{10,... | collective-permute-start | bytes 884744 | tf_op jit(solution)/shard_map/ppermute | solution.py:37
  89.3 2.1 %collective-permute-start.14 = (f32[576,256]{1,0:T(8,128)S(1)}, f32[576,256]{1,0:T(8,128)S(1)}, u32[]{:S(2)}, u32[]{:S(2)}) collective-permute-start(f32[576,256]{1,0:T(8,128)S(1)} %constant_dynamic-update-slice_fusion.10.low), channel_id=1, source_target_pairs={{0,1},{1,0},{2,3},{3,2},{4,5},{5,4},{6,7},{7,6},{8,9},{9,8},{10,11... | collective-permute-start | bytes 1769480 | tf_op jit(solution)/shard_map/ppermute | solution.py:37
  (1 other events, 0.7 us)
Sparse Core Ops, SparseCore 0:
  10.5 42.2 all-gather.2

commit v2 on v0

v2 whole, which is shorter than its diff:
```python
import functools

import jax
import jax.numpy as jnp
from jax import lax
from jax.experimental import pallas as pl
from jax.experimental.pallas import tpu as pltpu
from jax.sharding import PartitionSpec as P

VMEM = pl.BlockSpec(memory_space=pltpu.VMEM)
SMEM = pl.BlockSpec(memory_space=pltpu.SMEM)
ANY = pl.BlockSpec(memory_space=pl.ANY)
HBM = pl.BlockSpec(memory_space=pltpu.HBM)
LIMIT = 24 * 1024 * 1024
F32 = jnp.float32


def stage_masks(n):
    stages, low = [], 1
    while low < n:
        if low < 4 or low * 4 > n:
            stages.append([low])
            low *= 2
        else:
            stages.append([low, 2 * low, 3 * low])
            low *= 4
    return stages[::-1]


def swap(x, mask):
    n = lax.axis_size("obs")
    return lax.ppermute(x, "obs", [(i, i ^ mask) for i in range(n)])


def shift(masks, mask):
    return [m ^ mask for m in masks]


def call(kernel, ins, outs, scratch=(), flops=0, moved=0, pinned=False):
    return pl.pallas_call(
        kernel,
        out_shape=[pltpu.VMEM(s, F32) if pinned and len(s) == 4 else jax.ShapeDtypeStruct(s, F32) for s in outs],
        in_specs=ins,
        out_specs=[VMEM] * len(outs),
        scratch_shapes=list(scratch),
        compiler_params=pltpu.CompilerParams(vmem_limit_bytes=LIMIT),
        cost_estimate=pl.CostEstimate(flops=flops, bytes_accessed=moved, transcendentals=0),
    )


def pile_kernel(pitch, at, rows, *refs):
    *arrays, _, pile_out = refs
    i = 0
    for array in arrays:
        for start in range(0, array.shape[0], pitch):
            pile_out[i:i + rows, :] = array[start + at:start + at + rows, :]
            i += rows


def pile(arrays, pitch, at, rows, after):
    total = sum(a.shape[0] for a in arrays) // pitch * rows
    cols = arrays[0].shape[1]
    return call(
        functools.partial(pile_kernel, pitch, at, rows), [VMEM] * len(arrays) + [ANY], [(total, cols)],
        moved=8 * total * cols,
    )(*arrays, after)[0]


def far_stages(x, pitch, after):
    masks = [0]
    *lead, last = stage_masks(lax.axis_size("obs"))[:-2]
    for stage in lead:
        x = pile([x] + [swap(x, m) for m in stage], pitch, 0, pitch, after)
        masks = masks + [k for m in stage for k in shift(masks, m)]
    if len(last) == 1:
        return [([x], masks), ([swap(x, last[0])], shift(masks, last[0]))]
    near, *rest = last
    far = [swap(x, m) for m in rest]
    return [
        ([x, swap(x, near)], masks + shift(masks, near)),
        (far, [k for m in rest for k in shift(masks, m)]),
    ]


def near_stages(halves):
    last = stage_masks(lax.axis_size("obs"))[-2:]
    parts = list(halves)
    for (m,) in last:
        parts = parts + [(swap(x, m), shift(masks, m)) for x, masks in parts]
    return [x for x, _ in parts], [masks for _, masks in parts]


def spread(x):
    rows = x.shape[0]
    return near_stages([(pile(a, rows, 0, rows, x), m) for a, m in far_stages(x, rows, x)])


def bundle_kernel(tile_ids, me, flux, prior, precision, bundle_out, want_out, prior_in, sem):
    each, blocks = tile_ids.shape
    count = blocks * each
    own, cols = flux.shape
    copies = [
        pltpu.make_async_copy(flux, bundle_out.at[pl.ds(0, own)], sem.at[0]),
        pltpu.make_async_copy(precision, bundle_out.at[pl.ds(2 * own, own)], sem.at[1]),
        pltpu.make_async_copy(prior, prior_in, sem.at[2]),
    ]
    for c in copies:
        c.start()
    lane = lax.broadcasted_iota(jnp.int32, (8, cols), 1) % count
    tall = lax.broadcasted_iota(jnp.int32, want_out.shape, 0)
    across = jnp.zeros((8, cols), jnp.int32)
    down = me[0] * own + tall - count
    for t in range(count):
        tile = tile_ids[t % each, t // each]
        across = jnp.where(lane == t, tile, across)
        down = jnp.where(tall == t, tile, down)
    bundle_out[3 * own:, :] = across.astype(F32)
    want_out[...] = down.astype(F32)
    for c in copies:
        c.wait()
    bundle_out[own:2 * own, :] = bundle_out[2 * own:3 * own, :] * (bundle_out[:own, :] - prior_in[...])


def prepare_kernel(tile_ids, me, week_weight, counts, week_ids, observed, footprints, w_out, y_out, tiles_out,
                   ids_in, y_in, sem):
    del tile_ids, me
    small = [
        pltpu.make_async_copy(week_ids, ids_in, sem.at[0]),
        pltpu.make_async_copy(observed, y_in, sem.at[1]),
    ]
    copy = pltpu.make_async_copy(footprints, tiles_out, sem.at[2])
    for c in small:
        c.start()
    copy.start()
    for c in small:
        c.wait()
    blocks, rows = week_ids.shape
    ids = ids_in[...]
    table = jnp.zeros(ids.shape, F32)
    for week in range(week_weight.shape[0]):
        table = jnp.where(ids == week, week_weight[week], table)
    position = lax.broadcasted_iota(jnp.int32, ids.shape, 0) * rows + lax.broadcasted_iota(jnp.int32, ids.shape, 1)
    weights = jnp.where(position < counts[0], table, 0.0)
    fill = jnp.zeros((rows - blocks, rows), F32)
    w_out[...] = jnp.concatenate([weights, fill], axis=0).T
    y_out[...] = jnp.concatenate([y_in[...], fill], axis=0).T
    copy.wait()


def by_owner(me, masks, refs, pitch, at, rows, into):
    for ref, ms in zip(refs, masks, strict=True):
        for j, m in enumerate(ms):
            place = pl.ds(pl.multiple_of((me ^ m) * rows, 8), rows)
            into[place, :] = ref[j * pitch + at:j * pitch + at + rows, :]


def forward_block(tiles, values, lane, b, minus):
    total = None
    for k, v in enumerate(values):
        part = tiles[b, k] * v
        total = part if total is None else total + part
    half = total.shape[1] // 2
    total = total[:, :half] + total[:, half:]
    if minus is not None:
        total = total - jnp.where(lane == b, minus, 0.0)
    return jnp.sum(total, axis=1, keepdims=True)


def transpose_block(tiles, weights, column, lane, b, terms_out):
    w = jnp.sum(jnp.where(lane == b, weights[...], 0.0), axis=1, keepdims=True)
    scaled = w * column
    each = tiles.shape[1]
    for k in range(each):
        terms_out[pl.ds(b * each + k, 1), :] = jnp.sum(tiles[b, k] * scaled, axis=0, keepdims=True)


def first_kernel(masks, tile_ids, me, tiles, weights, observed, *refs):
    *parts, terms_out, departure_out, flux = refs
    blocks, each, tile_rows, _ = tiles.shape
    own = parts[0].shape[0] // len(masks[0])
    by_owner(me[0], masks, parts, own, 0, own, flux)
    lane = lax.broadcasted_iota(jnp.int32, (tile_rows, tile_rows), 1)
    departure_out[...] = jnp.zeros_like(departure_out)

    @pl.loop(0, blocks, unroll=4)
    def _(b):
        values = [flux[pl.ds(tile_ids[k, b], 1), :] for k in range(each)]
        depart = forward_block(tiles, values, lane, b, observed[...])
        departure_out[...] = jnp.where(lane == b, depart, departure_out[...])
        transpose_block(tiles, weights, depart, lane, b, terms_out)


def sum_terms(masks, parts, piece, name_masks, names, want, hot):
    lane = lax.broadcasted_iota(jnp.int32, (1, 128), 1)
    wanted = want[...]
    ids = {}
    for ref, ms in zip(names, name_masks, strict=True):
        pitch = ref.shape[0] // len(ms)
        for j, m in enumerate(ms):
            ids[m] = ref[(j + 1) * pitch - 8:(j + 1) * pitch - 7, :128]
    order = [m for ms in masks for m in ms]
    for j in range(0, len(order), 2):
        pair = jnp.where(lane < piece, ids[order[j]], ids[order[j + 1]])
        hot[:, j * piece:(j + 2) * piece] = jnp.where(wanted == pair, 1.0, 0.0)
    pitch = parts[0].shape[0] // len(masks[0])
    block = jnp.concatenate(
        [ref[j * pitch:j * pitch + piece, :] for ref, ms in zip(parts, masks, strict=True) for j in range(len(ms))], axis=0)
    return jnp.dot(hot[...], block, precision=lax.Precision.HIGHEST, preferred_element_type=F32)


def sums_row(gradient, precision, weights, image, shape):
    square = jnp.sum(gradient * gradient)
    below = jnp.sum(precision * gradient * gradient) + jnp.sum(weights * image * image)
    lane = lax.broadcasted_iota(jnp.int32, shape, 1)
    return jnp.where(lane == 0, square, jnp.where(lane == 1, below, 0.0))


def second_kernel(masks, name_masks, tile_ids, me, tiles, weights, want, bundle, *refs):
    parts, names = refs[:len(masks)], refs[len(masks):len(masks) + len(name_masks)]
    terms_out, gradient_out, image_out, hot, more = refs[len(masks) + len(name_masks):]
    blocks, each, tile_rows, _ = tiles.shape
    count = blocks * each
    own = want.shape[0] - count
    by_owner(me[0], name_masks, names, 2 * own + 8, 0, own, more)
    lane = lax.broadcasted_iota(jnp.int32, (tile_rows, tile_rows), 1)
    image_out[...] = jnp.zeros_like(image_out)
    gradient_out[...] = sum_terms(masks, parts, count, name_masks, names, want, hot)
    mine = gradient_out[count:, :] + bundle[own:2 * own, :]
    gradient_out[count:, :] = mine

    @pl.loop(0, blocks, unroll=4)
    def _(b):
        values = []
        for k in range(each):
            t = pl.ds(b * each + k, 1)
            value = gradient_out[t, :] + more[pl.ds(tile_ids[k, b], 1), :]
            gradient_out[t, :] = value
            values.append(value)
        image = forward_block(tiles, values, lane, b, None)
        image_out[...] = jnp.where(lane == b, image, image_out[...])
        transpose_block(tiles, weights, image, lane, b, terms_out)

    terms_out[count:, :] = sums_row(
        mine, bundle[2 * own:3 * own, :], weights[...], image_out[...], (8, terms_out.shape[1]))


def third_kernel(masks, name_masks, tile_ids, me, tiles, weights, want, bundle, gradient, departure, image, *refs):
    parts, names = refs[:len(masks)], refs[len(masks):len(masks) + len(name_masks)]
    (sums_out, flux_out, gradient_out, departure_out, image_out, hot, scale, second) = refs[len(masks) + len(name_masks):]
    blocks, each, tile_rows, _ = tiles.shape
    count = blocks * each
    own = want.shape[0] - count
    by_owner(me[0], name_masks, names, 2 * own + 8, own, own, scale)
    lane = lax.broadcasted_iota(jnp.int32, (tile_rows, tile_rows), 1)
    pitch = parts[0].shape[0] // len(masks[0])
    sums = jnp.zeros((1, 128), F32)
    for ref, ms in zip(parts, masks, strict=True):
        for j in range(len(ms)):
            sums = sums + ref[j * pitch + count:j * pitch + count + 1, :128]
    step = sums[:, 0:1] / sums[:, 1:2]
    second[...] = sum_terms(masks, parts, count, name_masks, names, want, hot)
    old = gradient[count:, :]
    precision = bundle[2 * own:3 * own, :]
    mine = old - step * (second[count:, :] + precision * old)
    gradient_out[...] = mine
    flux_out[...] = bundle[:own, :] - step * old
    second[:count, :] = gradient[:count, :] - step * second[:count, :]

    def block(b, columns):
        values = []
        for k in range(each):
            t = pl.ds(b * each + k, 1)
            values.append(second[t, :] - step * scale[pl.ds(tile_ids[k, b], 1), :] * gradient[t, :])
        return jnp.where(lane == b, forward_block(tiles, values, lane, b, None), columns)

    columns = lax.fori_loop(0, blocks, block, jnp.zeros((tile_rows, tile_rows), F32), unroll=4)
    row = sums_row(mine, precision, weights[...], columns, (1, 128))
    sums_out[...] = jnp.broadcast_to(row[None], sums_out.shape)
    departure_out[...] = (departure[...] - step * image[...]).T[:blocks]
    image_out[...] = columns.T[:blocks]


def last_kernel(sums, flux, gradient, departure, image, flux_out, departure_out):
    total = jnp.sum(sums[...], axis=0)
    step = total[:, 0:1] / total[:, 1:2]
    flux_out[...] = flux[...] - step * gradient[...]
    departure_out[...] = departure[...] - step * image[...]


def body(footprints, tile_index, observed, week_ids, week_weight, counts, flux_start, flux_prior, prior_precision):
    n = lax.axis_size("obs")
    blocks, each, tile_rows, cols = footprints.shape
    own = flux_start.shape[0]
    count = blocks * each
    square = (tile_rows, tile_rows)
    place = (tile_index.T, lax.axis_index("obs").astype(jnp.int32)[None])

    def in_hbm(*arrays):
        return [pltpu.with_memory_space_constraint(x, pltpu.HBM) for x in arrays]

    pitch = 3 * own + 8
    bundle, want = call(
        bundle_kernel, [SMEM] * 2 + [HBM] * 3, [(pitch, cols), (count + own, 128)],
        [pltpu.VMEM((own, cols), F32), pltpu.SemaphoreType.DMA((3,))], flops=10000, moved=12 * own * cols,
    )(*place, *in_hbm(flux_start, flux_prior, prior_precision))
    weights, observed_t, tiles = call(
        prepare_kernel, [SMEM] * 4 + [HBM] * 3, [square, square, footprints.shape],
        [pltpu.VMEM(week_ids.shape, jnp.int32), pltpu.VMEM(observed.shape, F32), pltpu.SemaphoreType.DMA((3,))],
        flops=10000, moved=8 * footprints.size, pinned=True,
    )(*place, week_weight, counts, *in_hbm(week_ids, observed, footprints))
    tiles = pltpu.with_memory_space_constraint(tiles, pltpu.VMEM)

    halves = far_stages(bundle, pitch, bundle)
    parts, masks = near_stages([(pile(a, pitch, 0, own, weights), m) for a, m in halves])

    hot = pltpu.VMEM((count + own, n * count), F32)
    whole = pltpu.VMEM((n * own, cols), F32)
    work = dict(flops=4 * footprints.size, moved=4 * footprints.size)
    terms, departure = call(
        functools.partial(first_kernel, masks), [SMEM] * 2 + [VMEM] * (3 + len(parts)),
        [(count, cols), square], [whole], **work,
    )(*place, tiles, weights, observed_t, *parts)

    rows = 2 * own + 8
    names, name_masks = near_stages(
        [(pile([x for a, _ in halves for x in a], pitch, own, rows, terms), [m for _, ms in halves for m in ms])])
    parts, masks = spread(terms)
    terms, gradient, image = call(
        functools.partial(second_kernel, masks, name_masks), [SMEM] * 2 + [VMEM] * (4 + len(parts) + len(names)),
        [(count + 8, cols), (count + own, cols), square], [hot, whole], **work,
    )(*place, tiles, weights, want, bundle, *parts, *names)

    parts, masks = spread(terms)
    sums, flux, gradient, departure, image = call(
        functools.partial(third_kernel, masks, name_masks), [SMEM] * 2 + [VMEM] * (7 + len(parts) + len(names)),
        [(n, 1, 128), (own, cols), (own, cols), (blocks, tile_rows), (blocks, tile_rows)],
        [hot, whole, pltpu.VMEM((count + own, cols), F32)], **work,
    )(*place, tiles, weights, want, bundle, gradient, departure, image, *parts, *names)

    sums = lax.all_to_all(sums, "obs", 0, 0)
    flux, departure = call(
        last_kernel, [VMEM] * 5, [(own, cols), (blocks, tile_rows)], flops=20000, moved=200000,
    )(sums, flux, gradient, departure, image)
    return flux, departure


def solution(mesh):
    rows = P(("groups", "obs"), None)
    return jax.shard_map(
        body,
        mesh=mesh,
        in_specs=(
            P(("groups", "obs"), None, None, None), rows, rows, rows,
            P("groups"), P(("groups", "obs")), rows, rows, rows,
        ),
        out_specs=(rows, rows),
        check_vma=False,
    )
```

time: 379 us -> 79.8 us (0.21)
  waiting for transfers between devices: 175 us -> 27.8 us
  blocking collectives: 130 us -> 10.7 us
  matrix products: 38.9 us -> 0 us
  starting transfers between devices: 0.08 us -> 24.3 us
  between operations: 20.2 us -> 1.45 us
  Pallas kernels: 0 us -> 14 us
  other arithmetic: 11 us -> 0 us
    psum x2 -> x0, waiting for transfers between devices: 175 us -> none  [body(): summed = lax.psum(spread, 'obs')]
    all_gather x3 -> x0, blocking collectives: 69.3 us -> none  [fetch_blocks(): gathered = lax.all_gather(owned, 'obs', axis=0, tiled=True)]
    psum x2 -> x0, blocking collectives: 60.9 us -> none  [body(): grad_square, grad_prior = lax.psum((grad_local, prior_local), 'obs')]
    dot_general x5 -> x0, matrix products: 38.9 us -> none  [the longest x3 28.5 us: forward(): jnp.einsum('bkrc,bkc->br', footprints, blocks, precision=lax.Precision.HI...]
    ppermute x0 -> x30, waiting for transfers between devices: none -> 27.8 us  [swap(): return lax.ppermute(x, 'obs', [(i, i ^ mask) for i in range(n)])]
    ppermute x0 -> x30, starting transfers between devices: none -> 24.3 us  [swap(): return lax.ppermute(x, 'obs', [(i, i ^ mask) for i in range(n)])]
    pallas_call x0 -> x13, Pallas kernels: none -> 14 us  [the longest x1 4.01 us: body(): call(prepare_kernel, [SMEM] * 4 + [HBM] * 3, [square, square, footprints....]
    all_to_all x0 -> x1, blocking collectives: none -> 10.7 us  [body(): sums = lax.all_to_all(sums, 'obs', 0, 0)]
  transfers between devices with their start and end apart: 2 -> 30, of which waited for: 2 -> 12; matrix products, arithmetic and copies ran while one was open for 0% -> 0% of each run, Pallas kernels for 0% -> 5%
where the time goes in v2:
time: 79.8 us; the launch traced here: 79.5 us
  waiting for transfers between devices  27.8 us (35%)
  starting transfers between devices  24.3 us (30%)
  Pallas kernels  14 us (18%)
  blocking collectives  10.7 us (13%)
  between operations  1.45 us (2%)
  local copies, waits for them, and re-layouts  1.33 us (2%)
    ppermute x30, waiting for transfers between devices, swap(): return lax.ppermute(x, 'obs', [(i, i ^ mask) for i in range(n)])  27.8 us
    ppermute x30, starting transfers between devices, swap(): return lax.ppermute(x, 'obs', [(i, i ^ mask) for i in range(n)])  24.3 us
    all_to_all x1, blocking collectives, body(): sums = lax.all_to_all(sums, 'obs', 0, 0)  10.7 us
    pallas_call x1, Pallas kernels, body(): call(prepare_kernel, [SMEM] * 4 + [HBM] * 3, [square, square, footprints....  4.01 us
    pallas_call x1, Pallas kernels, body(): call(functools.partial(second_kernel, masks, name_masks), [SMEM] * 2 + [V...  2.99 us
    pallas_call x1, Pallas kernels, body(): call(functools.partial(third_kernel, masks, name_masks), [SMEM] * 2 + [VM...  2.7 us
    pallas_call x1, Pallas kernels, body(): call(functools.partial(first_kernel, masks), [SMEM] * 2 + [VMEM] * (3 + l...  2.11 us
  transfers between devices with their start and end apart: 30, of which 12 were waited for; matrix products, arithmetic and copies ran while one was open for 0% of the time, Pallas kernels for 5%

profile of v2, /device:TPU:0, one launch (start us, length us, event | category | flops | bytes accessed | tf_op | source)
XLA Modules:
  0.0 79.5 jit_solution(8775484370940776323)
XLA Ops:
  1.3 1.4 %shard_map.105 = (f32[104,256]{1,0:T(8,128)S(1)}, f32[96,128]{1,0:T(8,128)S(1)}) custom-call(s32[4,16]{1,0:T(4,128)S(1)} %bitcast.2, s32[1]{0:T(128)} %bitcast.1.me, f32[32,256]{1,0:T(8,128)} %flux.1, f32[32,256]{1,0:T(8,128)} %prior.1, f32[32,256]{1,0:T(8,128)} %precision.1), custom_call_target="tpu_custom_call" | custom-call | flops 10000 | bytes 98304 | tf_op jit(solution)/shard_map/pallas_call | solution.py:302
  2.7 3.1 %collective-permute-start = (f32[104,256]{1,0:T(8,128)S(1)}, f32[104,256]{1,0:T(8,128)S(1)}, u32[]{:S(2)}, u32[]{:S(2)}) collective-permute-start(f32[104,256]{1,0:T(8,128)S(1)} %get-tuple-element.20.refs_0_.bundle), channel_id=1, source_target_pairs={{0,4},{1,5},{2,6},{3,7},{4,0},{5,1},{6,2},{7,3},{8,12},{9,13},{10,... | collective-permute-start | bytes 319496 | tf_op jit(solution)/shard_map/ppermute | solution.py:32
  5.8 2.5 %collective-permute-start.2 = (f32[104,256]{1,0:T(8,128)S(1)}, f32[104,256]{1,0:T(8,128)S(1)}, u32[]{:S(2)}, u32[]{:S(2)}) collective-permute-start(f32[104,256]{1,0:T(8,128)S(1)} %get-tuple-element.20.refs_0_.bundle), channel_id=1, source_target_pairs={{0,12},{1,13},{2,14},{3,15},{4,8},{5,9},{6,10},{7,11},{8,4},{9,5},... | collective-permute-start | bytes 319496 | tf_op jit(solution)/shard_map/ppermute | solution.py:32
  9.7 4.0 %shard_map.104 = (f32[128,128]{1,0:T(8,128)S(1)}, f32[128,128]{1,0:T(8,128)S(1)}, f32[16,4,128,256]{3,2,1,0:T(8,128)S(1)}) custom-call(s32[4,16]{1,0:T(4,128)S(1)} %bitcast.3, s32[1]{0:T(128)} %bitcast.1.me, f32[8]{0:T(128)S(1)} %copy-done.2, s32[1]{0:T(128)S(6)} %copy.11.counts, s32[16,128]{1,0:T(8,128)} %week_ids.1, f32[16,128]{1,0:T(8,128)} %observed.1, ...), custom_call_target="tpu_custom_call" | custom-call | flops 10000 | bytes 16777216 | tf_op jit(solution)/shard_map/pallas_call | solution.py:306
  13.8 1.6 %collective-permute-start.3 = (f32[64,256]{1,0:T(8,128)S(1)}, f32[64,256]{1,0:T(8,128)S(1)}, u32[]{:S(2)}, u32[]{:S(2)}) collective-permute-start(f32[64,256]{1,0:T(8,128)S(1)} %shard_map.106.refs_0_), channel_id=1, source_target_pairs={{0,2},{1,3},{2,0},{3,1},{4,6},{5,7},{6,4},{7,5},{8,10},{9,11},{10,... | collective-permute-start | bytes 196616 | tf_op jit(solution)/shard_map/ppermute | solution.py:32
  15.3 2.6 %collective-permute-done.1.refs_0_.refs_2_ = f32[104,256]{1,0:T(8,128)S(1)} collective-permute-done((f32[104,256]{1,0:T(8,128)S(1)}, f32[104,256]{1,0:T(8,128)S(1)}, u32[]{:S(2)}, u32[]{:S(2)}) %collective-permute-start.1) | collective-permute-done | bytes 106528 | tf_op jit(solution)/shard_map/ppermute | solution.py:32
  17.9 1.5 %collective-permute-start.4 = (f32[64,256]{1,0:T(8,128)S(1)}, f32[64,256]{1,0:T(8,128)S(1)}, u32[]{:S(2)}, u32[]{:S(2)}) collective-permute-start(f32[64,256]{1,0:T(8,128)S(1)} %shard_map.107.refs_1_), channel_id=1, source_target_pairs={{0,2},{1,3},{2,0},{3,1},{4,6},{5,7},{6,4},{7,5},{8,10},{9,11},{10,... | collective-permute-start | bytes 196616 | tf_op jit(solution)/shard_map/ppermute | solution.py:32
  20.0 2.2 %collective-permute-done.4.refs_3_ = f32[64,256]{1,0:T(8,128)S(1)} collective-permute-done((f32[64,256]{1,0:T(8,128)S(1)}, f32[64,256]{1,0:T(8,128)S(1)}, u32[]{:S(2)}, u32[]{:S(2)}) %collective-permute-start.4) | collective-permute-done | bytes 65568 | tf_op jit(solution)/shard_map/ppermute | solution.py:32
  23.5 2.1 %shard_map.108 = (f32[64,256]{1,0:T(8,128)S(1)}, f32[128,128]{1,0:T(8,128)S(1)}) custom-call(s32[4,16]{1,0:T(4,128)S(1)} %bitcast.4, s32[1]{0:T(128)} %bitcast.1.me, f32[16,4,128,256]{3,2,1,0:T(8,128)S(1)} %get-tuple-element.17.tiles, f32[128,128]{1,0:T(8,128)S(1)} %get-tuple-element.18.refs_2_.weights, f32[128,128]{1,0:T(8,128)S(1)} %get-tuple-element.21.observed, ...), custom_call_target="tpu_custom_call" | custom-call | flops 8388608 | bytes 8388608 | tf_op jit(solution)/shard_map/pallas_call | solution.py:319
  25.6 1.6 %collective-permute-start.18 = (f32[288,256]{1,0:T(8,128)S(1)}, f32[288,256]{1,0:T(8,128)S(1)}, u32[]{:S(2)}, u32[]{:S(2)}) collective-permute-start(f32[288,256]{1,0:T(8,128)S(1)} %shard_map.111.refs_8_), channel_id=1, source_target_pairs={{0,2},{1,3},{2,0},{3,1},{4,6},{5,7},{6,4},{7,5},{8,10},{9,11},{10,... | collective-permute-start | bytes 884744 | tf_op jit(solution)/shard_map/ppermute | solution.py:32
  27.2 2.6 %collective-permute-start.11 = (f32[64,256]{1,0:T(8,128)S(1)}, f32[64,256]{1,0:T(8,128)S(1)}, u32[]{:S(2)}, u32[]{:S(2)}) collective-permute-start(f32[64,256]{1,0:T(8,128)S(1)} %get-tuple-element.22.refs_0_.refs_2_.refs_4_), channel_id=1, source_target_pairs={{0,12},{1,13},{2,14},{3,15},{4,8},{5,9},{6,10},{7,11},{8,4},{9,5},... | collective-permute-start | bytes 196616 | tf_op jit(solution)/shard_map/ppermute | solution.py:32
  30.7 4.1 %collective-permute-done.18.refs_9_ = f32[288,256]{1,0:T(8,128)S(1)} collective-permute-done((f32[288,256]{1,0:T(8,128)S(1)}, f32[288,256]{1,0:T(8,128)S(1)}, u32[]{:S(2)}, u32[]{:S(2)}) %collective-permute-start.18) | collective-permute-done | bytes 294944 | tf_op jit(solution)/shard_map/ppermute | solution.py:32
  35.3 1.6 %collective-permute-start.12 = (f32[128,256]{1,0:T(8,128)S(1)}, f32[128,256]{1,0:T(8,128)S(1)}, u32[]{:S(2)}, u32[]{:S(2)}) collective-permute-start(f32[128,256]{1,0:T(8,128)S(1)} %shard_map.109.refs_0_), channel_id=1, source_target_pairs={{0,2},{1,3},{2,0},{3,1},{4,6},{5,7},{6,4},{7,5},{8,10},{9,11},{10,... | collective-permute-start | bytes 393224 | tf_op jit(solution)/shard_map/ppermute | solution.py:32
  37.4 4.2 %collective-permute-done.12.refs_2_ = f32[128,256]{1,0:T(8,128)S(1)} collective-permute-done((f32[128,256]{1,0:T(8,128)S(1)}, f32[128,256]{1,0:T(8,128)S(1)}, u32[]{:S(2)}, u32[]{:S(2)}) %collective-permute-start.12) | collective-permute-done | bytes 131104 | tf_op jit(solution)/shard_map/ppermute | solution.py:32
  41.7 1.9 %collective-permute-done.13.refs_3_ = f32[128,256]{1,0:T(8,128)S(1)} collective-permute-done((f32[128,256]{1,0:T(8,128)S(1)}, f32[128,256]{1,0:T(8,128)S(1)}, u32[]{:S(2)}, u32[]{:S(2)}) %collective-permute-start.13) | collective-permute-done | bytes 131104 | tf_op jit(solution)/shard_map/ppermute | solution.py:32
  45.0 3.0 %shard_map.112 = (f32[72,256]{1,0:T(8,128)S(1)}, f32[96,256]{1,0:T(8,128)S(1)}, f32[128,128]{1,0:T(8,128)S(1)}) custom-call(s32[4,16]{1,0:T(4,128)S(1)} %bitcast.5, s32[1]{0:T(128)} %bitcast.1.me, f32[16,4,128,256]{3,2,1,0:T(8,128)S(1)} %get-tuple-element.17.tiles, f32[128,128]{1,0:T(8,128)S(1)} %get-tuple-element.18.refs_2_.weights, ...), custom_call_target="tpu_custom_call" | custom-call | flops 8388608 | bytes 8388608 | tf_op jit(solution)/shard_map/pallas_call | solution.py:328
  48.1 2.7 %collective-permute-start.23 = (f32[72,256]{1,0:T(8,128)S(1)}, f32[72,256]{1,0:T(8,128)S(1)}, u32[]{:S(2)}, u32[]{:S(2)}) collective-permute-start(f32[72,256]{1,0:T(8,128)S(1)} %get-tuple-element.26.refs_0_.refs_2_), channel_id=1, source_target_pairs={{0,12},{1,13},{2,14},{3,15},{4,8},{5,9},{6,10},{7,11},{8,4},{9,5},... | collective-permute-start | bytes 221192 | tf_op jit(solution)/shard_map/ppermute | solution.py:32
  52.4 1.6 %collective-permute-start.24 = (f32[144,256]{1,0:T(8,128)S(1)}, f32[144,256]{1,0:T(8,128)S(1)}, u32[]{:S(2)}, u32[]{:S(2)}) collective-permute-start(f32[144,256]{1,0:T(8,128)S(1)} %shard_map.113.refs_0_), channel_id=1, source_target_pairs={{0,2},{1,3},{2,0},{3,1},{4,6},{5,7},{6,4},{7,5},{8,10},{9,11},{10,... | collective-permute-start | bytes 442376 | tf_op jit(solution)/shard_map/ppermute | solution.py:32
  54.0 1.4 %collective-permute-done.23.refs_1_ = f32[72,256]{1,0:T(8,128)S(1)} collective-permute-done((f32[72,256]{1,0:T(8,128)S(1)}, f32[72,256]{1,0:T(8,128)S(1)}, u32[]{:S(2)}, u32[]{:S(2)}) %collective-permute-start.23) | collective-permute-done | bytes 73760 | tf_op jit(solution)/shard_map/ppermute | solution.py:32
  55.4 3.0 %collective-permute-done.22.refs_0_ = f32[72,256]{1,0:T(8,128)S(1)} collective-permute-done((f32[72,256]{1,0:T(8,128)S(1)}, f32[72,256]{1,0:T(8,128)S(1)}, u32[]{:S(2)}, u32[]{:S(2)}) %collective-permute-start.22) | collective-permute-done | bytes 73760 | tf_op jit(solution)/shard_map/ppermute | solution.py:32
  58.5 1.6 %collective-permute-start.25 = (f32[144,256]{1,0:T(8,128)S(1)}, f32[144,256]{1,0:T(8,128)S(1)}, u32[]{:S(2)}, u32[]{:S(2)}) collective-permute-start(f32[144,256]{1,0:T(8,128)S(1)} %shard_map.114.refs_1_), channel_id=1, source_target_pairs={{0,2},{1,3},{2,0},{3,1},{4,6},{5,7},{6,4},{7,5},{8,10},{9,11},{10,... | collective-permute-start | bytes 442376 | tf_op jit(solution)/shard_map/ppermute | solution.py:32
  60.6 3.5 %collective-permute-done.25.refs_3_ = f32[144,256]{1,0:T(8,128)S(1)} collective-permute-done((f32[144,256]{1,0:T(8,128)S(1)}, f32[144,256]{1,0:T(8,128)S(1)}, u32[]{:S(2)}, u32[]{:S(2)}) %collective-permute-start.25) | collective-permute-done | bytes 147488 | tf_op jit(solution)/shard_map/ppermute | solution.py:32
  65.4 2.7 %shard_map.115 = (f32[16,1,128]{2,1,0:T(1,128)S(1)}, f32[32,256]{1,0:T(8,128)S(1)}, f32[32,256]{1,0:T(8,128)S(1)}, f32[16,128]{1,0:T(8,128)S(1)}, f32[16,128]{1,0:T(8,128)S(1)}) custom-call(s32[4,16]{1,0:T(4,128)S(1)} %bitcast.6, s32[1]{0:T(128)} %bitcast.1.me, f32[16,4,128,256]{3,2,1,0:T(8,128)S(1)} %get-tuple-element.17.tiles, ...), custom_call_target="tpu_custom_call" | custom-call | flops 8388608 | bytes 8388608 | tf_op jit(solution)/shard_map/pallas_call | solution.py:334
  68.1 10.7 %all_to_all.5.sums = f32[16,1,128]{2,1,0:T(1,128)S(1)} all-to-all(f32[16,1,128]{2,1,0:T(1,128)S(1)} %get-tuple-element.27), channel_id=1, replica_groups=mesh['groups'=2,'obs'=16] {'obs'}, dimensions={0} | all-to-all | bytes 16384 | tf_op jit(solution)/shard_map/all_to_all | solution.py:340
  (56 shorter events, 10.9 us)
Async XLA Ops:
  2.7 11.0 %collective-permute-start = (f32[104,256]{1,0:T(8,128)S(1)}, f32[104,256]{1,0:T(8,128)S(1)}, u32[]{:S(2)}, u32[]{:S(2)}) collective-permute-start(f32[104,256]{1,0:T(8,128)S(1)} %get-tuple-element.20.refs_0_.bundle), channel_id=1, source_target_pairs={{0,4},{1,5},{2,6},{3,7},{4,0},{5,1},{6,2},{7,3},{8,12},{9,13},{10,... | collective-permute-start | bytes 319496 | tf_op jit(solution)/shard_map/ppermute | solution.py:32
  5.8 9.5 %collective-permute-start.2 = (f32[104,256]{1,0:T(8,128)S(1)}, f32[104,256]{1,0:T(8,128)S(1)}, u32[]{:S(2)}, u32[]{:S(2)}) collective-permute-start(f32[104,256]{1,0:T(8,128)S(1)} %get-tuple-element.20.refs_0_.bundle), channel_id=1, source_target_pairs={{0,12},{1,13},{2,14},{3,15},{4,8},{5,9},{6,10},{7,11},{8,4},{9,5},... | collective-permute-start | bytes 319496 | tf_op jit(solution)/shard_map/ppermute | solution.py:32
  8.3 9.6 %collective-permute-start.1 = (f32[104,256]{1,0:T(8,128)S(1)}, f32[104,256]{1,0:T(8,128)S(1)}, u32[]{:S(2)}, u32[]{:S(2)}) collective-permute-start(f32[104,256]{1,0:T(8,128)S(1)} %get-tuple-element.20.refs_0_.bundle), channel_id=1, source_target_pairs={{0,8},{1,9},{2,10},{3,11},{4,12},{5,13},{6,14},{7,15},{8,0},{9,1},... | collective-permute-start | bytes 319496 | tf_op jit(solution)/shard_map/ppermute | solution.py:32
  13.8 6.2 %collective-permute-start.3 = (f32[64,256]{1,0:T(8,128)S(1)}, f32[64,256]{1,0:T(8,128)S(1)}, u32[]{:S(2)}, u32[]{:S(2)}) collective-permute-start(f32[64,256]{1,0:T(8,128)S(1)} %shard_map.106.refs_0_), channel_id=1, source_target_pairs={{0,2},{1,3},{2,0},{3,1},{4,6},{5,7},{6,4},{7,5},{8,10},{9,11},{10,... | collective-permute-start | bytes 196616 | tf_op jit(solution)/shard_map/ppermute | solution.py:32
  17.9 4.3 %collective-permute-start.4 = (f32[64,256]{1,0:T(8,128)S(1)}, f32[64,256]{1,0:T(8,128)S(1)}, u32[]{:S(2)}, u32[]{:S(2)}) collective-permute-start(f32[64,256]{1,0:T(8,128)S(1)} %shard_map.107.refs_1_), channel_id=1, source_target_pairs={{0,2},{1,3},{2,0},{3,1},{4,6},{5,7},{6,4},{7,5},{8,10},{9,11},{10,... | collective-permute-start | bytes 196616 | tf_op jit(solution)/shard_map/ppermute | solution.py:32
  19.5 2.8 %collective-permute-start.5 = (f32[64,256]{1,0:T(8,128)S(1)}, f32[64,256]{1,0:T(8,128)S(1)}, u32[]{:S(2)}, u32[]{:S(2)}) collective-permute-start(f32[64,256]{1,0:T(8,128)S(1)} %shard_map.106.refs_0_), channel_id=1, source_target_pairs={{0,1},{1,0},{2,3},{3,2},{4,5},{5,4},{6,7},{7,6},{8,9},{9,8},{10,11... | collective-permute-start | bytes 196616 | tf_op jit(solution)/shard_map/ppermute | solution.py:32
  19.5 2.8 %collective-permute-start.6 = (f32[64,256]{1,0:T(8,128)S(1)}, f32[64,256]{1,0:T(8,128)S(1)}, u32[]{:S(2)}, u32[]{:S(2)}) collective-permute-start(f32[64,256]{1,0:T(8,128)S(1)} %shard_map.107.refs_1_), channel_id=1, source_target_pairs={{0,1},{1,0},{2,3},{3,2},{4,5},{5,4},{6,7},{7,6},{8,9},{9,8},{10,11... | collective-permute-start | bytes 196616 | tf_op jit(solution)/shard_map/ppermute | solution.py:32
  25.6 9.1 %collective-permute-start.18 = (f32[288,256]{1,0:T(8,128)S(1)}, f32[288,256]{1,0:T(8,128)S(1)}, u32[]{:S(2)}, u32[]{:S(2)}) collective-permute-start(f32[288,256]{1,0:T(8,128)S(1)} %shard_map.111.refs_8_), channel_id=1, source_target_pairs={{0,2},{1,3},{2,0},{3,1},{4,6},{5,7},{6,4},{7,5},{8,10},{9,11},{10,... | collective-permute-start | bytes 884744 | tf_op jit(solution)/shard_map/ppermute | solution.py:32
  27.2 7.6 %collective-permute-start.9 = (f32[64,256]{1,0:T(8,128)S(1)}, f32[64,256]{1,0:T(8,128)S(1)}, u32[]{:S(2)}, u32[]{:S(2)}) collective-permute-start(f32[64,256]{1,0:T(8,128)S(1)} %get-tuple-element.22.refs_0_.refs_2_.refs_4_), channel_id=1, source_target_pairs={{0,4},{1,5},{2,6},{3,7},{4,0},{5,1},{6,2},{7,3},{8,12},{9,13},{10,... | collective-permute-start | bytes 196616 | tf_op jit(solution)/shard_map/ppermute | solution.py:32
  27.2 8.1 %collective-permute-start.11 = (f32[64,256]{1,0:T(8,128)S(1)}, f32[64,256]{1,0:T(8,128)S(1)}, u32[]{:S(2)}, u32[]{:S(2)}) collective-permute-start(f32[64,256]{1,0:T(8,128)S(1)} %get-tuple-element.22.refs_0_.refs_2_.refs_4_), channel_id=1, source_target_pairs={{0,12},{1,13},{2,14},{3,15},{4,8},{5,9},{6,10},{7,11},{8,4},{9,5},... | collective-permute-start | bytes 196616 | tf_op jit(solution)/shard_map/ppermute | solution.py:32
  29.8 7.1 %collective-permute-start.10 = (f32[64,256]{1,0:T(8,128)S(1)}, f32[64,256]{1,0:T(8,128)S(1)}, u32[]{:S(2)}, u32[]{:S(2)}) collective-permute-start(f32[64,256]{1,0:T(8,128)S(1)} %get-tuple-element.22.refs_0_.refs_2_.refs_4_), channel_id=1, source_target_pairs={{0,8},{1,9},{2,10},{3,11},{4,12},{5,13},{6,14},{7,15},{8,0},{9,1},... | collective-permute-start | bytes 196616 | tf_op jit(solution)/shard_map/ppermute | solution.py:32
  30.7 13.0 %collective-permute-start.19 = (f32[288,256]{1,0:T(8,128)S(1)}, f32[288,256]{1,0:T(8,128)S(1)}, u32[]{:S(2)}, u32[]{:S(2)}) collective-permute-start(f32[288,256]{1,0:T(8,128)S(1)} %shard_map.111.refs_8_), channel_id=1, source_target_pairs={{0,1},{1,0},{2,3},{3,2},{4,5},{5,4},{6,7},{7,6},{8,9},{9,8},{10,11... | collective-permute-start | bytes 884744 | tf_op jit(solution)/shard_map/ppermute | solution.py:32
  34.7 10.2 %collective-permute-start.20 = (f32[288,256]{1,0:T(8,128)S(1)}, f32[288,256]{1,0:T(8,128)S(1)}, u32[]{:S(2)}, u32[]{:S(2)}) collective-permute-start(f32[288,256]{1,0:T(8,128)S(1)} %collective-permute-done.18.refs_9_), channel_id=1, source_target_pairs={{0,1},{1,0},{2,3},{3,2},{4,5},{5,4},{6,7},{7,6},{8,9},{9,8},{10,11... | collective-permute-start | bytes 884744 | tf_op jit(solution)/shard_map/ppermute | solution.py:32
  35.3 6.4 %collective-permute-start.12 = (f32[128,256]{1,0:T(8,128)S(1)}, f32[128,256]{1,0:T(8,128)S(1)}, u32[]{:S(2)}, u32[]{:S(2)}) collective-permute-start(f32[128,256]{1,0:T(8,128)S(1)} %shard_map.109.refs_0_), channel_id=1, source_target_pairs={{0,2},{1,3},{2,0},{3,1},{4,6},{5,7},{6,4},{7,5},{8,10},{9,11},{10,... | collective-permute-start | bytes 393224 | tf_op jit(solution)/shard_map/ppermute | solution.py:32
  36.9 6.7 %collective-permute-start.13 = (f32[128,256]{1,0:T(8,128)S(1)}, f32[128,256]{1,0:T(8,128)S(1)}, u32[]{:S(2)}, u32[]{:S(2)}) collective-permute-start(f32[128,256]{1,0:T(8,128)S(1)} %shard_map.110.refs_1_), channel_id=1, source_target_pairs={{0,2},{1,3},{2,0},{3,1},{4,6},{5,7},{6,4},{7,5},{8,10},{9,11},{10,... | collective-permute-start | bytes 393224 | tf_op jit(solution)/shard_map/ppermute | solution.py:32
  37.4 6.2 %collective-permute-start.15 = (f32[128,256]{1,0:T(8,128)S(1)}, f32[128,256]{1,0:T(8,128)S(1)}, u32[]{:S(2)}, u32[]{:S(2)}) collective-permute-start(f32[128,256]{1,0:T(8,128)S(1)} %shard_map.110.refs_1_), channel_id=1, source_target_pairs={{0,1},{1,0},{2,3},{3,2},{4,5},{5,4},{6,7},{7,6},{8,9},{9,8},{10,11... | collective-permute-start | bytes 393224 | tf_op jit(solution)/shard_map/ppermute | solution.py:32
  48.0 4.4 %collective-permute-start.21 = (f32[72,256]{1,0:T(8,128)S(1)}, f32[72,256]{1,0:T(8,128)S(1)}, u32[]{:S(2)}, u32[]{:S(2)}) collective-permute-start(f32[72,256]{1,0:T(8,128)S(1)} %get-tuple-element.26.refs_0_.refs_2_), channel_id=1, source_target_pairs={{0,4},{1,5},{2,6},{3,7},{4,0},{5,1},{6,2},{7,3},{8,12},{9,13},{10,... | collective-permute-start | bytes 221192 | tf_op jit(solution)/shard_map/ppermute | solution.py:32
  48.1 7.4 %collective-permute-start.23 = (f32[72,256]{1,0:T(8,128)S(1)}, f32[72,256]{1,0:T(8,128)S(1)}, u32[]{:S(2)}, u32[]{:S(2)}) collective-permute-start(f32[72,256]{1,0:T(8,128)S(1)} %get-tuple-element.26.refs_0_.refs_2_), channel_id=1, source_target_pairs={{0,12},{1,13},{2,14},{3,15},{4,8},{5,9},{6,10},{7,11},{8,4},{9,5},... | collective-permute-start | bytes 221192 | tf_op jit(solution)/shard_map/ppermute | solution.py:32
  50.8 7.7 %collective-permute-start.22 = (f32[72,256]{1,0:T(8,128)S(1)}, f32[72,256]{1,0:T(8,128)S(1)}, u32[]{:S(2)}, u32[]{:S(2)}) collective-permute-start(f32[72,256]{1,0:T(8,128)S(1)} %get-tuple-element.26.refs_0_.refs_2_), channel_id=1, source_target_pairs={{0,8},{1,9},{2,10},{3,11},{4,12},{5,13},{6,14},{7,15},{8,0},{9,1},... | collective-permute-start | bytes 221192 | tf_op jit(solution)/shard_map/ppermute | solution.py:32
  52.4 8.2 %collective-permute-start.24 = (f32[144,256]{1,0:T(8,128)S(1)}, f32[144,256]{1,0:T(8,128)S(1)}, u32[]{:S(2)}, u32[]{:S(2)}) collective-permute-start(f32[144,256]{1,0:T(8,128)S(1)} %shard_map.113.refs_0_), channel_id=1, source_target_pairs={{0,2},{1,3},{2,0},{3,1},{4,6},{5,7},{6,4},{7,5},{8,10},{9,11},{10,... | collective-permute-start | bytes 442376 | tf_op jit(solution)/shard_map/ppermute | solution.py:32
  58.5 5.6 %collective-permute-start.25 = (f32[144,256]{1,0:T(8,128)S(1)}, f32[144,256]{1,0:T(8,128)S(1)}, u32[]{:S(2)}, u32[]{:S(2)}) collective-permute-start(f32[144,256]{1,0:T(8,128)S(1)} %shard_map.114.refs_1_), channel_id=1, source_target_pairs={{0,2},{1,3},{2,0},{3,1},{4,6},{5,7},{6,4},{7,5},{8,10},{9,11},{10,... | collective-permute-start | bytes 442376 | tf_op jit(solution)/shard_map/ppermute | solution.py:32
  60.1 4.0 %collective-permute-start.26 = (f32[144,256]{1,0:T(8,128)S(1)}, f32[144,256]{1,0:T(8,128)S(1)}, u32[]{:S(2)}, u32[]{:S(2)}) collective-permute-start(f32[144,256]{1,0:T(8,128)S(1)} %shard_map.113.refs_0_), channel_id=1, source_target_pairs={{0,1},{1,0},{2,3},{3,2},{4,5},{5,4},{6,7},{7,6},{8,9},{9,8},{10,11... | collective-permute-start | bytes 442376 | tf_op jit(solution)/shard_map/ppermute | solution.py:32
  60.1 4.0 %collective-permute-start.27 = (f32[144,256]{1,0:T(8,128)S(1)}, f32[144,256]{1,0:T(8,128)S(1)}, u32[]{:S(2)}, u32[]{:S(2)}) collective-permute-start(f32[144,256]{1,0:T(8,128)S(1)} %shard_map.114.refs_1_), channel_id=1, source_target_pairs={{0,1},{1,0},{2,3},{3,2},{4,5},{5,4},{6,7},{7,6},{8,9},{9,8},{10,11... | collective-permute-start | bytes 442376 | tf_op jit(solution)/shard_map/ppermute | solution.py:32
  60.6 3.5 %collective-permute-start.28 = (f32[144,256]{1,0:T(8,128)S(1)}, f32[144,256]{1,0:T(8,128)S(1)}, u32[]{:S(2)}, u32[]{:S(2)}) collective-permute-start(f32[144,256]{1,0:T(8,128)S(1)} %collective-permute-done.24.refs_2_), channel_id=1, source_target_pairs={{0,1},{1,0},{2,3},{3,2},{4,5},{5,4},{6,7},{7,6},{8,9},{9,8},{10,11... | collective-permute-start | bytes 442376 | tf_op jit(solution)/shard_map/ppermute | solution.py:32
  (9 other events, 47.5 us)

commit v3 on v2

v3 whole, which is shorter than its diff:
```python
import functools

import jax
import jax.numpy as jnp
from jax import lax
from jax.experimental import pallas as pl
from jax.experimental.pallas import tpu as pltpu
from jax.sharding import PartitionSpec as P

VMEM = pl.BlockSpec(memory_space=pltpu.VMEM)
SMEM = pl.BlockSpec(memory_space=pltpu.SMEM)
ANY = pl.BlockSpec(memory_space=pl.ANY)
HBM = pl.BlockSpec(memory_space=pltpu.HBM)
LIMIT = 24 * 1024 * 1024
F32 = jnp.float32
LONG = 20000000


def stage_masks(n):
    stages, low = [], 1
    while low < n:
        if low < 4 or low * 4 > n:
            stages.append([low])
            low *= 2
        else:
            stages.append([low, 2 * low, 3 * low])
            low *= 4
    return stages[::-1]


def swap(x, mask):
    n = lax.axis_size("obs")
    return lax.ppermute(x, "obs", [(i, i ^ mask) for i in range(n)])


def shift(masks, mask):
    return [m ^ mask for m in masks]


def call(kernel, ins, outs, scratch=(), flops=0, moved=0, pinned=False, aliases=()):
    return pl.pallas_call(
        kernel,
        input_output_aliases=dict(aliases),
        out_shape=[pltpu.VMEM(s, F32) if pinned and len(s) == 4 else jax.ShapeDtypeStruct(s, F32) for s in outs],
        in_specs=ins,
        out_specs=[VMEM] * len(outs),
        scratch_shapes=list(scratch),
        compiler_params=pltpu.CompilerParams(vmem_limit_bytes=LIMIT),
        cost_estimate=pl.CostEstimate(flops=flops, bytes_accessed=moved, transcendentals=0),
    )


def pile_kernel(cuts, *refs):
    *arrays, _, pile_out = refs
    i = 0
    for array, (pitch, at, rows) in zip(arrays, cuts, strict=True):
        for start in range(0, array.shape[0], pitch):
            pile_out[i:i + rows, :] = array[start + at:start + at + rows, :]
            i += rows


def pile(arrays, cuts, after, cost=0):
    total = sum(a.shape[0] // pitch * rows for a, (pitch, _, rows) in zip(arrays, cuts, strict=True))
    cols = arrays[0].shape[1]
    return call(
        functools.partial(pile_kernel, cuts), [VMEM] * len(arrays) + [ANY], [(total, cols)],
        moved=max(8 * total * cols, cost), flops=cost * 300,
    )(*arrays, after)[0]


def lead_stages(x):
    masks, cut = [0], (x.shape[0], 0, x.shape[0])
    for stage in stage_masks(lax.axis_size("obs"))[:-3]:
        x = pile([x] + [swap(x, m) for m in stage], [cut] * (1 + len(stage)), x)
        masks = masks + [k for m in stage for k in shift(masks, m)]
    return x, masks


class Part:
    def __init__(self, array, masks, rest_masks=()):
        self.array, self.masks, self.rest_masks = array, tuple(masks), tuple(rest_masks)

    def swap(self, mask):
        return Part(swap(self.array, mask), shift(self.masks, mask), shift(self.rest_masks, mask))


def near_stages(first, second, wait=None):
    (pair,), (core,) = stage_masks(lax.axis_size("obs"))[-2:]
    parts = [first, first.swap(pair)]
    later = second(None)
    other = later.swap(pair)
    after, cost = (first.array, LONG) if wait is None else (wait(later.array), 0)
    whole = (other.array.shape[0], 0, other.array.shape[0])
    parts = parts + [later, Part(pile([other.array], [whole], after, cost), other.masks)]
    return parts + [p.swap(core) for p in parts]


def spread(x, rest, at, rows):
    size = x.shape[0]
    cut = (size, 0, size)
    x, masks = lead_stages(x)
    arrays, held, pitch = rest
    near, far, both = stage_masks(lax.axis_size("obs"))[-3]
    few = (pitch, at, rows)
    beyond, across = swap(x, far), swap(x, both)
    beside = swap(pile([x, arrays[2]], [cut, few], x), near)
    count = len(masks) * size
    first = pile(
        [x, beside, *arrays, beside],
        [(count, 0, count), (beside.shape[0], 0, count)] + [few] * 3 + [(beside.shape[0], count, beside.shape[0] - count)], x)
    first = Part(first, masks + shift(masks, near), held + shift(held, near) + shift(held, far) + shift(held, both))
    return near_stages(
        first, lambda _: Part(pile([beyond, across], [cut] * 2, x, LONG), shift(masks, far) + shift(masks, both)))


def spread_bundle(flux, bundle, own, ready, wait):
    pitch = bundle.shape[0]
    x, masks = lead_stages(bundle)
    near, far, both = stage_masks(lax.axis_size("obs"))[-3]
    cut = (pitch, 0, own)
    lone = flux if len(masks) == 1 else pile([x], [cut], x)
    across, beyond, beside = swap(lone, both), swap(x, far), swap(x, near)
    first = Part(pile([x, beside], [cut] * 2, ready), masks + shift(masks, near))
    parts = near_stages(first, lambda after: Part(
        pile([beyond, across], [cut, (own, 0, own)], ready), shift(masks, far) + shift(masks, both)), wait)
    return parts, ((x, beside, beyond), masks, pitch)


def bundle_kernel(ids, me, flux, prior, precision, bundle_out, want_out, prior_in, tile_ids, sem):
    each, blocks = tile_ids.shape
    count = blocks * each
    own, cols = flux.shape
    first = pltpu.make_async_copy(ids, tile_ids, sem.at[3])
    first.start()
    copies = [
        pltpu.make_async_copy(flux, bundle_out.at[pl.ds(0, own)], sem.at[0]),
        pltpu.make_async_copy(precision, bundle_out.at[pl.ds(2 * own + 8, own)], sem.at[1]),
        pltpu.make_async_copy(prior, prior_in, sem.at[2]),
    ]
    for c in copies:
        c.start()
    first.wait()
    lane = lax.broadcasted_iota(jnp.int32, (8, cols), 1) % count
    tall = lax.broadcasted_iota(jnp.int32, want_out.shape, 0)
    across = jnp.zeros((8, cols), jnp.int32)
    down = me[0] * own + tall - count
    for t in range(count):
        tile = tile_ids[t % each, t // each]
        across = jnp.where(lane == t, tile, across)
        down = jnp.where(tall == t, tile, down)
    bundle_out[2 * own:2 * own + 8, :] = across.astype(F32)
    want_out[...] = down.astype(F32)
    for c in copies:
        c.wait()
    bundle_out[own:2 * own, :] = bundle_out[2 * own + 8:, :] * (bundle_out[:own, :] - prior_in[...])


def prepare_kernel(counts, table_in, week_ids, observed, footprints, w_out, y_out, tiles_out,
                   week_weight, ids_in, y_in, sem):
    small = [
        pltpu.make_async_copy(week_ids, ids_in, sem.at[0]),
        pltpu.make_async_copy(table_in, week_weight, sem.at[2 + week_ids.shape[0] // 4]),
        pltpu.make_async_copy(observed, y_in, sem.at[1]),
    ]
    large = [
        pltpu.make_async_copy(footprints.at[pl.ds(i, 2)], tiles_out.at[pl.ds(i, 2)], sem.at[2 + i // 2])
        for i in range(0, footprints.shape[0] // 2, 2)
    ]
    for c in small:
        c.start()
    for c in large:
        c.start()
    for c in small:
        c.wait()
    blocks, rows = week_ids.shape
    ids = ids_in[...]
    table = jnp.zeros(ids.shape, F32)
    for week in range(week_weight.shape[0]):
        table = jnp.where(ids == week, week_weight[week], table)
    position = lax.broadcasted_iota(jnp.int32, ids.shape, 0) * rows + lax.broadcasted_iota(jnp.int32, ids.shape, 1)
    weights = jnp.where(position < counts[0], table, 0.0)
    fill = jnp.zeros((rows - blocks, rows), F32)
    w_out[...] = jnp.concatenate([weights, fill], axis=0).T
    y_out[...] = jnp.concatenate([y_in[...], fill], axis=0).T
    for c in large:
        c.wait()


def rest_kernel(footprints, tiles_in, after, tiles_out, done_out, sem):
    del tiles_in, after
    done_out[...] = jnp.zeros_like(done_out)
    half = footprints.shape[0] // 2
    copies = [
        pltpu.make_async_copy(footprints.at[pl.ds(i, 2)], tiles_out.at[pl.ds(i, 2)], sem.at[(i - half) // 2])
        for i in range(half, 2 * half, 2)
    ]
    for c in copies:
        c.start()
    for c in copies:
        c.wait()


def by_owner(me, pieces, rows, into):
    for m, ref, at in pieces:
        into[pl.ds(pl.multiple_of((me ^ m) * rows, 8), rows), :] = ref[at:at + rows, :]


def layout(shapes, refs, pitch, rest):
    pieces, others = [], []
    for (masks, rest_masks), ref in zip(shapes, refs, strict=True):
        pieces += [(m, ref, i * pitch) for i, m in enumerate(masks)]
        others += [(m, ref, len(masks) * pitch + i * rest) for i, m in enumerate(rest_masks)]
    return pieces, others


def forward_block(tiles, values, lane, b, minus):
    total = None
    for k, v in enumerate(values):
        part = tiles[b, k] * v
        total = part if total is None else total + part
    half = total.shape[1] // 2
    total = total[:, :half] + total[:, half:]
    if minus is not None:
        total = total - jnp.where(lane == b, minus, 0.0)
    return jnp.sum(total, axis=1, keepdims=True)


def transpose_block(tiles, weights, column, lane, b, terms_out):
    w = jnp.sum(jnp.where(lane == b, weights[...], 0.0), axis=1, keepdims=True)
    scaled = w * column
    each = tiles.shape[1]
    for k in range(each):
        terms_out[pl.ds(b * each + k, 1), :] = jnp.sum(tiles[b, k] * scaled, axis=0, keepdims=True)


def first_kernel(shapes, tile_ids, me, tiles, weights, observed, *refs):
    *parts, terms_out, departure_out, flux = refs
    blocks, each, tile_rows, _ = tiles.shape
    own = parts[0].shape[0] // len(shapes[0][0])
    by_owner(me[0], layout(shapes, parts, own, 0)[0], own, flux)
    lane = lax.broadcasted_iota(jnp.int32, (tile_rows, tile_rows), 1)
    departure_out[...] = jnp.zeros_like(departure_out)

    @pl.loop(0, blocks, unroll=4)
    def _(b):
        values = [flux[pl.ds(tile_ids[k, b], 1), :] for k in range(each)]
        depart = forward_block(tiles, values, lane, b, observed[...])
        departure_out[...] = jnp.where(lane == b, depart, departure_out[...])
        transpose_block(tiles, weights, depart, lane, b, terms_out)


def one_hot(order, names, want, piece, hot):
    lane = lax.broadcasted_iota(jnp.int32, (1, 128), 1)
    wanted = want[...]
    ids = {m: ref[at:at + 1, :128] for m, ref, at in names}
    for j in range(0, len(order), 2):
        pair = jnp.where(lane < piece, ids[order[j]], ids[order[j + 1]])
        hot[:, j * piece:(j + 2) * piece] = jnp.where(wanted == pair, 1.0, 0.0)


def sum_terms(pieces, piece, hot):
    block = jnp.concatenate([ref[at:at + piece, :] for _, ref, at in pieces], axis=0)
    marks = hot[...].astype(jnp.bfloat16)
    total = None
    for _ in range(3):
        part = block.astype(jnp.bfloat16)
        block = block - part.astype(F32)
        sums = jnp.dot(marks, part, preferred_element_type=F32)
        total = sums if total is None else total + sums
    return total


def sums_row(gradient, precision, weights, image, shape):
    square = jnp.sum(gradient * gradient)
    below = jnp.sum(precision * gradient * gradient) + jnp.sum(weights * image * image)
    lane = lax.broadcasted_iota(jnp.int32, shape, 1)
    return jnp.where(lane == 0, square, jnp.where(lane == 1, below, 0.0))


def second_kernel(shapes, tile_ids, me, tiles, weights, want, bundle, *refs):
    parts = refs[:len(shapes)]
    terms_out, gradient_out, image_out, hot, more = refs[len(shapes):]
    blocks, each, tile_rows, _ = tiles.shape
    count = blocks * each
    own = want.shape[0] - count
    pieces, others = layout(shapes, parts, count, own + 8)
    by_owner(me[0], others, own, more)
    one_hot([m for m, _, _ in pieces], [(m, ref, at + own) for m, ref, at in others], want, count, hot)
    lane = lax.broadcasted_iota(jnp.int32, (tile_rows, tile_rows), 1)
    image_out[...] = jnp.zeros_like(image_out)
    gradient_out[...] = sum_terms(pieces, count, hot)
    mine = gradient_out[count:, :] + bundle[own:2 * own, :]
    gradient_out[count:, :] = mine

    @pl.loop(0, blocks, unroll=4)
    def _(b):
        values = []
        for k in range(each):
            t = pl.ds(b * each + k, 1)
            value = gradient_out[t, :] + more[pl.ds(tile_ids[k, b], 1), :]
            gradient_out[t, :] = value
            values.append(value)
        image = forward_block(tiles, values, lane, b, None)
        image_out[...] = jnp.where(lane == b, image, image_out[...])
        transpose_block(tiles, weights, image, lane, b, terms_out)

    terms_out[count:, :] = sums_row(
        mine, bundle[2 * own + 8:3 * own + 8, :], weights[...], image_out[...], (8, terms_out.shape[1]))


def third_kernel(shapes, tile_ids, me, tiles, weights, want, bundle, hot, gradient, departure, image, *refs):
    parts = refs[:len(shapes)]
    sums_out, flux_out, gradient_out, departure_out, image_out, scale, second = refs[len(shapes):]
    blocks, each, tile_rows, _ = tiles.shape
    count = blocks * each
    own = want.shape[0] - count
    pieces, others = layout(shapes, parts, count + 8, own)
    by_owner(me[0], others, own, scale)
    lane = lax.broadcasted_iota(jnp.int32, (tile_rows, tile_rows), 1)
    sums = jnp.zeros((1, 128), F32)
    for _, ref, at in pieces:
        sums = sums + ref[at + count:at + count + 1, :128]
    step = sums[:, 0:1] / sums[:, 1:2]
    second[...] = sum_terms(pieces, count, hot)
    old = gradient[count:, :]
    precision = bundle[2 * own + 8:, :]
    mine = old - step * (second[count:, :] + precision * old)
    gradient_out[...] = mine
    flux_out[...] = bundle[:own, :] - step * old
    second[:count, :] = gradient[:count, :] - step * second[:count, :]

    def block(b, columns):
        values = []
        for k in range(each):
            t = pl.ds(b * each + k, 1)
            values.append(second[t, :] - step * scale[pl.ds(tile_ids[k, b], 1), :] * gradient[t, :])
        return jnp.where(lane == b, forward_block(tiles, values, lane, b, None), columns)

    columns = lax.fori_loop(0, blocks, block, jnp.zeros((tile_rows, tile_rows), F32), unroll=4)
    row = sums_row(mine, precision, weights[...], columns, (1, 128))
    sums_out[...] = jnp.broadcast_to(row[None], sums_out.shape)
    departure_out[...] = (departure[...] - step * image[...]).T[:blocks]
    image_out[...] = columns.T[:blocks]


def last_kernel(sums, flux, gradient, departure, image, flux_out, departure_out):
    total = jnp.sum(sums[...], axis=0)
    step = total[:, 0:1] / total[:, 1:2]
    flux_out[...] = flux[...] - step * gradient[...]
    departure_out[...] = departure[...] - step * image[...]


def body(footprints, tile_index, observed, week_ids, week_weight, counts, flux_start, flux_prior, prior_precision):
    n = lax.axis_size("obs")
    blocks, each, tile_rows, cols = footprints.shape
    own = flux_start.shape[0]
    count = blocks * each
    square = (tile_rows, tile_rows)
    place = (tile_index.T, lax.axis_index("obs").astype(jnp.int32)[None])

    def in_hbm(*arrays):
        return [pltpu.with_memory_space_constraint(x, pltpu.HBM) for x in arrays]

    pitch = 3 * own + 8
    bundle, want = call(
        bundle_kernel, [HBM, SMEM] + [HBM] * 3, [(pitch, cols), (count + own, 128)],
        [pltpu.VMEM((own, cols), F32), pltpu.SMEM((each, blocks), jnp.int32), pltpu.SemaphoreType.DMA((4,))],
        flops=10000, moved=12 * own * cols,
    )(*in_hbm(place[0]), place[1], *in_hbm(flux_start, flux_prior, prior_precision))
    weights, observed_t, tiles = call(
        prepare_kernel, [SMEM] + [HBM] * 4, [square, square, footprints.shape],
        [pltpu.SMEM(week_weight.shape, F32), pltpu.VMEM(week_ids.shape, jnp.int32), pltpu.VMEM(observed.shape, F32),
         pltpu.SemaphoreType.DMA((3 + blocks // 4,))],
        flops=10000, moved=8 * footprints.size, pinned=True,
    )(counts, *in_hbm(week_weight, week_ids, observed, footprints))

    staged = []

    def stage_rest(after):
        staged.extend(call(
            rest_kernel, [HBM, VMEM, ANY], [footprints.shape, (8, 128)], [pltpu.SemaphoreType.DMA((blocks // 4,))],
            moved=4 * footprints.size, pinned=True, aliases={1: 0},
        )(*in_hbm(footprints), pltpu.with_memory_space_constraint(tiles, pltpu.VMEM), after))
        return staged[1]

    parts, rest = spread_bundle(flux_start, bundle, own, weights, stage_rest)
    tiles = pltpu.with_memory_space_constraint(staged[0], pltpu.VMEM)

    def shapes():
        return [(p.masks, p.rest_masks) for p in parts]

    def arrays():
        return [p.array for p in parts]

    hot_shape = (count + own, n * count)
    whole = pltpu.VMEM((n * own, cols), F32)
    work = dict(flops=4 * footprints.size, moved=4 * footprints.size)
    terms, departure = call(
        functools.partial(first_kernel, shapes()), [SMEM] * 2 + [VMEM] * (3 + len(parts)),
        [(count, cols), square], [whole], **work,
    )(*place, tiles, weights, observed_t, *arrays())

    parts = spread(terms, rest, own, own + 8)
    terms, gradient, image, hot = call(
        functools.partial(second_kernel, shapes()), [SMEM] * 2 + [VMEM] * (4 + len(parts)),
        [(count + 8, cols), (count + own, cols), square, hot_shape], [whole], **work,
    )(*place, tiles, weights, want, bundle, *arrays())

    parts = spread(terms, rest, 2 * own + 8, own)
    sums, flux, gradient, departure, image = call(
        functools.partial(third_kernel, shapes()), [SMEM] * 2 + [VMEM] * (8 + len(parts)),
        [(n, 1, 128), (own, cols), (own, cols), (blocks, tile_rows), (blocks, tile_rows)],
        [whole, pltpu.VMEM((count + own, cols), F32)], **work,
    )(*place, tiles, weights, want, bundle, hot, gradient, departure, image, *arrays())

    sums = lax.all_to_all(sums, "obs", 0, 0)
    flux, departure = call(
        last_kernel, [VMEM] * 5, [(own, cols), (blocks, tile_rows)], flops=20000, moved=200000,
    )(sums, flux, gradient, departure, image)
    return flux, departure


def solution(mesh):
    rows = P(("groups", "obs"), None)
    return jax.shard_map(
        body,
        mesh=mesh,
        in_specs=(
            P(("groups", "obs"), None, None, None), rows, rows, rows,
            P("groups"), P(("groups", "obs")), rows, rows, rows,
        ),
        out_specs=(rows, rows),
        check_vma=False,
    )
```

time: 79.8 us -> 75.2 us (0.942)
  blocking collectives: 10.7 us -> 8.98 us
  local copies, waits for them, and re-layouts: 1.33 us -> 0.01 us
  starting transfers between devices: 24.3 us -> 23.1 us
    all_to_all x1, blocking collectives: 10.7 us -> 8.98 us  [body(): sums = lax.all_to_all(sums, 'obs', 0, 0)]
    unnamed x6 -> x2, local copies, waits for them, and re-layouts: 1.33 us -> 0.01 us
    ppermute x30 -> x27, starting transfers between devices: 24.3 us -> 23.1 us  [swap(): return lax.ppermute(x, 'obs', [(i, i ^ mask) for i in range(n)])]
    pallas_call x12 -> x17, Pallas kernels: 13.3 us -> 12.5 us  [the longest x1 2.66 us: body(): call(functools.partial(second_kernel, shapes()), [SMEM] * 2 + [VMEM] * (4...]
    ppermute x30 -> x27, waiting for transfers between devices: 27.8 us -> 28.1 us  [swap(): return lax.ppermute(x, 'obs', [(i, i ^ mask) for i in range(n)])]
  transfers between devices with their start and end apart: 30 -> 27, of which waited for: 12 -> 14; matrix products, arithmetic and copies ran while one was open for 0% -> 0% of each run, Pallas kernels for 5% -> 6%
where the time goes in v3:
time: 75.2 us; the launch traced here: 74.9 us
  waiting for transfers between devices  28.1 us (37%)
  starting transfers between devices  23.1 us (31%)
  Pallas kernels  13.3 us (18%)
  blocking collectives  8.98 us (12%)
  between operations  1.47 us (2%)
    ppermute x27, waiting for transfers between devices, swap(): return lax.ppermute(x, 'obs', [(i, i ^ mask) for i in range(n)])  28.1 us
    ppermute x27, starting transfers between devices, swap(): return lax.ppermute(x, 'obs', [(i, i ^ mask) for i in range(n)])  23.1 us
    all_to_all x1, blocking collectives, body(): sums = lax.all_to_all(sums, 'obs', 0, 0)  8.98 us
    pallas_call x1, Pallas kernels, body(): call(functools.partial(second_kernel, shapes()), [SMEM] * 2 + [VMEM] * (4...  2.66 us
    pallas_call x1, Pallas kernels, body(): call(functools.partial(third_kernel, shapes()), [SMEM] * 2 + [VMEM] * (8...  2.35 us
    pallas_call x1, Pallas kernels, body(): call(prepare_kernel, [SMEM] + [HBM] * 4, [square, square, footprints.shap...  2.27 us
    pallas_call x1, Pallas kernels, stage_rest(): call(rest_kernel, [HBM, VMEM, ANY], [footprints.shape, (8, 128)], [pltpu....  2.22 us
    pallas_call x1, Pallas kernels, body(): call(functools.partial(first_kernel, shapes()), [SMEM] * 2 + [VMEM] * (3...  2.09 us
  transfers between devices with their start and end apart: 27, of which 14 were waited for; matrix products, arithmetic and copies ran while one was open for 0% of the time, Pallas kernels for 6%

profile of v3, /device:TPU:0, one launch (start us, length us, event | category | flops | bytes accessed | tf_op | source)
XLA Modules:
  0.0 74.9 jit_solution(3973046363863331958)
XLA Ops:
  1.5 4.1 %collective-permute-start = (f32[104,256]{1,0:T(8,128)S(1)}, f32[104,256]{1,0:T(8,128)S(1)}, u32[]{:S(2)}, u32[]{:S(2)}) collective-permute-start(f32[104,256]{1,0:T(8,128)S(1)} %get-tuple-element.21.refs_0_.refs_2_.bundle), channel_id=1, source_target_pairs={{0,8},{1,9},{2,10},{3,11},{4,12},{5,13},{6,14},{7,15},{8,0},{9,1},... | collective-permute-start | bytes 319496 | tf_op jit(solution)/shard_map/ppermute | solution.py:33
  5.6 1.6 %collective-permute-start.2 = (f32[104,256]{1,0:T(8,128)S(1)}, f32[104,256]{1,0:T(8,128)S(1)}, u32[]{:S(2)}, u32[]{:S(2)}) collective-permute-start(f32[104,256]{1,0:T(8,128)S(1)} %get-tuple-element.21.refs_0_.refs_2_.bundle), channel_id=1, source_target_pairs={{0,4},{1,5},{2,6},{3,7},{4,0},{5,1},{6,2},{7,3},{8,12},{9,13},{10,... | collective-permute-start | bytes 319496 | tf_op jit(solution)/shard_map/ppermute | solution.py:33
  7.8 2.3 %shard_map.104 = (f32[128,128]{1,0:T(8,128)S(1)}, f32[128,128]{1,0:T(8,128)S(1)}, f32[16,4,128,256]{3,2,1,0:T(8,128)S(1)}) custom-call(s32[1]{0:T(128)S(6)} %copy.13.counts, f32[8]{0:T(128)} %table_in.1, s32[16,128]{1,0:T(8,128)} %week_ids.1, f32[16,128]{1,0:T(8,128)} %observed.1, f32[16,4,128,256]{3,2,1,0:T(8,128)} %footprints.3), custom_call_target="tpu_custom_call" | custom-call | flops 10000 | bytes 16777216 | tf_op jit(solution)/shard_map/pallas_call | solution.py:370
  10.1 3.0 %collective-permute-done.1.refs_1_ = f32[32,256]{1,0:T(8,128)S(1)} collective-permute-done((f32[32,256]{1,0:T(8,128)}, f32[32,256]{1,0:T(8,128)S(1)}, u32[]{:S(2)}, u32[]{:S(2)}) %collective-permute-start.1) | collective-permute-done | bytes 32800 | tf_op jit(solution)/shard_map/ppermute | solution.py:33
  13.1 1.6 %collective-permute-start.4 = (f32[64,256]{1,0:T(8,128)S(1)}, f32[64,256]{1,0:T(8,128)S(1)}, u32[]{:S(2)}, u32[]{:S(2)}) collective-permute-start(f32[64,256]{1,0:T(8,128)S(1)} %shard_map.106.after.refs_2_), channel_id=1, source_target_pairs={{0,2},{1,3},{2,0},{3,1},{4,6},{5,7},{6,4},{7,5},{8,10},{9,11},{10,... | collective-permute-start | bytes 196616 | tf_op jit(solution)/shard_map/ppermute | solution.py:33
  15.8 2.2 %shard_map.107 = (f32[16,4,128,256]{3,2,1,0:T(8,128)S(1)}, f32[8,128]{1,0:T(8,128)S(1)}) custom-call(f32[16,4,128,256]{3,2,1,0:T(8,128)} %footprints.3, f32[16,4,128,256]{3,2,1,0:T(8,128)S(1)} %get-tuple-element.20.tiles_in, f32[64,256]{1,0:T(8,128)S(1)} %shard_map.106.after.refs_2_), custom_call_target="tpu_custom_call", output_to_operand_aliasing={{0}: (1, {})} | custom-call | bytes 8388608 | tf_op jit(solution)/shard_map/pallas_call | solution.py:380
  20.3 2.1 %shard_map.110 = (f32[64,256]{1,0:T(8,128)S(1)}, f32[128,128]{1,0:T(8,128)S(1)}) custom-call(s32[4,16]{1,0:T(4,128)S(1)} %bitcast.3, s32[1]{0:T(128)} %bitcast.1.me, f32[16,4,128,256]{3,2,1,0:T(8,128)S(1)} %get-tuple-element.23.tiles, f32[128,128]{1,0:T(8,128)S(1)} %get-tuple-element.22.refs_2_.weights, f32[128,128]{1,0:T(8,128)S(1)} %get-tuple-element.25.observed, ...), custom_call_target="tpu_custom_call" | custom-call | flops 8388608 | bytes 8388608 | tf_op jit(solution)/shard_map/pallas_call | solution.py:398
  22.5 2.6 %collective-permute-start.11 = (f32[64,256]{1,0:T(8,128)S(1)}, f32[64,256]{1,0:T(8,128)S(1)}, u32[]{:S(2)}, u32[]{:S(2)}) collective-permute-start(f32[64,256]{1,0:T(8,128)S(1)} %get-tuple-element.27.refs_0_.refs_2_.refs_6_), channel_id=1, source_target_pairs={{0,8},{1,9},{2,10},{3,11},{4,12},{5,13},{6,14},{7,15},{8,0},{9,1},... | collective-permute-start | bytes 196616 | tf_op jit(solution)/shard_map/ppermute | solution.py:33
  25.1 1.7 %collective-permute-start.12 = (f32[64,256]{1,0:T(8,128)S(1)}, f32[64,256]{1,0:T(8,128)S(1)}, u32[]{:S(2)}, u32[]{:S(2)}) collective-permute-start(f32[64,256]{1,0:T(8,128)S(1)} %get-tuple-element.27.refs_0_.refs_2_.refs_6_), channel_id=1, source_target_pairs={{0,12},{1,13},{2,14},{3,15},{4,8},{5,9},{6,10},{7,11},{8,4},{9,5},... | collective-permute-start | bytes 196616 | tf_op jit(solution)/shard_map/ppermute | solution.py:33
  26.8 2.1 %collective-permute-done.9.refs_1_.refs_5_ = f32[104,256]{1,0:T(8,128)S(1)} collective-permute-done((f32[104,256]{1,0:T(8,128)S(1)}, f32[104,256]{1,0:T(8,128)S(1)}, u32[]{:S(2)}, u32[]{:S(2)}) %collective-permute-start.9) | collective-permute-done | bytes 106528 | tf_op jit(solution)/shard_map/ppermute | solution.py:33
  29.9 1.7 %collective-permute-done.12.refs_1_ = f32[64,256]{1,0:T(8,128)S(1)} collective-permute-done((f32[64,256]{1,0:T(8,128)S(1)}, f32[64,256]{1,0:T(8,128)S(1)}, u32[]{:S(2)}, u32[]{:S(2)}) %collective-permute-start.12) | collective-permute-done | bytes 65568 | tf_op jit(solution)/shard_map/ppermute | solution.py:33
  33.3 5.3 %collective-permute-done.10.refs_1_ = f32[288,256]{1,0:T(8,128)S(1)} collective-permute-done((f32[288,256]{1,0:T(8,128)S(1)}, f32[288,256]{1,0:T(8,128)S(1)}, u32[]{:S(2)}, u32[]{:S(2)}) %collective-permute-start.10) | collective-permute-done | bytes 294944 | tf_op jit(solution)/shard_map/ppermute | solution.py:33
  38.6 1.4 %collective-permute-done.13.refs_0_ = f32[128,256]{1,0:T(8,128)S(1)} collective-permute-done((f32[128,256]{1,0:T(8,128)S(1)}, f32[128,256]{1,0:T(8,128)S(1)}, u32[]{:S(2)}, u32[]{:S(2)}) %collective-permute-start.13) | collective-permute-done | bytes 131104 | tf_op jit(solution)/shard_map/ppermute | solution.py:33
  40.2 1.3 %collective-permute-done.17.refs_7_ = f32[128,256]{1,0:T(8,128)S(1)} collective-permute-done((f32[128,256]{1,0:T(8,128)S(1)}, f32[128,256]{1,0:T(8,128)S(1)}, u32[]{:S(2)}, u32[]{:S(2)}) %collective-permute-start.17) | collective-permute-done | bytes 131104 | tf_op jit(solution)/shard_map/ppermute | solution.py:33
  41.5 2.7 %shard_map.115 = (f32[72,256]{1,0:T(8,128)S(1)}, f32[96,256]{1,0:T(8,128)S(1)}, f32[128,128]{1,0:T(8,128)S(1)}, f32[96,1024]{1,0:T(8,128)S(1)}) custom-call(s32[4,16]{1,0:T(4,128)S(1)} %bitcast.4, s32[1]{0:T(128)} %bitcast.1.me, f32[16,4,128,256]{3,2,1,0:T(8,128)S(1)} %get-tuple-element.23.tiles, f32[128,128]{1,0:T(8,128)S(1)} %get-tuple-element.22.refs_2_.weights, ...), custom_call_target="tpu_custom_call" | custom-call | flops 8388608 | bytes 8388608 | tf_op jit(solution)/shard_map/pallas_call | solution.py:404
  44.3 1.2 %collective-permute-start.20 = (f32[72,256]{1,0:T(8,128)S(1)}, f32[72,256]{1,0:T(8,128)S(1)}, u32[]{:S(2)}, u32[]{:S(2)}) collective-permute-start(f32[72,256]{1,0:T(8,128)S(1)} %get-tuple-element.32.refs_0_.refs_2_.refs_6_), channel_id=1, source_target_pairs={{0,8},{1,9},{2,10},{3,11},{4,12},{5,13},{6,14},{7,15},{8,0},{9,1},... | collective-permute-start | bytes 221192 | tf_op jit(solution)/shard_map/ppermute | solution.py:33
  45.5 3.1 %collective-permute-start.21 = (f32[72,256]{1,0:T(8,128)S(1)}, f32[72,256]{1,0:T(8,128)S(1)}, u32[]{:S(2)}, u32[]{:S(2)}) collective-permute-start(f32[72,256]{1,0:T(8,128)S(1)} %get-tuple-element.32.refs_0_.refs_2_.refs_6_), channel_id=1, source_target_pairs={{0,12},{1,13},{2,14},{3,15},{4,8},{5,9},{6,10},{7,11},{8,4},{9,5},... | collective-permute-start | bytes 221192 | tf_op jit(solution)/shard_map/ppermute | solution.py:33
  48.6 2.2 %collective-permute-done.18.refs_1_.refs_5_ = f32[104,256]{1,0:T(8,128)S(1)} collective-permute-done((f32[104,256]{1,0:T(8,128)S(1)}, f32[104,256]{1,0:T(8,128)S(1)}, u32[]{:S(2)}, u32[]{:S(2)}) %collective-permute-start.18) | collective-permute-done | bytes 106528 | tf_op jit(solution)/shard_map/ppermute | solution.py:33
  52.1 1.4 %collective-permute-done.20.refs_0_ = f32[72,256]{1,0:T(8,128)S(1)} collective-permute-done((f32[72,256]{1,0:T(8,128)S(1)}, f32[72,256]{1,0:T(8,128)S(1)}, u32[]{:S(2)}, u32[]{:S(2)}) %collective-permute-start.20) | collective-permute-done | bytes 73760 | tf_op jit(solution)/shard_map/ppermute | solution.py:33
  55.2 4.6 %collective-permute-done.19.refs_1_ = f32[272,256]{1,0:T(8,128)S(1)} collective-permute-done((f32[272,256]{1,0:T(8,128)S(1)}, f32[272,256]{1,0:T(8,128)S(1)}, u32[]{:S(2)}, u32[]{:S(2)}) %collective-permute-start.19) | collective-permute-done | bytes 278560 | tf_op jit(solution)/shard_map/ppermute | solution.py:33
  59.8 1.6 %collective-permute-done.22.refs_0_ = f32[144,256]{1,0:T(8,128)S(1)} collective-permute-done((f32[144,256]{1,0:T(8,128)S(1)}, f32[144,256]{1,0:T(8,128)S(1)}, u32[]{:S(2)}, u32[]{:S(2)}) %collective-permute-start.22) | collective-permute-done | bytes 147488 | tf_op jit(solution)/shard_map/ppermute | solution.py:33
  61.5 1.3 %collective-permute-done.26.refs_7_ = f32[144,256]{1,0:T(8,128)S(1)} collective-permute-done((f32[144,256]{1,0:T(8,128)S(1)}, f32[144,256]{1,0:T(8,128)S(1)}, u32[]{:S(2)}, u32[]{:S(2)}) %collective-permute-start.26) | collective-permute-done | bytes 147488 | tf_op jit(solution)/shard_map/ppermute | solution.py:33
  62.9 2.3 %shard_map.120 = (f32[16,1,128]{2,1,0:T(1,128)S(1)}, f32[32,256]{1,0:T(8,128)S(1)}, f32[32,256]{1,0:T(8,128)S(1)}, f32[16,128]{1,0:T(8,128)S(1)}, f32[16,128]{1,0:T(8,128)S(1)}) custom-call(s32[4,16]{1,0:T(4,128)S(1)} %bitcast.5, s32[1]{0:T(128)} %bitcast.1.me, f32[16,4,128,256]{3,2,1,0:T(8,128)S(1)} %get-tuple-element.23.tiles, ...), custom_call_target="tpu_custom_call" | custom-call | flops 8388608 | bytes 8388608 | tf_op jit(solution)/shard_map/pallas_call | solution.py:410
  65.2 9.0 %all_to_all.5.sums = f32[16,1,128]{2,1,0:T(1,128)S(1)} all-to-all(f32[16,1,128]{2,1,0:T(1,128)S(1)} %get-tuple-element.33), channel_id=1, replica_groups=mesh['groups'=2,'obs'=16] {'obs'}, dimensions={0} | all-to-all | bytes 16384 | tf_op jit(solution)/shard_map/all_to_all | solution.py:416
  (51 shorter events, 11.0 us)
Async XLA Ops:
  1.5 11.6 %collective-permute-start = (f32[104,256]{1,0:T(8,128)S(1)}, f32[104,256]{1,0:T(8,128)S(1)}, u32[]{:S(2)}, u32[]{:S(2)}) collective-permute-start(f32[104,256]{1,0:T(8,128)S(1)} %get-tuple-element.21.refs_0_.refs_2_.bundle), channel_id=1, source_target_pairs={{0,8},{1,9},{2,10},{3,11},{4,12},{5,13},{6,14},{7,15},{8,0},{9,1},... | collective-permute-start | bytes 319496 | tf_op jit(solution)/shard_map/ppermute | solution.py:33
  5.6 9.1 %collective-permute-start.2 = (f32[104,256]{1,0:T(8,128)S(1)}, f32[104,256]{1,0:T(8,128)S(1)}, u32[]{:S(2)}, u32[]{:S(2)}) collective-permute-start(f32[104,256]{1,0:T(8,128)S(1)} %get-tuple-element.21.refs_0_.refs_2_.bundle), channel_id=1, source_target_pairs={{0,4},{1,5},{2,6},{3,7},{4,0},{5,1},{6,2},{7,3},{8,12},{9,13},{10,... | collective-permute-start | bytes 319496 | tf_op jit(solution)/shard_map/ppermute | solution.py:33
  7.2 5.9 %collective-permute-start.1 = (f32[32,256]{1,0:T(8,128)}, f32[32,256]{1,0:T(8,128)S(1)}, u32[]{:S(2)}, u32[]{:S(2)}) collective-permute-start(f32[32,256]{1,0:T(8,128)} %flux.1), channel_id=1, source_target_pairs={{0,12},{1,13},{2,14},{3,15},{4,8},{5,9},{6,10},{7,11},{8,4},{9,5},... | collective-permute-start | bytes 98312 | tf_op jit(solution)/shard_map/ppermute | solution.py:33
  13.1 4.9 %collective-permute-start.4 = (f32[64,256]{1,0:T(8,128)S(1)}, f32[64,256]{1,0:T(8,128)S(1)}, u32[]{:S(2)}, u32[]{:S(2)}) collective-permute-start(f32[64,256]{1,0:T(8,128)S(1)} %shard_map.106.after.refs_2_), channel_id=1, source_target_pairs={{0,2},{1,3},{2,0},{3,1},{4,6},{5,7},{6,4},{7,5},{8,10},{9,11},{10,... | collective-permute-start | bytes 196616 | tf_op jit(solution)/shard_map/ppermute | solution.py:33
  14.7 4.3 %collective-permute-start.3 = (f32[64,256]{1,0:T(8,128)S(1)}, f32[64,256]{1,0:T(8,128)S(1)}, u32[]{:S(2)}, u32[]{:S(2)}) collective-permute-start(f32[64,256]{1,0:T(8,128)S(1)} %shard_map.108.refs_0_), channel_id=1, source_target_pairs={{0,2},{1,3},{2,0},{3,1},{4,6},{5,7},{6,4},{7,5},{8,10},{9,11},{10,... | collective-permute-start | bytes 196616 | tf_op jit(solution)/shard_map/ppermute | solution.py:33
  15.3 3.8 %collective-permute-start.5 = (f32[64,256]{1,0:T(8,128)S(1)}, f32[64,256]{1,0:T(8,128)S(1)}, u32[]{:S(2)}, u32[]{:S(2)}) collective-permute-start(f32[64,256]{1,0:T(8,128)S(1)} %shard_map.108.refs_0_), channel_id=1, source_target_pairs={{0,1},{1,0},{2,3},{3,2},{4,5},{5,4},{6,7},{7,6},{8,9},{9,8},{10,11... | collective-permute-start | bytes 196616 | tf_op jit(solution)/shard_map/ppermute | solution.py:33
  15.3 3.8 %collective-permute-start.7 = (f32[64,256]{1,0:T(8,128)S(1)}, f32[64,256]{1,0:T(8,128)S(1)}, u32[]{:S(2)}, u32[]{:S(2)}) collective-permute-start(f32[64,256]{1,0:T(8,128)S(1)} %shard_map.106.after.refs_2_), channel_id=1, source_target_pairs={{0,1},{1,0},{2,3},{3,2},{4,5},{5,4},{6,7},{7,6},{8,9},{9,8},{10,11... | collective-permute-start | bytes 196616 | tf_op jit(solution)/shard_map/ppermute | solution.py:33
  22.4 6.5 %collective-permute-start.9 = (f32[104,256]{1,0:T(8,128)S(1)}, f32[104,256]{1,0:T(8,128)S(1)}, u32[]{:S(2)}, u32[]{:S(2)}) collective-permute-start(f32[104,256]{1,0:T(8,128)S(1)} %shard_map.111), channel_id=1, source_target_pairs={{0,4},{1,5},{2,6},{3,7},{4,0},{5,1},{6,2},{7,3},{8,12},{9,13},{10,... | collective-permute-start | bytes 319496 | tf_op jit(solution)/shard_map/ppermute | solution.py:33
  22.5 7.5 %collective-permute-start.11 = (f32[64,256]{1,0:T(8,128)S(1)}, f32[64,256]{1,0:T(8,128)S(1)}, u32[]{:S(2)}, u32[]{:S(2)}) collective-permute-start(f32[64,256]{1,0:T(8,128)S(1)} %get-tuple-element.27.refs_0_.refs_2_.refs_6_), channel_id=1, source_target_pairs={{0,8},{1,9},{2,10},{3,11},{4,12},{5,13},{6,14},{7,15},{8,0},{9,1},... | collective-permute-start | bytes 196616 | tf_op jit(solution)/shard_map/ppermute | solution.py:33
  25.1 6.5 %collective-permute-start.12 = (f32[64,256]{1,0:T(8,128)S(1)}, f32[64,256]{1,0:T(8,128)S(1)}, u32[]{:S(2)}, u32[]{:S(2)}) collective-permute-start(f32[64,256]{1,0:T(8,128)S(1)} %get-tuple-element.27.refs_0_.refs_2_.refs_6_), channel_id=1, source_target_pairs={{0,12},{1,13},{2,14},{3,15},{4,8},{5,9},{6,10},{7,11},{8,4},{9,5},... | collective-permute-start | bytes 196616 | tf_op jit(solution)/shard_map/ppermute | solution.py:33
  28.9 9.7 %collective-permute-start.10 = (f32[288,256]{1,0:T(8,128)S(1)}, f32[288,256]{1,0:T(8,128)S(1)}, u32[]{:S(2)}, u32[]{:S(2)}) collective-permute-start(f32[288,256]{1,0:T(8,128)S(1)} %shard_map.112.refs_1_.refs_0_), channel_id=1, source_target_pairs={{0,2},{1,3},{2,0},{3,1},{4,6},{5,7},{6,4},{7,5},{8,10},{9,11},{10,... | collective-permute-start | bytes 884744 | tf_op jit(solution)/shard_map/ppermute | solution.py:33
  31.7 8.4 %collective-permute-start.13 = (f32[128,256]{1,0:T(8,128)S(1)}, f32[128,256]{1,0:T(8,128)S(1)}, u32[]{:S(2)}, u32[]{:S(2)}) collective-permute-start(f32[128,256]{1,0:T(8,128)S(1)} %shard_map.113.refs_2_), channel_id=1, source_target_pairs={{0,2},{1,3},{2,0},{3,1},{4,6},{5,7},{6,4},{7,5},{8,10},{9,11},{10,... | collective-permute-start | bytes 393224 | tf_op jit(solution)/shard_map/ppermute | solution.py:33
  32.8 7.4 %collective-permute-start.16 = (f32[128,256]{1,0:T(8,128)S(1)}, f32[128,256]{1,0:T(8,128)S(1)}, u32[]{:S(2)}, u32[]{:S(2)}) collective-permute-start(f32[128,256]{1,0:T(8,128)S(1)} %shard_map.113.refs_2_), channel_id=1, source_target_pairs={{0,1},{1,0},{2,3},{3,2},{4,5},{5,4},{6,7},{7,6},{8,9},{9,8},{10,11... | collective-permute-start | bytes 393224 | tf_op jit(solution)/shard_map/ppermute | solution.py:33
  32.8 8.7 %collective-permute-start.14 = (f32[288,256]{1,0:T(8,128)S(1)}, f32[288,256]{1,0:T(8,128)S(1)}, u32[]{:S(2)}, u32[]{:S(2)}) collective-permute-start(f32[288,256]{1,0:T(8,128)S(1)} %shard_map.112.refs_1_.refs_0_), channel_id=1, source_target_pairs={{0,1},{1,0},{2,3},{3,2},{4,5},{5,4},{6,7},{7,6},{8,9},{9,8},{10,11... | collective-permute-start | bytes 884744 | tf_op jit(solution)/shard_map/ppermute | solution.py:33
  38.6 2.8 %collective-permute-start.15 = (f32[288,256]{1,0:T(8,128)S(1)}, f32[288,256]{1,0:T(8,128)S(1)}, u32[]{:S(2)}, u32[]{:S(2)}) collective-permute-start(f32[288,256]{1,0:T(8,128)S(1)} %collective-permute-done.10.refs_1_), channel_id=1, source_target_pairs={{0,1},{1,0},{2,3},{3,2},{4,5},{5,4},{6,7},{7,6},{8,9},{9,8},{10,11... | collective-permute-start | bytes 884744 | tf_op jit(solution)/shard_map/ppermute | solution.py:33
  44.2 6.6 %collective-permute-start.18 = (f32[104,256]{1,0:T(8,128)S(1)}, f32[104,256]{1,0:T(8,128)S(1)}, u32[]{:S(2)}, u32[]{:S(2)}) collective-permute-start(f32[104,256]{1,0:T(8,128)S(1)} %shard_map.116), channel_id=1, source_target_pairs={{0,4},{1,5},{2,6},{3,7},{4,0},{5,1},{6,2},{7,3},{8,12},{9,13},{10,... | collective-permute-start | bytes 319496 | tf_op jit(solution)/shard_map/ppermute | solution.py:33
  44.3 9.2 %collective-permute-start.20 = (f32[72,256]{1,0:T(8,128)S(1)}, f32[72,256]{1,0:T(8,128)S(1)}, u32[]{:S(2)}, u32[]{:S(2)}) collective-permute-start(f32[72,256]{1,0:T(8,128)S(1)} %get-tuple-element.32.refs_0_.refs_2_.refs_6_), channel_id=1, source_target_pairs={{0,8},{1,9},{2,10},{3,11},{4,12},{5,13},{6,14},{7,15},{8,0},{9,1},... | collective-permute-start | bytes 221192 | tf_op jit(solution)/shard_map/ppermute | solution.py:33
  45.5 8.0 %collective-permute-start.21 = (f32[72,256]{1,0:T(8,128)S(1)}, f32[72,256]{1,0:T(8,128)S(1)}, u32[]{:S(2)}, u32[]{:S(2)}) collective-permute-start(f32[72,256]{1,0:T(8,128)S(1)} %get-tuple-element.32.refs_0_.refs_2_.refs_6_), channel_id=1, source_target_pairs={{0,12},{1,13},{2,14},{3,15},{4,8},{5,9},{6,10},{7,11},{8,4},{9,5},... | collective-permute-start | bytes 221192 | tf_op jit(solution)/shard_map/ppermute | solution.py:33
  50.8 9.0 %collective-permute-start.19 = (f32[272,256]{1,0:T(8,128)S(1)}, f32[272,256]{1,0:T(8,128)S(1)}, u32[]{:S(2)}, u32[]{:S(2)}) collective-permute-start(f32[272,256]{1,0:T(8,128)S(1)} %shard_map.117.refs_1_.refs_0_), channel_id=1, source_target_pairs={{0,2},{1,3},{2,0},{3,1},{4,6},{5,7},{6,4},{7,5},{8,10},{9,11},{10,... | collective-permute-start | bytes 835592 | tf_op jit(solution)/shard_map/ppermute | solution.py:33
  53.5 7.9 %collective-permute-start.22 = (f32[144,256]{1,0:T(8,128)S(1)}, f32[144,256]{1,0:T(8,128)S(1)}, u32[]{:S(2)}, u32[]{:S(2)}) collective-permute-start(f32[144,256]{1,0:T(8,128)S(1)} %shard_map.118.refs_2_), channel_id=1, source_target_pairs={{0,2},{1,3},{2,0},{3,1},{4,6},{5,7},{6,4},{7,5},{8,10},{9,11},{10,... | collective-permute-start | bytes 442376 | tf_op jit(solution)/shard_map/ppermute | solution.py:33
  54.7 6.8 %collective-permute-start.25 = (f32[144,256]{1,0:T(8,128)S(1)}, f32[144,256]{1,0:T(8,128)S(1)}, u32[]{:S(2)}, u32[]{:S(2)}) collective-permute-start(f32[144,256]{1,0:T(8,128)S(1)} %shard_map.118.refs_2_), channel_id=1, source_target_pairs={{0,1},{1,0},{2,3},{3,2},{4,5},{5,4},{6,7},{7,6},{8,9},{9,8},{10,11... | collective-permute-start | bytes 442376 | tf_op jit(solution)/shard_map/ppermute | solution.py:33
  54.7 8.1 %collective-permute-start.23 = (f32[272,256]{1,0:T(8,128)S(1)}, f32[272,256]{1,0:T(8,128)S(1)}, u32[]{:S(2)}, u32[]{:S(2)}) collective-permute-start(f32[272,256]{1,0:T(8,128)S(1)} %shard_map.117.refs_1_.refs_0_), channel_id=1, source_target_pairs={{0,1},{1,0},{2,3},{3,2},{4,5},{5,4},{6,7},{7,6},{8,9},{9,8},{10,11... | collective-permute-start | bytes 835592 | tf_op jit(solution)/shard_map/ppermute | solution.py:33
  59.8 3.0 %collective-permute-start.24 = (f32[272,256]{1,0:T(8,128)S(1)}, f32[272,256]{1,0:T(8,128)S(1)}, u32[]{:S(2)}, u32[]{:S(2)}) collective-permute-start(f32[272,256]{1,0:T(8,128)S(1)} %collective-permute-done.19.refs_1_), channel_id=1, source_target_pairs={{0,1},{1,0},{2,3},{3,2},{4,5},{5,4},{6,7},{7,6},{8,9},{9,8},{10,11... | collective-permute-start | bytes 835592 | tf_op jit(solution)/shard_map/ppermute | solution.py:33
  61.4 1.4 %collective-permute-start.26 = (f32[144,256]{1,0:T(8,128)S(1)}, f32[144,256]{1,0:T(8,128)S(1)}, u32[]{:S(2)}, u32[]{:S(2)}) collective-permute-start(f32[144,256]{1,0:T(8,128)S(1)} %shard_map.119.refs_3_), channel_id=1, source_target_pairs={{0,1},{1,0},{2,3},{3,2},{4,5},{5,4},{6,7},{7,6},{8,9},{9,8},{10,11... | collective-permute-start | bytes 442376 | tf_op jit(solution)/shard_map/ppermute | solution.py:33
  (4 other events, 8.5 us)

commit v4 on v3

--- a/solution.py
+++ b/solution.py
@@ -37,10 +37,9 @@
     return [m ^ mask for m in masks]
 
 
-def call(kernel, ins, outs, scratch=(), flops=0, moved=0, pinned=False, aliases=()):
+def call(kernel, ins, outs, scratch=(), flops=0, moved=0, pinned=False):
     return pl.pallas_call(
         kernel,
-        input_output_aliases=dict(aliases),
         out_shape=[pltpu.VMEM(s, F32) if pinned and len(s) == 4 else jax.ShapeDtypeStruct(s, F32) for s in outs],
         in_specs=ins,
         out_specs=[VMEM] * len(outs),
@@ -84,14 +83,13 @@
         return Part(swap(self.array, mask), shift(self.masks, mask), shift(self.rest_masks, mask))
 
 
-def near_stages(first, second, wait=None):
+def near_stages(first, second, wide=None, cost=0):
     (pair,), (core,) = stage_masks(lax.axis_size("obs"))[-2:]
-    parts = [first, first.swap(pair)]
-    later = second(None)
-    other = later.swap(pair)
-    after, cost = (first.array, LONG) if wait is None else (wait(later.array), 0)
+    other = second.swap(pair)
     whole = (other.array.shape[0], 0, other.array.shape[0])
-    parts = parts + [later, Part(pile([other.array], [whole], after, cost), other.masks)]
+    if cost:
+        other = Part(pile([other.array], [whole], first.array, cost), other.masks)
+    parts = [wide or first, first.swap(pair), second, other]
     return parts + [p.swap(core) for p in parts]
 
 
@@ -99,31 +97,37 @@
     size = x.shape[0]
     cut = (size, 0, size)
     x, masks = lead_stages(x)
-    arrays, held, pitch = rest
+    bundle_far, mine, paired, held, pitch, own = rest
     near, far, both = stage_masks(lax.axis_size("obs"))[-3]
-    few = (pitch, at, rows)
+    (pair,) = stage_masks(lax.axis_size("obs"))[-2]
     beyond, across = swap(x, far), swap(x, both)
-    beside = swap(pile([x, arrays[2]], [cut, few], x), near)
-    count = len(masks) * size
-    first = pile(
-        [x, beside, *arrays, beside],
-        [(count, 0, count), (beside.shape[0], 0, count)] + [few] * 3 + [(beside.shape[0], count, beside.shape[0] - count)], x)
-    first = Part(first, masks + shift(masks, near), held + shift(held, near) + shift(held, far) + shift(held, both))
-    return near_stages(
-        first, lambda _: Part(pile([beyond, across], [cut] * 2, x, LONG), shift(masks, far) + shift(masks, both)))
-
-
-def spread_bundle(flux, bundle, own, ready, wait):
+    beside = swap(pile([x, bundle_far], [cut, (pitch, own + at, rows)], x), near)
+    count, extra = len(masks) * size, len(held) * rows
+    first = Part(
+        pile([x, beside, beside], [(count, 0, count), (count + extra, 0, count), (count + extra, count, extra)], x),
+        masks + shift(masks, near), shift(held, both))
+    second = Part(pile([beyond, across], [cut] * 2, x, LONG), shift(masks, far) + shift(masks, both))
+    few = (pitch - own, at, rows)
+    more = held + shift(held, near) + shift(held, far)
+    wide = Part(
+        pile([first.array, mine, paired], [(2 * count + extra, 0, 2 * count + extra), few, few], x),
+        first.masks, list(first.rest_masks) + more + shift(more, pair))
+    return near_stages(first, second, wide, LONG)
+
+
+def spread_bundle(flux, bundle, own, ready):
     pitch = bundle.shape[0]
     x, masks = lead_stages(bundle)
     near, far, both = stage_masks(lax.axis_size("obs"))[-3]
+    (pair,) = stage_masks(lax.axis_size("obs"))[-2]
     cut = (pitch, 0, own)
     lone = flux if len(masks) == 1 else pile([x], [cut], x)
     across, beyond, beside = swap(lone, both), swap(x, far), swap(x, near)
     first = Part(pile([x, beside], [cut] * 2, ready), masks + shift(masks, near))
-    parts = near_stages(first, lambda after: Part(
-        pile([beyond, across], [cut, (own, 0, own)], ready), shift(masks, far) + shift(masks, both)), wait)
-    return parts, ((x, beside, beyond), masks, pitch)
+    second = Part(pile([beyond, across], [cut, (own, 0, own)], ready), shift(masks, far) + shift(masks, both))
+    parts = near_stages(first, second)
+    mine = pile([x, beside, beyond], [(pitch, own, pitch - own)] * 3, second.array)
+    return parts, (beyond, mine, swap(mine, pair), masks, pitch, own)
 
 
 def bundle_kernel(ids, me, flux, prior, precision, bundle_out, want_out, prior_in, tile_ids, sem):
@@ -159,12 +163,12 @@
                    week_weight, ids_in, y_in, sem):
     small = [
         pltpu.make_async_copy(week_ids, ids_in, sem.at[0]),
-        pltpu.make_async_copy(table_in, week_weight, sem.at[2 + week_ids.shape[0] // 4]),
+        pltpu.make_async_copy(table_in, week_weight, sem.at[2 + week_ids.shape[0] // 2]),
         pltpu.make_async_copy(observed, y_in, sem.at[1]),
     ]
     large = [
         pltpu.make_async_copy(footprints.at[pl.ds(i, 2)], tiles_out.at[pl.ds(i, 2)], sem.at[2 + i // 2])
-        for i in range(0, footprints.shape[0] // 2, 2)
+        for i in range(0, footprints.shape[0], 2)
     ]
     for c in small:
         c.start()
@@ -186,20 +190,6 @@
         c.wait()
 
 
-def rest_kernel(footprints, tiles_in, after, tiles_out, done_out, sem):
-    del tiles_in, after
-    done_out[...] = jnp.zeros_like(done_out)
-    half = footprints.shape[0] // 2
-    copies = [
-        pltpu.make_async_copy(footprints.at[pl.ds(i, 2)], tiles_out.at[pl.ds(i, 2)], sem.at[(i - half) // 2])
-        for i in range(half, 2 * half, 2)
-    ]
-    for c in copies:
-        c.start()
-    for c in copies:
-        c.wait()
-
-
 def by_owner(me, pieces, rows, into):
     for m, ref, at in pieces:
         into[pl.ds(pl.multiple_of((me ^ m) * rows, 8), rows), :] = ref[at:at + rows, :]
@@ -239,14 +229,14 @@
     own = parts[0].shape[0] // len(shapes[0][0])
     by_owner(me[0], layout(shapes, parts, own, 0)[0], own, flux)
     lane = lax.broadcasted_iota(jnp.int32, (tile_rows, tile_rows), 1)
-    departure_out[...] = jnp.zeros_like(departure_out)
-
-    @pl.loop(0, blocks, unroll=4)
-    def _(b):
+
+    def block(b, columns):
         values = [flux[pl.ds(tile_ids[k, b], 1), :] for k in range(each)]
         depart = forward_block(tiles, values, lane, b, observed[...])
-        departure_out[...] = jnp.where(lane == b, depart, departure_out[...])
         transpose_block(tiles, weights, depart, lane, b, terms_out)
+        return jnp.where(lane == b, depart, columns)
+
+    departure_out[...] = lax.fori_loop(0, blocks, block, jnp.zeros((tile_rows, tile_rows), F32), unroll=16)
 
 
 def one_hot(order, names, want, piece, hot):
@@ -258,9 +248,9 @@
         hot[:, j * piece:(j + 2) * piece] = jnp.where(wanted == pair, 1.0, 0.0)
 
 
-def sum_terms(pieces, piece, hot):
+def sum_terms(pieces, piece, hot, start):
     block = jnp.concatenate([ref[at:at + piece, :] for _, ref, at in pieces], axis=0)
-    marks = hot[...].astype(jnp.bfloat16)
+    marks = hot[:, start:start + len(pieces) * piece].astype(jnp.bfloat16)
     total = None
     for _ in range(3):
         part = block.astype(jnp.bfloat16)
@@ -277,23 +267,33 @@
     return jnp.where(lane == 0, square, jnp.where(lane == 1, below, 0.0))
 
 
-def second_kernel(shapes, tile_ids, me, tiles, weights, want, bundle, *refs):
+def early_kernel(shapes, pitch, rest, count, make_hot, me, want, *refs):
+    parts, others = refs[:len(shapes)], refs[len(shapes):]
+    pieces, more = layout(shapes, parts, pitch, rest)
+    if make_hot:
+        total_out, rows_out, hot = others
+        marks = [(m, ref, at + rest - 8) for m, ref, at in more]
+        late = [m for m, _, _ in more if m not in {p for p, _, _ in pieces}]
+        one_hot([m for m, _, _ in pieces] + late, marks, want, count, hot)
+    else:
+        hot, total_out, rows_out = others
+    by_owner(me[0], more, rows_out.shape[0] // len(more), rows_out)
+    total_out[...] = sum_terms(pieces, count, hot, 0)
+
+
+def second_kernel(shapes, tile_ids, me, tiles, weights, want, bundle, total, more, hot, *refs):
     parts = refs[:len(shapes)]
-    terms_out, gradient_out, image_out, hot, more = refs[len(shapes):]
+    terms_out, gradient_out, image_out = refs[len(shapes):]
     blocks, each, tile_rows, _ = tiles.shape
     count = blocks * each
     own = want.shape[0] - count
-    pieces, others = layout(shapes, parts, count, own + 8)
-    by_owner(me[0], others, own, more)
-    one_hot([m for m, _, _ in pieces], [(m, ref, at + own) for m, ref, at in others], want, count, hot)
+    pieces, _ = layout(shapes, parts, count, 0)
     lane = lax.broadcasted_iota(jnp.int32, (tile_rows, tile_rows), 1)
-    image_out[...] = jnp.zeros_like(image_out)
-    gradient_out[...] = sum_terms(pieces, count, hot)
+    gradient_out[...] = total[...] + sum_terms(pieces, count, hot, hot.shape[1] - len(pieces) * count)
     mine = gradient_out[count:, :] + bundle[own:2 * own, :]
     gradient_out[count:, :] = mine
 
-    @pl.loop(0, blocks, unroll=4)
-    def _(b):
+    def block(b, columns):
         values = []
         for k in range(each):
             t = pl.ds(b * each + k, 1)
@@ -301,27 +301,30 @@
             gradient_out[t, :] = value
             values.append(value)
         image = forward_block(tiles, values, lane, b, None)
-        image_out[...] = jnp.where(lane == b, image, image_out[...])
         transpose_block(tiles, weights, image, lane, b, terms_out)
-
+        return jnp.where(lane == b, image, columns)
+
+    columns = lax.fori_loop(0, blocks, block, jnp.zeros((tile_rows, tile_rows), F32), unroll=16)
+    image_out[...] = columns
     terms_out[count:, :] = sums_row(
-        mine, bundle[2 * own + 8:3 * own + 8, :], weights[...], image_out[...], (8, terms_out.shape[1]))
-
-
-def third_kernel(shapes, tile_ids, me, tiles, weights, want, bundle, hot, gradient, departure, image, *refs):
-    parts = refs[:len(shapes)]
-    sums_out, flux_out, gradient_out, departure_out, image_out, scale, second = refs[len(shapes):]
+        mine, bundle[2 * own + 8:3 * own + 8, :], weights[...], columns, (8, terms_out.shape[1]))
+
+
+def third_kernel(shapes, late_shapes, tile_ids, me, tiles, weights, want, bundle, total, scale, hot, gradient, departure,
+                 image, *refs):
+    parts, late = refs[:len(shapes)], refs[len(shapes):len(shapes) + len(late_shapes)]
+    sums_out, flux_out, gradient_out, departure_out, image_out, second = refs[len(shapes) + len(late_shapes):]
     blocks, each, tile_rows, _ = tiles.shape
     count = blocks * each
     own = want.shape[0] - count
-    pieces, others = layout(shapes, parts, count + 8, own)
-    by_owner(me[0], others, own, scale)
     lane = lax.broadcasted_iota(jnp.int32, (tile_rows, tile_rows), 1)
+    late, _ = layout(late_shapes, late, count + 8, own)
+    pieces = layout(shapes, parts, count + 8, own)[0] + late
     sums = jnp.zeros((1, 128), F32)
     for _, ref, at in pieces:
         sums = sums + ref[at + count:at + count + 1, :128]
     step = sums[:, 0:1] / sums[:, 1:2]
-    second[...] = sum_terms(pieces, count, hot)
+    second[...] = total[...] + sum_terms(late, count, hot, hot.shape[1] - len(late) * count)
     old = gradient[count:, :]
     precision = bundle[2 * own + 8:, :]
     mine = old - step * (second[count:, :] + precision * old)
@@ -336,7 +339,7 @@
             values.append(second[t, :] - step * scale[pl.ds(tile_ids[k, b], 1), :] * gradient[t, :])
         return jnp.where(lane == b, forward_block(tiles, values, lane, b, None), columns)
 
-    columns = lax.fori_loop(0, blocks, block, jnp.zeros((tile_rows, tile_rows), F32), unroll=4)
+    columns = lax.fori_loop(0, blocks, block, jnp.zeros((tile_rows, tile_rows), F32), unroll=16)
     row = sums_row(mine, precision, weights[...], columns, (1, 128))
     sums_out[...] = jnp.broadcast_to(row[None], sums_out.shape)
     departure_out[...] = (departure[...] - step * image[...]).T[:blocks]
@@ -370,48 +373,53 @@
     weights, observed_t, tiles = call(
         prepare_kernel, [SMEM] + [HBM] * 4, [square, square, footprints.shape],
         [pltpu.SMEM(week_weight.shape, F32), pltpu.VMEM(week_ids.shape, jnp.int32), pltpu.VMEM(observed.shape, F32),
-         pltpu.SemaphoreType.DMA((3 + blocks // 4,))],
+         pltpu.SemaphoreType.DMA((3 + blocks // 2,))],
         flops=10000, moved=8 * footprints.size, pinned=True,
     )(counts, *in_hbm(week_weight, week_ids, observed, footprints))
 
-    staged = []
-
-    def stage_rest(after):
-        staged.extend(call(
-            rest_kernel, [HBM, VMEM, ANY], [footprints.shape, (8, 128)], [pltpu.SemaphoreType.DMA((blocks // 4,))],
-            moved=4 * footprints.size, pinned=True, aliases={1: 0},
-        )(*in_hbm(footprints), pltpu.with_memory_space_constraint(tiles, pltpu.VMEM), after))
-        return staged[1]
-
-    parts, rest = spread_bundle(flux_start, bundle, own, weights, stage_rest)
-    tiles = pltpu.with_memory_space_constraint(staged[0], pltpu.VMEM)
-
-    def shapes():
+    parts, rest = spread_bundle(flux_start, bundle, own, weights)
+    tiles = pltpu.with_memory_space_constraint(tiles, pltpu.VMEM)
+
+    def shapes(parts):
         return [(p.masks, p.rest_masks) for p in parts]
 
-    def arrays():
+    def arrays(parts):
         return [p.array for p in parts]
 
+    def split(parts):
+        return [p for i, p in enumerate(parts) if i % 4 != 3], parts[3::4]
+
     hot_shape = (count + own, n * count)
-    whole = pltpu.VMEM((n * own, cols), F32)
+    whole = (n * own, cols)
     work = dict(flops=4 * footprints.size, moved=4 * footprints.size)
     terms, departure = call(
-        functools.partial(first_kernel, shapes()), [SMEM] * 2 + [VMEM] * (3 + len(parts)),
-        [(count, cols), square], [whole], **work,
-    )(*place, tiles, weights, observed_t, *arrays())
-
-    parts = spread(terms, rest, own, own + 8)
-    terms, gradient, image, hot = call(
-        functools.partial(second_kernel, shapes()), [SMEM] * 2 + [VMEM] * (4 + len(parts)),
-        [(count + 8, cols), (count + own, cols), square, hot_shape], [whole], **work,
-    )(*place, tiles, weights, want, bundle, *arrays())
-
-    parts = spread(terms, rest, 2 * own + 8, own)
+        functools.partial(first_kernel, shapes(parts)), [SMEM] * 2 + [VMEM] * (3 + len(parts)),
+        [(count, cols), square], [pltpu.VMEM(whole, F32)], **work,
+    )(*place, tiles, weights, observed_t, *arrays(parts))
+
+    parts = spread(terms, rest, 0, own + 8)
+    early, late = split(parts)
+    total, more, hot = call(
+        functools.partial(early_kernel, shapes(early), count, own + 8, count, True), [SMEM] + [VMEM] * (1 + len(early)),
+        [(count + own, cols), whole, hot_shape], moved=4 * n * count * cols,
+    )(place[1], want, *arrays(early))
+    terms, gradient, image = call(
+        functools.partial(second_kernel, shapes(late)), [SMEM] * 2 + [VMEM] * (7 + len(late)),
+        [(count + 8, cols), (count + own, cols), square], **work,
+    )(*place, tiles, weights, want, bundle, total, more, hot, *arrays(late))
+
+    parts = spread(terms, rest, own + 8, own)
+    early, late = split(parts)
+    total, scale = call(
+        functools.partial(early_kernel, shapes(early), count + 8, own, count, False),
+        [SMEM] + [VMEM] * (2 + len(early)), [(count + own, cols), whole], moved=4 * n * count * cols,
+    )(place[1], want, *arrays(early), hot)
     sums, flux, gradient, departure, image = call(
-        functools.partial(third_kernel, shapes()), [SMEM] * 2 + [VMEM] * (8 + len(parts)),
+        functools.partial(third_kernel, shapes(early), shapes(late)),
+        [SMEM] * 2 + [VMEM] * (10 + len(early) + len(late)),
         [(n, 1, 128), (own, cols), (own, cols), (blocks, tile_rows), (blocks, tile_rows)],
-        [whole, pltpu.VMEM((count + own, cols), F32)], **work,
-    )(*place, tiles, weights, want, bundle, hot, gradient, departure, image, *arrays())
+        [pltpu.VMEM((count + own, cols), F32)], **work,
+    )(*place, tiles, weights, want, bundle, total, scale, hot, gradient, departure, image, *arrays(early), *arrays(late))
 
     sums = lax.all_to_all(sums, "obs", 0, 0)
     flux, departure = call(

time: 75.2 us -> 72.9 us (0.969)
  waiting for transfers between devices: 28.1 us -> 22.6 us
  starting transfers between devices: 23.1 us -> 25.6 us
  blocking collectives: 8.98 us -> 10.7 us
  Pallas kernels: 13.3 us -> 12.3 us
    ppermute x27 -> x28, waiting for transfers between devices: 28.1 us -> 22.6 us  [swap(): return lax.ppermute(x, 'obs', [(i, i ^ mask) for i in range(n)])]
    ppermute x27 -> x28, starting transfers between devices: 23.1 us -> 25.6 us  [swap(): return lax.ppermute(x, 'obs', [(i, i ^ mask) for i in range(n)])]
    pallas_call x4 -> x5, Pallas kernels: 9.32 us -> 6.88 us  [the longest x1 2.38 us: body(): call(functools.partial(second_kernel, shapes(late)), [SMEM] * 2 + [VMEM]...]
    all_to_all x1, blocking collectives: 8.98 us -> 10.7 us  [body(): sums = lax.all_to_all(sums, 'obs', 0, 0)]
    pallas_call x1, Pallas kernels: 2.27 us -> 3.53 us  [body(): call(prepare_kernel, [SMEM] + [HBM] * 4, [square, square, footprints.shap...]
  transfers between devices with their start and end apart: 27 -> 28, of which waited for: 14 -> 15; matrix products, arithmetic and copies ran while one was open for 0% -> 0% of each run, Pallas kernels for 6% -> 6%
where the time goes in v4:
time: 72.9 us; the launch traced here: 72.7 us
  starting transfers between devices  25.6 us (35%)
  waiting for transfers between devices  22.6 us (31%)
  Pallas kernels  12.3 us (17%)
  blocking collectives  10.7 us (15%)
  between operations  1.51 us (2%)
    ppermute x28, starting transfers between devices, swap(): return lax.ppermute(x, 'obs', [(i, i ^ mask) for i in range(n)])  25.6 us
    ppermute x28, waiting for transfers between devices, swap(): return lax.ppermute(x, 'obs', [(i, i ^ mask) for i in range(n)])  22.6 us
    all_to_all x1, blocking collectives, body(): sums = lax.all_to_all(sums, 'obs', 0, 0)  10.7 us
    pallas_call x1, Pallas kernels, body(): call(prepare_kernel, [SMEM] + [HBM] * 4, [square, square, footprints.shap...  3.53 us
    pallas_call x1, Pallas kernels, body(): call(functools.partial(second_kernel, shapes(late)), [SMEM] * 2 + [VMEM]...  2.38 us
    pallas_call x1, Pallas kernels, body(): call(functools.partial(first_kernel, shapes(parts)), [SMEM] * 2 + [VMEM]...  2.04 us
    pallas_call x1, Pallas kernels, body(): call(functools.partial(third_kernel, shapes(early), shapes(late)), [SMEM]...  1.65 us
  transfers between devices with their start and end apart: 28, of which 15 were waited for; matrix products, arithmetic and copies ran while one was open for 0% of the time, Pallas kernels for 6%

profile of v4, /device:TPU:0, one launch (start us, length us, event | category | flops | bytes accessed | tf_op | source)
XLA Modules:
  0.0 72.7 jit_solution(453198561022155991)
XLA Ops:
  1.6 3.1 %collective-permute-start = (f32[104,256]{1,0:T(8,128)S(1)}, f32[104,256]{1,0:T(8,128)S(1)}, u32[]{:S(2)}, u32[]{:S(2)}) collective-permute-start(f32[104,256]{1,0:T(8,128)S(1)} %get-tuple-element.25.refs_0_.bundle), channel_id=1, source_target_pairs={{0,4},{1,5},{2,6},{3,7},{4,0},{5,1},{6,2},{7,3},{8,12},{9,13},{10,... | collective-permute-start | bytes 319496 | tf_op jit(solution)/shard_map/ppermute | solution.py:33
  4.7 2.6 %collective-permute-start.2 = (f32[104,256]{1,0:T(8,128)S(1)}, f32[104,256]{1,0:T(8,128)S(1)}, u32[]{:S(2)}, u32[]{:S(2)}) collective-permute-start(f32[104,256]{1,0:T(8,128)S(1)} %get-tuple-element.25.refs_0_.bundle), channel_id=1, source_target_pairs={{0,8},{1,9},{2,10},{3,11},{4,12},{5,13},{6,14},{7,15},{8,0},{9,1},... | collective-permute-start | bytes 319496 | tf_op jit(solution)/shard_map/ppermute | solution.py:33
  7.9 3.5 %shard_map.104 = (f32[128,128]{1,0:T(8,128)S(1)}, f32[128,128]{1,0:T(8,128)S(1)}, f32[16,4,128,256]{3,2,1,0:T(8,128)S(1)}) custom-call(s32[1]{0:T(128)S(6)} %copy.11.counts, f32[8]{0:T(128)} %table_in.1, s32[16,128]{1,0:T(8,128)} %week_ids.1, f32[16,128]{1,0:T(8,128)} %observed.1, f32[16,4,128,256]{3,2,1,0:T(8,128)} %footprints.1), custom_call_target="tpu_custom_call" | custom-call | flops 10000 | bytes 16777216 | tf_op jit(solution)/shard_map/pallas_call | solution.py:373
  11.5 1.8 %collective-permute-start.1 = (f32[64,256]{1,0:T(8,128)S(1)}, f32[64,256]{1,0:T(8,128)S(1)}, u32[]{:S(2)}, u32[]{:S(2)}) collective-permute-start(f32[64,256]{1,0:T(8,128)S(1)} %shard_map.106.refs_0_), channel_id=1, source_target_pairs={{0,2},{1,3},{2,0},{3,1},{4,6},{5,7},{6,4},{7,5},{8,10},{9,11},{10,... | collective-permute-start | bytes 196616 | tf_op jit(solution)/shard_map/ppermute | solution.py:33
  13.4 1.5 %collective-permute-start.4 = (f32[64,256]{1,0:T(8,128)S(1)}, f32[64,256]{1,0:T(8,128)S(1)}, u32[]{:S(2)}, u32[]{:S(2)}) collective-permute-start(f32[64,256]{1,0:T(8,128)S(1)} %shard_map.107.refs_2_.refs_3_), channel_id=1, source_target_pairs={{0,2},{1,3},{2,0},{3,1},{4,6},{5,7},{6,4},{7,5},{8,10},{9,11},{10,... | collective-permute-start | bytes 196616 | tf_op jit(solution)/shard_map/ppermute | solution.py:33
  16.2 1.5 %collective-permute-done.4.refs_3_ = f32[64,256]{1,0:T(8,128)S(1)} collective-permute-done((f32[64,256]{1,0:T(8,128)S(1)}, f32[64,256]{1,0:T(8,128)S(1)}, u32[]{:S(2)}, u32[]{:S(2)}) %collective-permute-start.4) | collective-permute-done | bytes 65568 | tf_op jit(solution)/shard_map/ppermute | solution.py:33
  17.7 1.2 %collective-permute-done.8.refs_7_ = f32[64,256]{1,0:T(8,128)S(1)} collective-permute-done((f32[64,256]{1,0:T(8,128)S(1)}, f32[64,256]{1,0:T(8,128)S(1)}, u32[]{:S(2)}, u32[]{:S(2)}) %collective-permute-start.8) | collective-permute-done | bytes 65568 | tf_op jit(solution)/shard_map/ppermute | solution.py:33
  18.9 2.0 %shard_map.108 = (f32[64,256]{1,0:T(8,128)S(1)}, f32[128,128]{1,0:T(8,128)S(1)}) custom-call(s32[4,16]{1,0:T(4,128)S(1)} %bitcast.3, s32[1]{0:T(128)} %bitcast.1.me, f32[16,4,128,256]{3,2,1,0:T(8,128)S(1)} %get-tuple-element.22.tiles, f32[128,128]{1,0:T(8,128)S(1)} %get-tuple-element.23.refs_2_.weights, f32[128,128]{1,0:T(8,128)S(1)} %get-tuple-element.26.observed, ...), custom_call_target="tpu_custom_call" | custom-call | flops 8388608 | bytes 8388608 | tf_op jit(solution)/shard_map/pallas_call | solution.py:395
  21.0 1.1 %collective-permute-start.9 = (f32[104,256]{1,0:T(8,128)S(1)}, f32[104,256]{1,0:T(8,128)S(1)}, u32[]{:S(2)}, u32[]{:S(2)}) collective-permute-start(f32[104,256]{1,0:T(8,128)S(1)} %shard_map.109), channel_id=1, source_target_pairs={{0,4},{1,5},{2,6},{3,7},{4,0},{5,1},{6,2},{7,3},{8,12},{9,13},{10,... | collective-permute-start | bytes 319496 | tf_op jit(solution)/shard_map/ppermute | solution.py:33
  22.1 3.1 %collective-permute-start.12 = (f32[64,256]{1,0:T(8,128)S(1)}, f32[64,256]{1,0:T(8,128)S(1)}, u32[]{:S(2)}, u32[]{:S(2)}) collective-permute-start(f32[64,256]{1,0:T(8,128)S(1)} %get-tuple-element.27.refs_0_.refs_2_.refs_3_), channel_id=1, source_target_pairs={{0,8},{1,9},{2,10},{3,11},{4,12},{5,13},{6,14},{7,15},{8,0},{9,1},... | collective-permute-start | bytes 196616 | tf_op jit(solution)/shard_map/ppermute | solution.py:33
  25.5 1.6 %collective-permute-start.10 = (f32[216,256]{1,0:T(8,128)S(1)}, f32[216,256]{1,0:T(8,128)S(1)}, u32[]{:S(2)}, u32[]{:S(2)}) collective-permute-start(f32[216,256]{1,0:T(8,128)S(1)} %shard_map.111.refs_1_), channel_id=1, source_target_pairs={{0,2},{1,3},{2,0},{3,1},{4,6},{5,7},{6,4},{7,5},{8,10},{9,11},{10,... | collective-permute-start | bytes 663560 | tf_op jit(solution)/shard_map/ppermute | solution.py:33
  27.3 1.4 %collective-permute-start.11 = (f32[168,256]{1,0:T(8,128)S(1)}, f32[168,256]{1,0:T(8,128)S(1)}, u32[]{:S(2)}, u32[]{:S(2)}) collective-permute-start(f32[168,256]{1,0:T(8,128)S(1)} %shard_map.110.refs_0_.refs_1_), channel_id=1, source_target_pairs={{0,2},{1,3},{2,0},{3,1},{4,6},{5,7},{6,4},{7,5},{8,10},{9,11},{10,... | collective-permute-start | bytes 516104 | tf_op jit(solution)/shard_map/ppermute | solution.py:33
  28.7 2.6 %collective-permute-done.13.refs_1_ = f32[64,256]{1,0:T(8,128)S(1)} collective-permute-done((f32[64,256]{1,0:T(8,128)S(1)}, f32[64,256]{1,0:T(8,128)S(1)}, u32[]{:S(2)}, u32[]{:S(2)}) %collective-permute-start.13) | collective-permute-done | bytes 65568 | tf_op jit(solution)/shard_map/ppermute | solution.py:33
  32.2 1.7 %collective-permute-done.10.refs_2_ = f32[216,256]{1,0:T(8,128)S(1)} collective-permute-done((f32[216,256]{1,0:T(8,128)S(1)}, f32[216,256]{1,0:T(8,128)S(1)}, u32[]{:S(2)}, u32[]{:S(2)}) %collective-permute-start.10) | collective-permute-done | bytes 221216 | tf_op jit(solution)/shard_map/ppermute | solution.py:33
  34.0 3.3 %collective-permute-done.11.refs_1_ = f32[168,256]{1,0:T(8,128)S(1)} collective-permute-done((f32[168,256]{1,0:T(8,128)S(1)}, f32[168,256]{1,0:T(8,128)S(1)}, u32[]{:S(2)}, u32[]{:S(2)}) %collective-permute-start.11) | collective-permute-done | bytes 172064 | tf_op jit(solution)/shard_map/ppermute | solution.py:33
  37.3 1.4 %collective-permute-done.17.refs_0_ = f32[128,256]{1,0:T(8,128)S(1)} collective-permute-done((f32[128,256]{1,0:T(8,128)S(1)}, f32[128,256]{1,0:T(8,128)S(1)}, u32[]{:S(2)}, u32[]{:S(2)}) %collective-permute-start.17) | collective-permute-done | bytes 131104 | tf_op jit(solution)/shard_map/ppermute | solution.py:33
  40.1 2.4 %shard_map.116 = (f32[72,256]{1,0:T(8,128)S(1)}, f32[96,256]{1,0:T(8,128)S(1)}, f32[128,128]{1,0:T(8,128)S(1)}) custom-call(s32[4,16]{1,0:T(4,128)S(1)} %bitcast.4, s32[1]{0:T(128)} %bitcast.1.me, f32[16,4,128,256]{3,2,1,0:T(8,128)S(1)} %get-tuple-element.22.tiles, f32[128,128]{1,0:T(8,128)S(1)} %get-tuple-element.23.refs_2_.weights, ...), custom_call_target="tpu_custom_call" | custom-call | flops 8388608 | bytes 8388608 | tf_op jit(solution)/shard_map/pallas_call | solution.py:406
  43.2 3.5 %collective-permute-start.21 = (f32[72,256]{1,0:T(8,128)S(1)}, f32[72,256]{1,0:T(8,128)S(1)}, u32[]{:S(2)}, u32[]{:S(2)}) collective-permute-start(f32[72,256]{1,0:T(8,128)S(1)} %get-tuple-element.31.refs_0_.refs_2_.refs_3_), channel_id=1, source_target_pairs={{0,8},{1,9},{2,10},{3,11},{4,12},{5,13},{6,14},{7,15},{8,0},{9,1},... | collective-permute-start | bytes 221192 | tf_op jit(solution)/shard_map/ppermute | solution.py:33
  47.0 1.9 %collective-permute-done.19.refs_1_.refs_2_ = f32[104,256]{1,0:T(8,128)S(1)} collective-permute-done((f32[104,256]{1,0:T(8,128)S(1)}, f32[104,256]{1,0:T(8,128)S(1)}, u32[]{:S(2)}, u32[]{:S(2)}) %collective-permute-start.19) | collective-permute-done | bytes 106528 | tf_op jit(solution)/shard_map/ppermute | solution.py:33
  48.9 1.9 %collective-permute-start.20 = (f32[176,256]{1,0:T(8,128)S(1)}, f32[176,256]{1,0:T(8,128)S(1)}, u32[]{:S(2)}, u32[]{:S(2)}) collective-permute-start(f32[176,256]{1,0:T(8,128)S(1)} %shard_map.118.refs_0_.refs_1_), channel_id=1, source_target_pairs={{0,2},{1,3},{2,0},{3,1},{4,6},{5,7},{6,4},{7,5},{8,10},{9,11},{10,... | collective-permute-start | bytes 540680 | tf_op jit(solution)/shard_map/ppermute | solution.py:33
  50.8 2.1 %collective-permute-done.22.refs_1_ = f32[72,256]{1,0:T(8,128)S(1)} collective-permute-done((f32[72,256]{1,0:T(8,128)S(1)}, f32[72,256]{1,0:T(8,128)S(1)}, u32[]{:S(2)}, u32[]{:S(2)}) %collective-permute-start.22) | collective-permute-done | bytes 73760 | tf_op jit(solution)/shard_map/ppermute | solution.py:33
  55.2 3.0 %collective-permute-done.26.refs_0_ = f32[144,256]{1,0:T(8,128)S(1)} collective-permute-done((f32[144,256]{1,0:T(8,128)S(1)}, f32[144,256]{1,0:T(8,128)S(1)}, u32[]{:S(2)}, u32[]{:S(2)}) %collective-permute-start.26) | collective-permute-done | bytes 147488 | tf_op jit(solution)/shard_map/ppermute | solution.py:33
  59.6 1.6 %shard_map.123 = (f32[16,1,128]{2,1,0:T(1,128)S(1)}, f32[32,256]{1,0:T(8,128)S(1)}, f32[32,256]{1,0:T(8,128)S(1)}, f32[16,128]{1,0:T(8,128)S(1)}, f32[16,128]{1,0:T(8,128)S(1)}) custom-call(s32[4,16]{1,0:T(4,128)S(1)} %bitcast.5, s32[1]{0:T(128)} %bitcast.1.me, f32[16,4,128,256]{3,2,1,0:T(8,128)S(1)} %get-tuple-element.22.tiles, ...), custom_call_target="tpu_custom_call" | custom-call | flops 8388608 | bytes 8388608 | tf_op jit(solution)/shard_map/pallas_call | solution.py:417
  61.3 10.7 %all_to_all.5.sums = f32[16,1,128]{2,1,0:T(1,128)S(1)} all-to-all(f32[16,1,128]{2,1,0:T(1,128)S(1)} %get-tuple-element.37), channel_id=1, replica_groups=mesh['groups'=2,'obs'=16] {'obs'}, dimensions={0} | all-to-all | bytes 16384 | tf_op jit(solution)/shard_map/all_to_all | solution.py:424
  (56 shorter events, 10.4 us)
Async XLA Ops:
  1.6 9.9 %collective-permute-start = (f32[104,256]{1,0:T(8,128)S(1)}, f32[104,256]{1,0:T(8,128)S(1)}, u32[]{:S(2)}, u32[]{:S(2)}) collective-permute-start(f32[104,256]{1,0:T(8,128)S(1)} %get-tuple-element.25.refs_0_.bundle), channel_id=1, source_target_pairs={{0,4},{1,5},{2,6},{3,7},{4,0},{5,1},{6,2},{7,3},{8,12},{9,13},{10,... | collective-permute-start | bytes 319496 | tf_op jit(solution)/shard_map/ppermute | solution.py:33
  4.7 8.7 %collective-permute-start.2 = (f32[104,256]{1,0:T(8,128)S(1)}, f32[104,256]{1,0:T(8,128)S(1)}, u32[]{:S(2)}, u32[]{:S(2)}) collective-permute-start(f32[104,256]{1,0:T(8,128)S(1)} %get-tuple-element.25.refs_0_.bundle), channel_id=1, source_target_pairs={{0,8},{1,9},{2,10},{3,11},{4,12},{5,13},{6,14},{7,15},{8,0},{9,1},... | collective-permute-start | bytes 319496 | tf_op jit(solution)/shard_map/ppermute | solution.py:33
  7.3 6.0 %collective-permute-start.3 = (f32[32,256]{1,0:T(8,128)}, f32[32,256]{1,0:T(8,128)S(1)}, u32[]{:S(2)}, u32[]{:S(2)}) collective-permute-start(f32[32,256]{1,0:T(8,128)} %flux.1), channel_id=1, source_target_pairs={{0,12},{1,13},{2,14},{3,15},{4,8},{5,9},{6,10},{7,11},{8,4},{9,5},... | collective-permute-start | bytes 98312 | tf_op jit(solution)/shard_map/ppermute | solution.py:33
  11.5 4.7 %collective-permute-start.1 = (f32[64,256]{1,0:T(8,128)S(1)}, f32[64,256]{1,0:T(8,128)S(1)}, u32[]{:S(2)}, u32[]{:S(2)}) collective-permute-start(f32[64,256]{1,0:T(8,128)S(1)} %shard_map.106.refs_0_), channel_id=1, source_target_pairs={{0,2},{1,3},{2,0},{3,1},{4,6},{5,7},{6,4},{7,5},{8,10},{9,11},{10,... | collective-permute-start | bytes 196616 | tf_op jit(solution)/shard_map/ppermute | solution.py:33
  13.4 4.3 %collective-permute-start.4 = (f32[64,256]{1,0:T(8,128)S(1)}, f32[64,256]{1,0:T(8,128)S(1)}, u32[]{:S(2)}, u32[]{:S(2)}) collective-permute-start(f32[64,256]{1,0:T(8,128)S(1)} %shard_map.107.refs_2_.refs_3_), channel_id=1, source_target_pairs={{0,2},{1,3},{2,0},{3,1},{4,6},{5,7},{6,4},{7,5},{8,10},{9,11},{10,... | collective-permute-start | bytes 196616 | tf_op jit(solution)/shard_map/ppermute | solution.py:33
  14.9 2.8 %collective-permute-start.5 = (f32[64,256]{1,0:T(8,128)S(1)}, f32[64,256]{1,0:T(8,128)S(1)}, u32[]{:S(2)}, u32[]{:S(2)}) collective-permute-start(f32[64,256]{1,0:T(8,128)S(1)} %shard_map.106.refs_0_), channel_id=1, source_target_pairs={{0,1},{1,0},{2,3},{3,2},{4,5},{5,4},{6,7},{7,6},{8,9},{9,8},{10,11... | collective-permute-start | bytes 196616 | tf_op jit(solution)/shard_map/ppermute | solution.py:33
  14.9 2.8 %collective-permute-start.7 = (f32[64,256]{1,0:T(8,128)S(1)}, f32[64,256]{1,0:T(8,128)S(1)}, u32[]{:S(2)}, u32[]{:S(2)}) collective-permute-start(f32[64,256]{1,0:T(8,128)S(1)} %shard_map.107.refs_2_.refs_3_), channel_id=1, source_target_pairs={{0,1},{1,0},{2,3},{3,2},{4,5},{5,4},{6,7},{7,6},{8,9},{9,8},{10,11... | collective-permute-start | bytes 196616 | tf_op jit(solution)/shard_map/ppermute | solution.py:33
  16.2 1.5 %collective-permute-start.6 = (f32[64,256]{1,0:T(8,128)S(1)}, f32[64,256]{1,0:T(8,128)S(1)}, u32[]{:S(2)}, u32[]{:S(2)}) collective-permute-start(f32[64,256]{1,0:T(8,128)S(1)} %collective-permute-done.1.refs_1_), channel_id=1, source_target_pairs={{0,1},{1,0},{2,3},{3,2},{4,5},{5,4},{6,7},{7,6},{8,9},{9,8},{10,11... | collective-permute-start | bytes 196616 | tf_op jit(solution)/shard_map/ppermute | solution.py:33
  21.0 6.3 %collective-permute-start.9 = (f32[104,256]{1,0:T(8,128)S(1)}, f32[104,256]{1,0:T(8,128)S(1)}, u32[]{:S(2)}, u32[]{:S(2)}) collective-permute-start(f32[104,256]{1,0:T(8,128)S(1)} %shard_map.109), channel_id=1, source_target_pairs={{0,4},{1,5},{2,6},{3,7},{4,0},{5,1},{6,2},{7,3},{8,12},{9,13},{10,... | collective-permute-start | bytes 319496 | tf_op jit(solution)/shard_map/ppermute | solution.py:33
  22.1 6.6 %collective-permute-start.12 = (f32[64,256]{1,0:T(8,128)S(1)}, f32[64,256]{1,0:T(8,128)S(1)}, u32[]{:S(2)}, u32[]{:S(2)}) collective-permute-start(f32[64,256]{1,0:T(8,128)S(1)} %get-tuple-element.27.refs_0_.refs_2_.refs_3_), channel_id=1, source_target_pairs={{0,8},{1,9},{2,10},{3,11},{4,12},{5,13},{6,14},{7,15},{8,0},{9,1},... | collective-permute-start | bytes 196616 | tf_op jit(solution)/shard_map/ppermute | solution.py:33
  25.2 6.1 %collective-permute-start.13 = (f32[64,256]{1,0:T(8,128)S(1)}, f32[64,256]{1,0:T(8,128)S(1)}, u32[]{:S(2)}, u32[]{:S(2)}) collective-permute-start(f32[64,256]{1,0:T(8,128)S(1)} %get-tuple-element.27.refs_0_.refs_2_.refs_3_), channel_id=1, source_target_pairs={{0,12},{1,13},{2,14},{3,15},{4,8},{5,9},{6,10},{7,11},{8,4},{9,5},... | collective-permute-start | bytes 196616 | tf_op jit(solution)/shard_map/ppermute | solution.py:33
  25.5 8.4 %collective-permute-start.10 = (f32[216,256]{1,0:T(8,128)S(1)}, f32[216,256]{1,0:T(8,128)S(1)}, u32[]{:S(2)}, u32[]{:S(2)}) collective-permute-start(f32[216,256]{1,0:T(8,128)S(1)} %shard_map.111.refs_1_), channel_id=1, source_target_pairs={{0,2},{1,3},{2,0},{3,1},{4,6},{5,7},{6,4},{7,5},{8,10},{9,11},{10,... | collective-permute-start | bytes 663560 | tf_op jit(solution)/shard_map/ppermute | solution.py:33
  27.3 10.1 %collective-permute-start.11 = (f32[168,256]{1,0:T(8,128)S(1)}, f32[168,256]{1,0:T(8,128)S(1)}, u32[]{:S(2)}, u32[]{:S(2)}) collective-permute-start(f32[168,256]{1,0:T(8,128)S(1)} %shard_map.110.refs_0_.refs_1_), channel_id=1, source_target_pairs={{0,2},{1,3},{2,0},{3,1},{4,6},{5,7},{6,4},{7,5},{8,10},{9,11},{10,... | collective-permute-start | bytes 516104 | tf_op jit(solution)/shard_map/ppermute | solution.py:33
  31.3 7.4 %collective-permute-start.17 = (f32[128,256]{1,0:T(8,128)S(1)}, f32[128,256]{1,0:T(8,128)S(1)}, u32[]{:S(2)}, u32[]{:S(2)}) collective-permute-start(f32[128,256]{1,0:T(8,128)S(1)} %shard_map.113.refs_2_), channel_id=1, source_target_pairs={{0,2},{1,3},{2,0},{3,1},{4,6},{5,7},{6,4},{7,5},{8,10},{9,11},{10,... | collective-permute-start | bytes 393224 | tf_op jit(solution)/shard_map/ppermute | solution.py:33
  32.2 6.7 %collective-permute-start.16 = (f32[128,256]{1,0:T(8,128)S(1)}, f32[128,256]{1,0:T(8,128)S(1)}, u32[]{:S(2)}, u32[]{:S(2)}) collective-permute-start(f32[128,256]{1,0:T(8,128)S(1)} %shard_map.113.refs_2_), channel_id=1, source_target_pairs={{0,1},{1,0},{2,3},{3,2},{4,5},{5,4},{6,7},{7,6},{8,9},{9,8},{10,11... | collective-permute-start | bytes 393224 | tf_op jit(solution)/shard_map/ppermute | solution.py:33
  33.9 4.9 %collective-permute-start.14 = (f32[408,256]{1,0:T(8,128)S(1)}, f32[408,256]{1,0:T(8,128)S(1)}, u32[]{:S(2)}, u32[]{:S(2)}) collective-permute-start(f32[408,256]{1,0:T(8,128)S(1)} %shard_map.112.refs_0_), channel_id=1, source_target_pairs={{0,1},{1,0},{2,3},{3,2},{4,5},{5,4},{6,7},{7,6},{8,9},{9,8},{10,11... | collective-permute-start | bytes 1253384 | tf_op jit(solution)/shard_map/ppermute | solution.py:33
  42.5 6.4 %collective-permute-start.19 = (f32[104,256]{1,0:T(8,128)S(1)}, f32[104,256]{1,0:T(8,128)S(1)}, u32[]{:S(2)}, u32[]{:S(2)}) collective-permute-start(f32[104,256]{1,0:T(8,128)S(1)} %shard_map.117), channel_id=1, source_target_pairs={{0,4},{1,5},{2,6},{3,7},{4,0},{5,1},{6,2},{7,3},{8,12},{9,13},{10,... | collective-permute-start | bytes 319496 | tf_op jit(solution)/shard_map/ppermute | solution.py:33
  43.2 7.6 %collective-permute-start.21 = (f32[72,256]{1,0:T(8,128)S(1)}, f32[72,256]{1,0:T(8,128)S(1)}, u32[]{:S(2)}, u32[]{:S(2)}) collective-permute-start(f32[72,256]{1,0:T(8,128)S(1)} %get-tuple-element.31.refs_0_.refs_2_.refs_3_), channel_id=1, source_target_pairs={{0,8},{1,9},{2,10},{3,11},{4,12},{5,13},{6,14},{7,15},{8,0},{9,1},... | collective-permute-start | bytes 221192 | tf_op jit(solution)/shard_map/ppermute | solution.py:33
  46.7 6.2 %collective-permute-start.22 = (f32[72,256]{1,0:T(8,128)S(1)}, f32[72,256]{1,0:T(8,128)S(1)}, u32[]{:S(2)}, u32[]{:S(2)}) collective-permute-start(f32[72,256]{1,0:T(8,128)S(1)} %get-tuple-element.31.refs_0_.refs_2_.refs_3_), channel_id=1, source_target_pairs={{0,12},{1,13},{2,14},{3,15},{4,8},{5,9},{6,10},{7,11},{8,4},{9,5},... | collective-permute-start | bytes 221192 | tf_op jit(solution)/shard_map/ppermute | solution.py:33
  48.9 6.2 %collective-permute-start.20 = (f32[176,256]{1,0:T(8,128)S(1)}, f32[176,256]{1,0:T(8,128)S(1)}, u32[]{:S(2)}, u32[]{:S(2)}) collective-permute-start(f32[176,256]{1,0:T(8,128)S(1)} %shard_map.118.refs_0_.refs_1_), channel_id=1, source_target_pairs={{0,2},{1,3},{2,0},{3,1},{4,6},{5,7},{6,4},{7,5},{8,10},{9,11},{10,... | collective-permute-start | bytes 540680 | tf_op jit(solution)/shard_map/ppermute | solution.py:33
  52.9 5.2 %collective-permute-start.26 = (f32[144,256]{1,0:T(8,128)S(1)}, f32[144,256]{1,0:T(8,128)S(1)}, u32[]{:S(2)}, u32[]{:S(2)}) collective-permute-start(f32[144,256]{1,0:T(8,128)S(1)} %shard_map.120.refs_2_), channel_id=1, source_target_pairs={{0,2},{1,3},{2,0},{3,1},{4,6},{5,7},{6,4},{7,5},{8,10},{9,11},{10,... | collective-permute-start | bytes 442376 | tf_op jit(solution)/shard_map/ppermute | solution.py:33
  53.6 4.6 %collective-permute-start.25 = (f32[144,256]{1,0:T(8,128)S(1)}, f32[144,256]{1,0:T(8,128)S(1)}, u32[]{:S(2)}, u32[]{:S(2)}) collective-permute-start(f32[144,256]{1,0:T(8,128)S(1)} %shard_map.120.refs_2_), channel_id=1, source_target_pairs={{0,1},{1,0},{2,3},{3,2},{4,5},{5,4},{6,7},{7,6},{8,9},{9,8},{10,11... | collective-permute-start | bytes 442376 | tf_op jit(solution)/shard_map/ppermute | solution.py:33
  53.6 4.6 %collective-permute-start.23 = (f32[368,256]{1,0:T(8,128)S(1)}, f32[368,256]{1,0:T(8,128)S(1)}, u32[]{:S(2)}, u32[]{:S(2)}) collective-permute-start(f32[368,256]{1,0:T(8,128)S(1)} %shard_map.119.refs_0_), channel_id=1, source_target_pairs={{0,1},{1,0},{2,3},{3,2},{4,5},{5,4},{6,7},{7,6},{8,9},{9,8},{10,11... | collective-permute-start | bytes 1130504 | tf_op jit(solution)/shard_map/ppermute | solution.py:33
  55.2 3.1 %collective-permute-start.24 = (f32[176,256]{1,0:T(8,128)S(1)}, f32[176,256]{1,0:T(8,128)S(1)}, u32[]{:S(2)}, u32[]{:S(2)}) collective-permute-start(f32[176,256]{1,0:T(8,128)S(1)} %collective-permute-done.20.refs_1_), channel_id=1, source_target_pairs={{0,1},{1,0},{2,3},{3,2},{4,5},{5,4},{6,7},{7,6},{8,9},{9,8},{10,11... | collective-permute-start | bytes 540680 | tf_op jit(solution)/shard_map/ppermute | solution.py:33
  (5 other events, 23.9 us)

commit v5 on v4

--- a/solution.py
+++ b/solution.py
@@ -104,7 +104,7 @@
     beside = swap(pile([x, bundle_far], [cut, (pitch, own + at, rows)], x), near)
     count, extra = len(masks) * size, len(held) * rows
     first = Part(
-        pile([x, beside, beside], [(count, 0, count), (count + extra, 0, count), (count + extra, count, extra)], x),
+        pile([x, beside, beside], [(count, 0, count), (count + extra, 0, count), (count + extra, count, extra)], paired),
         masks + shift(masks, near), shift(held, both))
     second = Part(pile([beyond, across], [cut] * 2, x, LONG), shift(masks, far) + shift(masks, both))
     few = (pitch - own, at, rows)
@@ -223,11 +223,14 @@
         terms_out[pl.ds(b * each + k, 1), :] = jnp.sum(tiles[b, k] * scaled, axis=0, keepdims=True)
 
 
-def first_kernel(shapes, tile_ids, me, tiles, weights, observed, *refs):
-    *parts, terms_out, departure_out, flux = refs
+def first_kernel(shapes, ids, me, tiles, weights, observed, *refs):
+    *parts, terms_out, departure_out, flux, tile_ids, sem = refs
+    copy = pltpu.make_async_copy(ids, tile_ids, sem)
+    copy.start()
     blocks, each, tile_rows, _ = tiles.shape
     own = parts[0].shape[0] // len(shapes[0][0])
     by_owner(me[0], layout(shapes, parts, own, 0)[0], own, flux)
+    copy.wait()
     lane = lax.broadcasted_iota(jnp.int32, (tile_rows, tile_rows), 1)
 
     def block(b, columns):
@@ -281,15 +284,18 @@
     total_out[...] = sum_terms(pieces, count, hot, 0)
 
 
-def second_kernel(shapes, tile_ids, me, tiles, weights, want, bundle, total, more, hot, *refs):
+def second_kernel(shapes, ids, me, tiles, weights, want, bundle, total, more, hot, *refs):
     parts = refs[:len(shapes)]
-    terms_out, gradient_out, image_out = refs[len(shapes):]
+    terms_out, gradient_out, image_out, tile_ids, sem = refs[len(shapes):]
+    copy = pltpu.make_async_copy(ids, tile_ids, sem)
+    copy.start()
     blocks, each, tile_rows, _ = tiles.shape
     count = blocks * each
     own = want.shape[0] - count
     pieces, _ = layout(shapes, parts, count, 0)
     lane = lax.broadcasted_iota(jnp.int32, (tile_rows, tile_rows), 1)
     gradient_out[...] = total[...] + sum_terms(pieces, count, hot, hot.shape[1] - len(pieces) * count)
+    copy.wait()
     mine = gradient_out[count:, :] + bundle[own:2 * own, :]
     gradient_out[count:, :] = mine
 
@@ -310,10 +316,12 @@
         mine, bundle[2 * own + 8:3 * own + 8, :], weights[...], columns, (8, terms_out.shape[1]))
 
 
-def third_kernel(shapes, late_shapes, tile_ids, me, tiles, weights, want, bundle, total, scale, hot, gradient, departure,
+def third_kernel(shapes, late_shapes, ids, me, tiles, weights, want, bundle, total, scale, hot, gradient, departure,
                  image, *refs):
     parts, late = refs[:len(shapes)], refs[len(shapes):len(shapes) + len(late_shapes)]
-    sums_out, flux_out, gradient_out, departure_out, image_out, second = refs[len(shapes) + len(late_shapes):]
+    sums_out, flux_out, gradient_out, departure_out, image_out, second, tile_ids, sem = refs[len(shapes) + len(late_shapes):]
+    copy = pltpu.make_async_copy(ids, tile_ids, sem)
+    copy.start()
     blocks, each, tile_rows, _ = tiles.shape
     count = blocks * each
     own = want.shape[0] - count
@@ -325,6 +333,7 @@
         sums = sums + ref[at + count:at + count + 1, :128]
     step = sums[:, 0:1] / sums[:, 1:2]
     second[...] = total[...] + sum_terms(late, count, hot, hot.shape[1] - len(late) * count)
+    copy.wait()
     old = gradient[count:, :]
     precision = bundle[2 * own + 8:, :]
     mine = old - step * (second[count:, :] + precision * old)
@@ -389,12 +398,13 @@
     def split(parts):
         return [p for i, p in enumerate(parts) if i % 4 != 3], parts[3::4]
 
+    ids_scratch = [pltpu.SMEM((each, blocks), jnp.int32), pltpu.SemaphoreType.DMA]
     hot_shape = (count + own, n * count)
     whole = (n * own, cols)
     work = dict(flops=4 * footprints.size, moved=4 * footprints.size)
     terms, departure = call(
-        functools.partial(first_kernel, shapes(parts)), [SMEM] * 2 + [VMEM] * (3 + len(parts)),
-        [(count, cols), square], [pltpu.VMEM(whole, F32)], **work,
+        functools.partial(first_kernel, shapes(parts)), [VMEM, SMEM] + [VMEM] * (3 + len(parts)),
+        [(count, cols), square], [pltpu.VMEM(whole, F32), *ids_scratch], **work,
     )(*place, tiles, weights, observed_t, *arrays(parts))
 
     parts = spread(terms, rest, 0, own + 8)
@@ -404,8 +414,8 @@
         [(count + own, cols), whole, hot_shape], moved=4 * n * count * cols,
     )(place[1], want, *arrays(early))
     terms, gradient, image = call(
-        functools.partial(second_kernel, shapes(late)), [SMEM] * 2 + [VMEM] * (7 + len(late)),
-        [(count + 8, cols), (count + own, cols), square], **work,
+        functools.partial(second_kernel, shapes(late)), [VMEM, SMEM] + [VMEM] * (7 + len(late)),
+        [(count + 8, cols), (count + own, cols), square], ids_scratch, **work,
     )(*place, tiles, weights, want, bundle, total, more, hot, *arrays(late))
 
     parts = spread(terms, rest, own + 8, own)
@@ -416,9 +426,9 @@
     )(place[1], want, *arrays(early), hot)
     sums, flux, gradient, departure, image = call(
         functools.partial(third_kernel, shapes(early), shapes(late)),
-        [SMEM] * 2 + [VMEM] * (10 + len(early) + len(late)),
+        [VMEM, SMEM] + [VMEM] * (10 + len(early) + len(late)),
         [(n, 1, 128), (own, cols), (own, cols), (blocks, tile_rows), (blocks, tile_rows)],
-        [pltpu.VMEM((count + own, cols), F32)], **work,
+        [pltpu.VMEM((count + own, cols), F32), *ids_scratch], **work,
     )(*place, tiles, weights, want, bundle, total, scale, hot, gradient, departure, image, *arrays(early), *arrays(late))
 
     sums = lax.all_to_all(sums, "obs", 0, 0)

time: 72.9 us -> 70.6 us (0.968)
  waiting for transfers between devices: 22.6 us -> 20.3 us
    ppermute x28, waiting for transfers between devices: 22.6 us -> 20.3 us  [swap(): return lax.ppermute(x, 'obs', [(i, i ^ mask) for i in range(n)])]
  transfers between devices with their start and end apart: 28 -> 28, of which waited for: 15 -> 12; matrix products, arithmetic and copies ran while one was open for 0% -> 0% of each run, Pallas kernels for 6% -> 9%
where the time goes in v5:
time: 70.6 us; the launch traced here: 70.4 us
  starting transfers between devices  26.1 us (37%)
  waiting for transfers between devices  20.3 us (29%)
  Pallas kernels  11.9 us (17%)
  blocking collectives  10.5 us (15%)
  between operations  1.51 us (2%)
    ppermute x28, starting transfers between devices, swap(): return lax.ppermute(x, 'obs', [(i, i ^ mask) for i in range(n)])  26.1 us
    ppermute x28, waiting for transfers between devices, swap(): return lax.ppermute(x, 'obs', [(i, i ^ mask) for i in range(n)])  20.3 us
    all_to_all x1, blocking collectives, body(): sums = lax.all_to_all(sums, 'obs', 0, 0)  10.5 us
    pallas_call x1, Pallas kernels, body(): call(prepare_kernel, [SMEM] + [HBM] * 4, [square, square, footprints.shap...  3.53 us
    pallas_call x1, Pallas kernels, body(): call(functools.partial(second_kernel, shapes(late)), [VMEM, SMEM] + [VMEM...  2.11 us
    pallas_call x1, Pallas kernels, body(): call(functools.partial(first_kernel, shapes(parts)), [VMEM, SMEM] + [VMEM...  2.05 us
    pallas_call x1, Pallas kernels, body(): call(functools.partial(third_kernel, shapes(early), shapes(late)), [VMEM,...  1.58 us
  transfers between devices with their start and end apart: 28, of which 12 were waited for; matrix products, arithmetic and copies ran while one was open for 0% of the time, Pallas kernels for 9%

profile of v5, /device:TPU:0, one launch (start us, length us, event | category | flops | bytes accessed | tf_op | source)
XLA Modules:
  0.0 70.4 jit_solution(2455511677708504053)
XLA Ops:
  1.6 3.1 %collective-permute-start = (f32[104,256]{1,0:T(8,128)S(1)}, f32[104,256]{1,0:T(8,128)S(1)}, u32[]{:S(2)}, u32[]{:S(2)}) collective-permute-start(f32[104,256]{1,0:T(8,128)S(1)} %get-tuple-element.25.refs_0_.bundle), channel_id=1, source_target_pairs={{0,4},{1,5},{2,6},{3,7},{4,0},{5,1},{6,2},{7,3},{8,12},{9,13},{10,... | collective-permute-start | bytes 319496 | tf_op jit(solution)/shard_map/ppermute | solution.py:33
  4.7 2.6 %collective-permute-start.2 = (f32[104,256]{1,0:T(8,128)S(1)}, f32[104,256]{1,0:T(8,128)S(1)}, u32[]{:S(2)}, u32[]{:S(2)}) collective-permute-start(f32[104,256]{1,0:T(8,128)S(1)} %get-tuple-element.25.refs_0_.bundle), channel_id=1, source_target_pairs={{0,8},{1,9},{2,10},{3,11},{4,12},{5,13},{6,14},{7,15},{8,0},{9,1},... | collective-permute-start | bytes 319496 | tf_op jit(solution)/shard_map/ppermute | solution.py:33
  7.9 3.5 %shard_map.104 = (f32[128,128]{1,0:T(8,128)S(1)}, f32[128,128]{1,0:T(8,128)S(1)}, f32[16,4,128,256]{3,2,1,0:T(8,128)S(1)}) custom-call(s32[1]{0:T(128)S(6)} %copy.11.counts, f32[8]{0:T(128)} %table_in.1, s32[16,128]{1,0:T(8,128)} %week_ids.1, f32[16,128]{1,0:T(8,128)} %observed.1, f32[16,4,128,256]{3,2,1,0:T(8,128)} %footprints.1), custom_call_target="tpu_custom_call" | custom-call | flops 10000 | bytes 16777216 | tf_op jit(solution)/shard_map/pallas_call | solution.py:382
  11.5 1.8 %collective-permute-start.1 = (f32[64,256]{1,0:T(8,128)S(1)}, f32[64,256]{1,0:T(8,128)S(1)}, u32[]{:S(2)}, u32[]{:S(2)}) collective-permute-start(f32[64,256]{1,0:T(8,128)S(1)} %shard_map.106.refs_0_), channel_id=1, source_target_pairs={{0,2},{1,3},{2,0},{3,1},{4,6},{5,7},{6,4},{7,5},{8,10},{9,11},{10,... | collective-permute-start | bytes 196616 | tf_op jit(solution)/shard_map/ppermute | solution.py:33
  13.4 1.5 %collective-permute-start.4 = (f32[64,256]{1,0:T(8,128)S(1)}, f32[64,256]{1,0:T(8,128)S(1)}, u32[]{:S(2)}, u32[]{:S(2)}) collective-permute-start(f32[64,256]{1,0:T(8,128)S(1)} %shard_map.107.refs_2_.refs_3_), channel_id=1, source_target_pairs={{0,2},{1,3},{2,0},{3,1},{4,6},{5,7},{6,4},{7,5},{8,10},{9,11},{10,... | collective-permute-start | bytes 196616 | tf_op jit(solution)/shard_map/ppermute | solution.py:33
  16.4 2.0 %collective-permute-done.4.refs_3_ = f32[64,256]{1,0:T(8,128)S(1)} collective-permute-done((f32[64,256]{1,0:T(8,128)S(1)}, f32[64,256]{1,0:T(8,128)S(1)}, u32[]{:S(2)}, u32[]{:S(2)}) %collective-permute-start.4) | collective-permute-done | bytes 65568 | tf_op jit(solution)/shard_map/ppermute | solution.py:33
  18.5 1.2 %collective-permute-done.8.refs_7_ = f32[64,256]{1,0:T(8,128)S(1)} collective-permute-done((f32[64,256]{1,0:T(8,128)S(1)}, f32[64,256]{1,0:T(8,128)S(1)}, u32[]{:S(2)}, u32[]{:S(2)}) %collective-permute-start.8) | collective-permute-done | bytes 65568 | tf_op jit(solution)/shard_map/ppermute | solution.py:33
  19.7 2.0 %shard_map.108 = (f32[64,256]{1,0:T(8,128)S(1)}, f32[128,128]{1,0:T(8,128)S(1)}) custom-call(s32[4,16]{1,0:T(4,128)S(1)} %bitcast.3, s32[1]{0:T(128)} %bitcast.1.me, f32[16,4,128,256]{3,2,1,0:T(8,128)S(1)} %get-tuple-element.22.tiles, f32[128,128]{1,0:T(8,128)S(1)} %get-tuple-element.23.refs_2_.weights, f32[128,128]{1,0:T(8,128)S(1)} %get-tuple-element.26.observed, ...), custom_call_target="tpu_custom_call" | custom-call | flops 8388608 | bytes 8388608 | tf_op jit(solution)/shard_map/pallas_call | solution.py:405
  22.8 3.2 %collective-permute-start.12 = (f32[64,256]{1,0:T(8,128)S(1)}, f32[64,256]{1,0:T(8,128)S(1)}, u32[]{:S(2)}, u32[]{:S(2)}) collective-permute-start(f32[64,256]{1,0:T(8,128)S(1)} %get-tuple-element.27.refs_0_.refs_2_.refs_3_), channel_id=1, source_target_pairs={{0,8},{1,9},{2,10},{3,11},{4,12},{5,13},{6,14},{7,15},{8,0},{9,1},... | collective-permute-start | bytes 196616 | tf_op jit(solution)/shard_map/ppermute | solution.py:33
  26.2 1.8 %collective-permute-done.9.refs_1_.refs_2_ = f32[104,256]{1,0:T(8,128)S(1)} collective-permute-done((f32[104,256]{1,0:T(8,128)S(1)}, f32[104,256]{1,0:T(8,128)S(1)}, u32[]{:S(2)}, u32[]{:S(2)}) %collective-permute-start.9) | collective-permute-done | bytes 106528 | tf_op jit(solution)/shard_map/ppermute | solution.py:33
  28.0 1.6 %collective-permute-start.11 = (f32[168,256]{1,0:T(8,128)S(1)}, f32[168,256]{1,0:T(8,128)S(1)}, u32[]{:S(2)}, u32[]{:S(2)}) collective-permute-start(f32[168,256]{1,0:T(8,128)S(1)} %shard_map.111.refs_0_.refs_1_), channel_id=1, source_target_pairs={{0,2},{1,3},{2,0},{3,1},{4,6},{5,7},{6,4},{7,5},{8,10},{9,11},{10,... | collective-permute-start | bytes 516104 | tf_op jit(solution)/shard_map/ppermute | solution.py:33
  29.7 2.4 %collective-permute-done.13.refs_1_ = f32[64,256]{1,0:T(8,128)S(1)} collective-permute-done((f32[64,256]{1,0:T(8,128)S(1)}, f32[64,256]{1,0:T(8,128)S(1)}, u32[]{:S(2)}, u32[]{:S(2)}) %collective-permute-start.13) | collective-permute-done | bytes 65568 | tf_op jit(solution)/shard_map/ppermute | solution.py:33
  32.1 1.3 %collective-permute-start.17 = (f32[128,256]{1,0:T(8,128)S(1)}, f32[128,256]{1,0:T(8,128)S(1)}, u32[]{:S(2)}, u32[]{:S(2)}) collective-permute-start(f32[128,256]{1,0:T(8,128)S(1)} %shard_map.113.refs_2_), channel_id=1, source_target_pairs={{0,2},{1,3},{2,0},{3,1},{4,6},{5,7},{6,4},{7,5},{8,10},{9,11},{10,... | collective-permute-start | bytes 393224 | tf_op jit(solution)/shard_map/ppermute | solution.py:33
  34.1 3.0 %collective-permute-done.17.refs_0_ = f32[128,256]{1,0:T(8,128)S(1)} collective-permute-done((f32[128,256]{1,0:T(8,128)S(1)}, f32[128,256]{1,0:T(8,128)S(1)}, u32[]{:S(2)}, u32[]{:S(2)}) %collective-permute-start.17) | collective-permute-done | bytes 131104 | tf_op jit(solution)/shard_map/ppermute | solution.py:33
  38.6 2.1 %shard_map.116 = (f32[72,256]{1,0:T(8,128)S(1)}, f32[96,256]{1,0:T(8,128)S(1)}, f32[128,128]{1,0:T(8,128)S(1)}) custom-call(s32[4,16]{1,0:T(4,128)S(1)} %bitcast.4, s32[1]{0:T(128)} %bitcast.1.me, f32[16,4,128,256]{3,2,1,0:T(8,128)S(1)} %get-tuple-element.22.tiles, f32[128,128]{1,0:T(8,128)S(1)} %get-tuple-element.23.refs_2_.weights, ...), custom_call_target="tpu_custom_call" | custom-call | flops 8388608 | bytes 8388608 | tf_op jit(solution)/shard_map/pallas_call | solution.py:416
  41.7 2.4 %collective-permute-start.21 = (f32[72,256]{1,0:T(8,128)S(1)}, f32[72,256]{1,0:T(8,128)S(1)}, u32[]{:S(2)}, u32[]{:S(2)}) collective-permute-start(f32[72,256]{1,0:T(8,128)S(1)} %get-tuple-element.31.refs_0_.refs_2_.refs_3_), channel_id=1, source_target_pairs={{0,8},{1,9},{2,10},{3,11},{4,12},{5,13},{6,14},{7,15},{8,0},{9,1},... | collective-permute-start | bytes 221192 | tf_op jit(solution)/shard_map/ppermute | solution.py:33
  44.0 1.1 %collective-permute-start.22 = (f32[72,256]{1,0:T(8,128)S(1)}, f32[72,256]{1,0:T(8,128)S(1)}, u32[]{:S(2)}, u32[]{:S(2)}) collective-permute-start(f32[72,256]{1,0:T(8,128)S(1)} %get-tuple-element.31.refs_0_.refs_2_.refs_3_), channel_id=1, source_target_pairs={{0,12},{1,13},{2,14},{3,15},{4,8},{5,9},{6,10},{7,11},{8,4},{9,5},... | collective-permute-start | bytes 221192 | tf_op jit(solution)/shard_map/ppermute | solution.py:33
  45.2 1.6 %collective-permute-done.19.refs_1_.refs_2_ = f32[104,256]{1,0:T(8,128)S(1)} collective-permute-done((f32[104,256]{1,0:T(8,128)S(1)}, f32[104,256]{1,0:T(8,128)S(1)}, u32[]{:S(2)}, u32[]{:S(2)}) %collective-permute-start.19) | collective-permute-done | bytes 106528 | tf_op jit(solution)/shard_map/ppermute | solution.py:33
  46.8 1.3 %collective-permute-start.20 = (f32[176,256]{1,0:T(8,128)S(1)}, f32[176,256]{1,0:T(8,128)S(1)}, u32[]{:S(2)}, u32[]{:S(2)}) collective-permute-start(f32[176,256]{1,0:T(8,128)S(1)} %shard_map.118.refs_0_.refs_1_), channel_id=1, source_target_pairs={{0,2},{1,3},{2,0},{3,1},{4,6},{5,7},{6,4},{7,5},{8,10},{9,11},{10,... | collective-permute-start | bytes 540680 | tf_op jit(solution)/shard_map/ppermute | solution.py:33
  48.1 2.7 %collective-permute-done.21.refs_0_ = f32[72,256]{1,0:T(8,128)S(1)} collective-permute-done((f32[72,256]{1,0:T(8,128)S(1)}, f32[72,256]{1,0:T(8,128)S(1)}, u32[]{:S(2)}, u32[]{:S(2)}) %collective-permute-start.21) | collective-permute-done | bytes 73760 | tf_op jit(solution)/shard_map/ppermute | solution.py:33
  50.8 1.4 %collective-permute-start.26 = (f32[144,256]{1,0:T(8,128)S(1)}, f32[144,256]{1,0:T(8,128)S(1)}, u32[]{:S(2)}, u32[]{:S(2)}) collective-permute-start(f32[144,256]{1,0:T(8,128)S(1)} %shard_map.120.refs_2_), channel_id=1, source_target_pairs={{0,2},{1,3},{2,0},{3,1},{4,6},{5,7},{6,4},{7,5},{8,10},{9,11},{10,... | collective-permute-start | bytes 442376 | tf_op jit(solution)/shard_map/ppermute | solution.py:33
  52.9 3.1 %collective-permute-done.26.refs_0_ = f32[144,256]{1,0:T(8,128)S(1)} collective-permute-done((f32[144,256]{1,0:T(8,128)S(1)}, f32[144,256]{1,0:T(8,128)S(1)}, u32[]{:S(2)}, u32[]{:S(2)}) %collective-permute-start.26) | collective-permute-done | bytes 147488 | tf_op jit(solution)/shard_map/ppermute | solution.py:33
  57.5 1.6 %shard_map.123 = (f32[16,1,128]{2,1,0:T(1,128)S(1)}, f32[32,256]{1,0:T(8,128)S(1)}, f32[32,256]{1,0:T(8,128)S(1)}, f32[16,128]{1,0:T(8,128)S(1)}, f32[16,128]{1,0:T(8,128)S(1)}) custom-call(s32[4,16]{1,0:T(4,128)S(1)} %bitcast.5, s32[1]{0:T(128)} %bitcast.1.me, f32[16,4,128,256]{3,2,1,0:T(8,128)S(1)} %get-tuple-element.22.tiles, ...), custom_call_target="tpu_custom_call" | custom-call | flops 8388608 | bytes 8388608 | tf_op jit(solution)/shard_map/pallas_call | solution.py:427
  59.1 10.5 %all_to_all.5.sums = f32[16,1,128]{2,1,0:T(1,128)S(1)} all-to-all(f32[16,1,128]{2,1,0:T(1,128)S(1)} %get-tuple-element.37), channel_id=1, replica_groups=mesh['groups'=2,'obs'=16] {'obs'}, dimensions={0} | all-to-all | bytes 16384 | tf_op jit(solution)/shard_map/all_to_all | solution.py:434
  (56 shorter events, 9.8 us)
Async XLA Ops:
  1.6 9.9 %collective-permute-start = (f32[104,256]{1,0:T(8,128)S(1)}, f32[104,256]{1,0:T(8,128)S(1)}, u32[]{:S(2)}, u32[]{:S(2)}) collective-permute-start(f32[104,256]{1,0:T(8,128)S(1)} %get-tuple-element.25.refs_0_.bundle), channel_id=1, source_target_pairs={{0,4},{1,5},{2,6},{3,7},{4,0},{5,1},{6,2},{7,3},{8,12},{9,13},{10,... | collective-permute-start | bytes 319496 | tf_op jit(solution)/shard_map/ppermute | solution.py:33
  4.7 8.7 %collective-permute-start.2 = (f32[104,256]{1,0:T(8,128)S(1)}, f32[104,256]{1,0:T(8,128)S(1)}, u32[]{:S(2)}, u32[]{:S(2)}) collective-permute-start(f32[104,256]{1,0:T(8,128)S(1)} %get-tuple-element.25.refs_0_.bundle), channel_id=1, source_target_pairs={{0,8},{1,9},{2,10},{3,11},{4,12},{5,13},{6,14},{7,15},{8,0},{9,1},... | collective-permute-start | bytes 319496 | tf_op jit(solution)/shard_map/ppermute | solution.py:33
  7.3 6.0 %collective-permute-start.3 = (f32[32,256]{1,0:T(8,128)}, f32[32,256]{1,0:T(8,128)S(1)}, u32[]{:S(2)}, u32[]{:S(2)}) collective-permute-start(f32[32,256]{1,0:T(8,128)} %flux.1), channel_id=1, source_target_pairs={{0,12},{1,13},{2,14},{3,15},{4,8},{5,9},{6,10},{7,11},{8,4},{9,5},... | collective-permute-start | bytes 98312 | tf_op jit(solution)/shard_map/ppermute | solution.py:33
  11.5 4.9 %collective-permute-start.1 = (f32[64,256]{1,0:T(8,128)S(1)}, f32[64,256]{1,0:T(8,128)S(1)}, u32[]{:S(2)}, u32[]{:S(2)}) collective-permute-start(f32[64,256]{1,0:T(8,128)S(1)} %shard_map.106.refs_0_), channel_id=1, source_target_pairs={{0,2},{1,3},{2,0},{3,1},{4,6},{5,7},{6,4},{7,5},{8,10},{9,11},{10,... | collective-permute-start | bytes 196616 | tf_op jit(solution)/shard_map/ppermute | solution.py:33
  13.4 5.0 %collective-permute-start.4 = (f32[64,256]{1,0:T(8,128)S(1)}, f32[64,256]{1,0:T(8,128)S(1)}, u32[]{:S(2)}, u32[]{:S(2)}) collective-permute-start(f32[64,256]{1,0:T(8,128)S(1)} %shard_map.107.refs_2_.refs_3_), channel_id=1, source_target_pairs={{0,2},{1,3},{2,0},{3,1},{4,6},{5,7},{6,4},{7,5},{8,10},{9,11},{10,... | collective-permute-start | bytes 196616 | tf_op jit(solution)/shard_map/ppermute | solution.py:33
  14.9 11.3 %collective-permute-start.10 = (f32[216,256]{1,0:T(8,128)S(1)}, f32[216,256]{1,0:T(8,128)S(1)}, u32[]{:S(2)}, u32[]{:S(2)}) collective-permute-start(f32[216,256]{1,0:T(8,128)S(1)} %shard_map.110.refs_1_), channel_id=1, source_target_pairs={{0,2},{1,3},{2,0},{3,1},{4,6},{5,7},{6,4},{7,5},{8,10},{9,11},{10,... | collective-permute-start | bytes 663560 | tf_op jit(solution)/shard_map/ppermute | solution.py:33
  15.5 2.9 %collective-permute-start.5 = (f32[64,256]{1,0:T(8,128)S(1)}, f32[64,256]{1,0:T(8,128)S(1)}, u32[]{:S(2)}, u32[]{:S(2)}) collective-permute-start(f32[64,256]{1,0:T(8,128)S(1)} %shard_map.106.refs_0_), channel_id=1, source_target_pairs={{0,1},{1,0},{2,3},{3,2},{4,5},{5,4},{6,7},{7,6},{8,9},{9,8},{10,11... | collective-permute-start | bytes 196616 | tf_op jit(solution)/shard_map/ppermute | solution.py:33
  15.5 2.9 %collective-permute-start.7 = (f32[64,256]{1,0:T(8,128)S(1)}, f32[64,256]{1,0:T(8,128)S(1)}, u32[]{:S(2)}, u32[]{:S(2)}) collective-permute-start(f32[64,256]{1,0:T(8,128)S(1)} %shard_map.107.refs_2_.refs_3_), channel_id=1, source_target_pairs={{0,1},{1,0},{2,3},{3,2},{4,5},{5,4},{6,7},{7,6},{8,9},{9,8},{10,11... | collective-permute-start | bytes 196616 | tf_op jit(solution)/shard_map/ppermute | solution.py:33
  21.8 6.3 %collective-permute-start.9 = (f32[104,256]{1,0:T(8,128)S(1)}, f32[104,256]{1,0:T(8,128)S(1)}, u32[]{:S(2)}, u32[]{:S(2)}) collective-permute-start(f32[104,256]{1,0:T(8,128)S(1)} %shard_map.109), channel_id=1, source_target_pairs={{0,4},{1,5},{2,6},{3,7},{4,0},{5,1},{6,2},{7,3},{8,12},{9,13},{10,... | collective-permute-start | bytes 319496 | tf_op jit(solution)/shard_map/ppermute | solution.py:33
  22.8 6.9 %collective-permute-start.12 = (f32[64,256]{1,0:T(8,128)S(1)}, f32[64,256]{1,0:T(8,128)S(1)}, u32[]{:S(2)}, u32[]{:S(2)}) collective-permute-start(f32[64,256]{1,0:T(8,128)S(1)} %get-tuple-element.27.refs_0_.refs_2_.refs_3_), channel_id=1, source_target_pairs={{0,8},{1,9},{2,10},{3,11},{4,12},{5,13},{6,14},{7,15},{8,0},{9,1},... | collective-permute-start | bytes 196616 | tf_op jit(solution)/shard_map/ppermute | solution.py:33
  26.0 6.1 %collective-permute-start.13 = (f32[64,256]{1,0:T(8,128)S(1)}, f32[64,256]{1,0:T(8,128)S(1)}, u32[]{:S(2)}, u32[]{:S(2)}) collective-permute-start(f32[64,256]{1,0:T(8,128)S(1)} %get-tuple-element.27.refs_0_.refs_2_.refs_3_), channel_id=1, source_target_pairs={{0,12},{1,13},{2,14},{3,15},{4,8},{5,9},{6,10},{7,11},{8,4},{9,5},... | collective-permute-start | bytes 196616 | tf_op jit(solution)/shard_map/ppermute | solution.py:33
  28.0 6.0 %collective-permute-start.11 = (f32[168,256]{1,0:T(8,128)S(1)}, f32[168,256]{1,0:T(8,128)S(1)}, u32[]{:S(2)}, u32[]{:S(2)}) collective-permute-start(f32[168,256]{1,0:T(8,128)S(1)} %shard_map.111.refs_0_.refs_1_), channel_id=1, source_target_pairs={{0,2},{1,3},{2,0},{3,1},{4,6},{5,7},{6,4},{7,5},{8,10},{9,11},{10,... | collective-permute-start | bytes 516104 | tf_op jit(solution)/shard_map/ppermute | solution.py:33
  32.1 5.0 %collective-permute-start.17 = (f32[128,256]{1,0:T(8,128)S(1)}, f32[128,256]{1,0:T(8,128)S(1)}, u32[]{:S(2)}, u32[]{:S(2)}) collective-permute-start(f32[128,256]{1,0:T(8,128)S(1)} %shard_map.113.refs_2_), channel_id=1, source_target_pairs={{0,2},{1,3},{2,0},{3,1},{4,6},{5,7},{6,4},{7,5},{8,10},{9,11},{10,... | collective-permute-start | bytes 393224 | tf_op jit(solution)/shard_map/ppermute | solution.py:33
  33.4 3.8 %collective-permute-start.16 = (f32[128,256]{1,0:T(8,128)S(1)}, f32[128,256]{1,0:T(8,128)S(1)}, u32[]{:S(2)}, u32[]{:S(2)}) collective-permute-start(f32[128,256]{1,0:T(8,128)S(1)} %shard_map.113.refs_2_), channel_id=1, source_target_pairs={{0,1},{1,0},{2,3},{3,2},{4,5},{5,4},{6,7},{7,6},{8,9},{9,8},{10,11... | collective-permute-start | bytes 393224 | tf_op jit(solution)/shard_map/ppermute | solution.py:33
  33.5 3.8 %collective-permute-start.14 = (f32[408,256]{1,0:T(8,128)S(1)}, f32[408,256]{1,0:T(8,128)S(1)}, u32[]{:S(2)}, u32[]{:S(2)}) collective-permute-start(f32[408,256]{1,0:T(8,128)S(1)} %shard_map.112.refs_0_), channel_id=1, source_target_pairs={{0,1},{1,0},{2,3},{3,2},{4,5},{5,4},{6,7},{7,6},{8,9},{9,8},{10,11... | collective-permute-start | bytes 1253384 | tf_op jit(solution)/shard_map/ppermute | solution.py:33
  34.0 3.2 %collective-permute-start.15 = (f32[168,256]{1,0:T(8,128)S(1)}, f32[168,256]{1,0:T(8,128)S(1)}, u32[]{:S(2)}, u32[]{:S(2)}) collective-permute-start(f32[168,256]{1,0:T(8,128)S(1)} %collective-permute-done.11.refs_1_), channel_id=1, source_target_pairs={{0,1},{1,0},{2,3},{3,2},{4,5},{5,4},{6,7},{7,6},{8,9},{9,8},{10,11... | collective-permute-start | bytes 516104 | tf_op jit(solution)/shard_map/ppermute | solution.py:33
  40.7 6.1 %collective-permute-start.19 = (f32[104,256]{1,0:T(8,128)S(1)}, f32[104,256]{1,0:T(8,128)S(1)}, u32[]{:S(2)}, u32[]{:S(2)}) collective-permute-start(f32[104,256]{1,0:T(8,128)S(1)} %shard_map.117), channel_id=1, source_target_pairs={{0,4},{1,5},{2,6},{3,7},{4,0},{5,1},{6,2},{7,3},{8,12},{9,13},{10,... | collective-permute-start | bytes 319496 | tf_op jit(solution)/shard_map/ppermute | solution.py:33
  41.7 9.1 %collective-permute-start.21 = (f32[72,256]{1,0:T(8,128)S(1)}, f32[72,256]{1,0:T(8,128)S(1)}, u32[]{:S(2)}, u32[]{:S(2)}) collective-permute-start(f32[72,256]{1,0:T(8,128)S(1)} %get-tuple-element.31.refs_0_.refs_2_.refs_3_), channel_id=1, source_target_pairs={{0,8},{1,9},{2,10},{3,11},{4,12},{5,13},{6,14},{7,15},{8,0},{9,1},... | collective-permute-start | bytes 221192 | tf_op jit(solution)/shard_map/ppermute | solution.py:33
  44.0 6.8 %collective-permute-start.22 = (f32[72,256]{1,0:T(8,128)S(1)}, f32[72,256]{1,0:T(8,128)S(1)}, u32[]{:S(2)}, u32[]{:S(2)}) collective-permute-start(f32[72,256]{1,0:T(8,128)S(1)} %get-tuple-element.31.refs_0_.refs_2_.refs_3_), channel_id=1, source_target_pairs={{0,12},{1,13},{2,14},{3,15},{4,8},{5,9},{6,10},{7,11},{8,4},{9,5},... | collective-permute-start | bytes 221192 | tf_op jit(solution)/shard_map/ppermute | solution.py:33
  46.8 6.0 %collective-permute-start.20 = (f32[176,256]{1,0:T(8,128)S(1)}, f32[176,256]{1,0:T(8,128)S(1)}, u32[]{:S(2)}, u32[]{:S(2)}) collective-permute-start(f32[176,256]{1,0:T(8,128)S(1)} %shard_map.118.refs_0_.refs_1_), channel_id=1, source_target_pairs={{0,2},{1,3},{2,0},{3,1},{4,6},{5,7},{6,4},{7,5},{8,10},{9,11},{10,... | collective-permute-start | bytes 540680 | tf_op jit(solution)/shard_map/ppermute | solution.py:33
  50.8 5.2 %collective-permute-start.26 = (f32[144,256]{1,0:T(8,128)S(1)}, f32[144,256]{1,0:T(8,128)S(1)}, u32[]{:S(2)}, u32[]{:S(2)}) collective-permute-start(f32[144,256]{1,0:T(8,128)S(1)} %shard_map.120.refs_2_), channel_id=1, source_target_pairs={{0,2},{1,3},{2,0},{3,1},{4,6},{5,7},{6,4},{7,5},{8,10},{9,11},{10,... | collective-permute-start | bytes 442376 | tf_op jit(solution)/shard_map/ppermute | solution.py:33
  52.2 3.9 %collective-permute-start.25 = (f32[144,256]{1,0:T(8,128)S(1)}, f32[144,256]{1,0:T(8,128)S(1)}, u32[]{:S(2)}, u32[]{:S(2)}) collective-permute-start(f32[144,256]{1,0:T(8,128)S(1)} %shard_map.120.refs_2_), channel_id=1, source_target_pairs={{0,1},{1,0},{2,3},{3,2},{4,5},{5,4},{6,7},{7,6},{8,9},{9,8},{10,11... | collective-permute-start | bytes 442376 | tf_op jit(solution)/shard_map/ppermute | solution.py:33
  52.3 3.9 %collective-permute-start.23 = (f32[368,256]{1,0:T(8,128)S(1)}, f32[368,256]{1,0:T(8,128)S(1)}, u32[]{:S(2)}, u32[]{:S(2)}) collective-permute-start(f32[368,256]{1,0:T(8,128)S(1)} %shard_map.119.refs_0_), channel_id=1, source_target_pairs={{0,1},{1,0},{2,3},{3,2},{4,5},{5,4},{6,7},{7,6},{8,9},{9,8},{10,11... | collective-permute-start | bytes 1130504 | tf_op jit(solution)/shard_map/ppermute | solution.py:33
  52.8 3.3 %collective-permute-start.24 = (f32[176,256]{1,0:T(8,128)S(1)}, f32[176,256]{1,0:T(8,128)S(1)}, u32[]{:S(2)}, u32[]{:S(2)}) collective-permute-start(f32[176,256]{1,0:T(8,128)S(1)} %collective-permute-done.20.refs_1_), channel_id=1, source_target_pairs={{0,1},{1,0},{2,3},{3,2},{4,5},{5,4},{6,7},{7,6},{8,9},{9,8},{10,11... | collective-permute-start | bytes 540680 | tf_op jit(solution)/shard_map/ppermute | solution.py:33
  (5 other events, 25.2 us)

commit v6 on v5

--- a/solution.py
+++ b/solution.py
@@ -106,7 +106,7 @@
     first = Part(
         pile([x, beside, beside], [(count, 0, count), (count + extra, 0, count), (count + extra, count, extra)], paired),
         masks + shift(masks, near), shift(held, both))
-    second = Part(pile([beyond, across], [cut] * 2, x, LONG), shift(masks, far) + shift(masks, both))
+    second = Part(pile([beyond, across], [cut] * 2, x), shift(masks, far) + shift(masks, both))
     few = (pitch - own, at, rows)
     more = held + shift(held, near) + shift(held, far)
     wide = Part(
@@ -170,9 +170,9 @@
         pltpu.make_async_copy(footprints.at[pl.ds(i, 2)], tiles_out.at[pl.ds(i, 2)], sem.at[2 + i // 2])
         for i in range(0, footprints.shape[0], 2)
     ]
+    for c in large:
+        c.start()
     for c in small:
-        c.start()
-    for c in large:
         c.start()
     for c in small:
         c.wait()

time: 70.6 us -> 70.6 us (level)
  no operation moved by 1% of the time
where the time goes in v6:
time: 70.6 us; the launch traced here: 70.3 us
  starting transfers between devices  26 us (37%)
  waiting for transfers between devices  20.4 us (29%)
  Pallas kernels  11.9 us (17%)
  blocking collectives  10.5 us (15%)
  between operations  1.51 us (2%)
    ppermute x28, starting transfers between devices, swap(): return lax.ppermute(x, 'obs', [(i, i ^ mask) for i in range(n)])  26 us
    ppermute x28, waiting for transfers between devices, swap(): return lax.ppermute(x, 'obs', [(i, i ^ mask) for i in range(n)])  20.4 us
    all_to_all x1, blocking collectives, body(): sums = lax.all_to_all(sums, 'obs', 0, 0)  10.5 us
    pallas_call x1, Pallas kernels, body(): call(prepare_kernel, [SMEM] + [HBM] * 4, [square, square, footprints.shap...  3.5 us
    pallas_call x1, Pallas kernels, body(): call(functools.partial(second_kernel, shapes(late)), [VMEM, SMEM] + [VMEM...  2.11 us
    pallas_call x1, Pallas kernels, body(): call(functools.partial(first_kernel, shapes(parts)), [VMEM, SMEM] + [VMEM...  2.04 us
    pallas_call x1, Pallas kernels, body(): call(functools.partial(third_kernel, shapes(early), shapes(late)), [VMEM,...  1.58 us
  transfers between devices with their start and end apart: 28, of which 12 were waited for; matrix products, arithmetic and copies ran while one was open for 0% of the time, Pallas kernels for 9%

profile of v6, /device:TPU:0, one launch (start us, length us, event | category | flops | bytes accessed | tf_op | source)
XLA Modules:
  0.0 70.3 jit_solution(4583603282153204515)
XLA Ops:
  1.6 3.1 %collective-permute-start = (f32[104,256]{1,0:T(8,128)S(1)}, f32[104,256]{1,0:T(8,128)S(1)}, u32[]{:S(2)}, u32[]{:S(2)}) collective-permute-start(f32[104,256]{1,0:T(8,128)S(1)} %get-tuple-element.25.refs_0_.bundle), channel_id=1, source_target_pairs={{0,4},{1,5},{2,6},{3,7},{4,0},{5,1},{6,2},{7,3},{8,12},{9,13},{10,... | collective-permute-start | bytes 319496 | tf_op jit(solution)/shard_map/ppermute | solution.py:33
  4.7 2.6 %collective-permute-start.2 = (f32[104,256]{1,0:T(8,128)S(1)}, f32[104,256]{1,0:T(8,128)S(1)}, u32[]{:S(2)}, u32[]{:S(2)}) collective-permute-start(f32[104,256]{1,0:T(8,128)S(1)} %get-tuple-element.25.refs_0_.bundle), channel_id=1, source_target_pairs={{0,8},{1,9},{2,10},{3,11},{4,12},{5,13},{6,14},{7,15},{8,0},{9,1},... | collective-permute-start | bytes 319496 | tf_op jit(solution)/shard_map/ppermute | solution.py:33
  7.9 3.5 %shard_map.104 = (f32[128,128]{1,0:T(8,128)S(1)}, f32[128,128]{1,0:T(8,128)S(1)}, f32[16,4,128,256]{3,2,1,0:T(8,128)S(1)}) custom-call(s32[1]{0:T(128)S(6)} %copy.11.counts, f32[8]{0:T(128)} %table_in.1, s32[16,128]{1,0:T(8,128)} %week_ids.1, f32[16,128]{1,0:T(8,128)} %observed.1, f32[16,4,128,256]{3,2,1,0:T(8,128)} %footprints.1), custom_call_target="tpu_custom_call" | custom-call | flops 10000 | bytes 16777216 | tf_op jit(solution)/shard_map/pallas_call | solution.py:382
  11.5 1.8 %collective-permute-start.1 = (f32[64,256]{1,0:T(8,128)S(1)}, f32[64,256]{1,0:T(8,128)S(1)}, u32[]{:S(2)}, u32[]{:S(2)}) collective-permute-start(f32[64,256]{1,0:T(8,128)S(1)} %shard_map.106.refs_0_), channel_id=1, source_target_pairs={{0,2},{1,3},{2,0},{3,1},{4,6},{5,7},{6,4},{7,5},{8,10},{9,11},{10,... | collective-permute-start | bytes 196616 | tf_op jit(solution)/shard_map/ppermute | solution.py:33
  13.4 1.5 %collective-permute-start.4 = (f32[64,256]{1,0:T(8,128)S(1)}, f32[64,256]{1,0:T(8,128)S(1)}, u32[]{:S(2)}, u32[]{:S(2)}) collective-permute-start(f32[64,256]{1,0:T(8,128)S(1)} %shard_map.107.refs_2_.refs_3_), channel_id=1, source_target_pairs={{0,2},{1,3},{2,0},{3,1},{4,6},{5,7},{6,4},{7,5},{8,10},{9,11},{10,... | collective-permute-start | bytes 196616 | tf_op jit(solution)/shard_map/ppermute | solution.py:33
  16.4 2.0 %collective-permute-done.4.refs_3_ = f32[64,256]{1,0:T(8,128)S(1)} collective-permute-done((f32[64,256]{1,0:T(8,128)S(1)}, f32[64,256]{1,0:T(8,128)S(1)}, u32[]{:S(2)}, u32[]{:S(2)}) %collective-permute-start.4) | collective-permute-done | bytes 65568 | tf_op jit(solution)/shard_map/ppermute | solution.py:33
  18.5 1.2 %collective-permute-done.8.refs_7_ = f32[64,256]{1,0:T(8,128)S(1)} collective-permute-done((f32[64,256]{1,0:T(8,128)S(1)}, f32[64,256]{1,0:T(8,128)S(1)}, u32[]{:S(2)}, u32[]{:S(2)}) %collective-permute-start.8) | collective-permute-done | bytes 65568 | tf_op jit(solution)/shard_map/ppermute | solution.py:33
  19.7 2.0 %shard_map.108 = (f32[64,256]{1,0:T(8,128)S(1)}, f32[128,128]{1,0:T(8,128)S(1)}) custom-call(s32[4,16]{1,0:T(4,128)S(1)} %bitcast.3, s32[1]{0:T(128)} %bitcast.1.me, f32[16,4,128,256]{3,2,1,0:T(8,128)S(1)} %get-tuple-element.22.tiles, f32[128,128]{1,0:T(8,128)S(1)} %get-tuple-element.23.refs_2_.weights, f32[128,128]{1,0:T(8,128)S(1)} %get-tuple-element.26.observed, ...), custom_call_target="tpu_custom_call" | custom-call | flops 8388608 | bytes 8388608 | tf_op jit(solution)/shard_map/pallas_call | solution.py:405
  22.8 3.1 %collective-permute-start.12 = (f32[64,256]{1,0:T(8,128)S(1)}, f32[64,256]{1,0:T(8,128)S(1)}, u32[]{:S(2)}, u32[]{:S(2)}) collective-permute-start(f32[64,256]{1,0:T(8,128)S(1)} %get-tuple-element.27.refs_0_.refs_2_.refs_3_), channel_id=1, source_target_pairs={{0,8},{1,9},{2,10},{3,11},{4,12},{5,13},{6,14},{7,15},{8,0},{9,1},... | collective-permute-start | bytes 196616 | tf_op jit(solution)/shard_map/ppermute | solution.py:33
  26.2 1.8 %collective-permute-done.9.refs_1_.refs_2_ = f32[104,256]{1,0:T(8,128)S(1)} collective-permute-done((f32[104,256]{1,0:T(8,128)S(1)}, f32[104,256]{1,0:T(8,128)S(1)}, u32[]{:S(2)}, u32[]{:S(2)}) %collective-permute-start.9) | collective-permute-done | bytes 106528 | tf_op jit(solution)/shard_map/ppermute | solution.py:33
  28.0 1.6 %collective-permute-start.11 = (f32[168,256]{1,0:T(8,128)S(1)}, f32[168,256]{1,0:T(8,128)S(1)}, u32[]{:S(2)}, u32[]{:S(2)}) collective-permute-start(f32[168,256]{1,0:T(8,128)S(1)} %shard_map.111.refs_0_.refs_1_), channel_id=1, source_target_pairs={{0,2},{1,3},{2,0},{3,1},{4,6},{5,7},{6,4},{7,5},{8,10},{9,11},{10,... | collective-permute-start | bytes 516104 | tf_op jit(solution)/shard_map/ppermute | solution.py:33
  29.6 2.4 %collective-permute-done.13.refs_1_ = f32[64,256]{1,0:T(8,128)S(1)} collective-permute-done((f32[64,256]{1,0:T(8,128)S(1)}, f32[64,256]{1,0:T(8,128)S(1)}, u32[]{:S(2)}, u32[]{:S(2)}) %collective-permute-start.13) | collective-permute-done | bytes 65568 | tf_op jit(solution)/shard_map/ppermute | solution.py:33
  32.1 1.3 %collective-permute-start.17 = (f32[128,256]{1,0:T(8,128)S(1)}, f32[128,256]{1,0:T(8,128)S(1)}, u32[]{:S(2)}, u32[]{:S(2)}) collective-permute-start(f32[128,256]{1,0:T(8,128)S(1)} %shard_map.113.refs_2_), channel_id=1, source_target_pairs={{0,2},{1,3},{2,0},{3,1},{4,6},{5,7},{6,4},{7,5},{8,10},{9,11},{10,... | collective-permute-start | bytes 393224 | tf_op jit(solution)/shard_map/ppermute | solution.py:33
  34.1 3.0 %collective-permute-done.17.refs_0_ = f32[128,256]{1,0:T(8,128)S(1)} collective-permute-done((f32[128,256]{1,0:T(8,128)S(1)}, f32[128,256]{1,0:T(8,128)S(1)}, u32[]{:S(2)}, u32[]{:S(2)}) %collective-permute-start.17) | collective-permute-done | bytes 131104 | tf_op jit(solution)/shard_map/ppermute | solution.py:33
  38.6 2.1 %shard_map.116 = (f32[72,256]{1,0:T(8,128)S(1)}, f32[96,256]{1,0:T(8,128)S(1)}, f32[128,128]{1,0:T(8,128)S(1)}) custom-call(s32[4,16]{1,0:T(4,128)S(1)} %bitcast.4, s32[1]{0:T(128)} %bitcast.1.me, f32[16,4,128,256]{3,2,1,0:T(8,128)S(1)} %get-tuple-element.22.tiles, f32[128,128]{1,0:T(8,128)S(1)} %get-tuple-element.23.refs_2_.weights, ...), custom_call_target="tpu_custom_call" | custom-call | flops 8388608 | bytes 8388608 | tf_op jit(solution)/shard_map/pallas_call | solution.py:416
  41.7 2.3 %collective-permute-start.21 = (f32[72,256]{1,0:T(8,128)S(1)}, f32[72,256]{1,0:T(8,128)S(1)}, u32[]{:S(2)}, u32[]{:S(2)}) collective-permute-start(f32[72,256]{1,0:T(8,128)S(1)} %get-tuple-element.31.refs_0_.refs_2_.refs_3_), channel_id=1, source_target_pairs={{0,8},{1,9},{2,10},{3,11},{4,12},{5,13},{6,14},{7,15},{8,0},{9,1},... | collective-permute-start | bytes 221192 | tf_op jit(solution)/shard_map/ppermute | solution.py:33
  44.0 1.1 %collective-permute-start.22 = (f32[72,256]{1,0:T(8,128)S(1)}, f32[72,256]{1,0:T(8,128)S(1)}, u32[]{:S(2)}, u32[]{:S(2)}) collective-permute-start(f32[72,256]{1,0:T(8,128)S(1)} %get-tuple-element.31.refs_0_.refs_2_.refs_3_), channel_id=1, source_target_pairs={{0,12},{1,13},{2,14},{3,15},{4,8},{5,9},{6,10},{7,11},{8,4},{9,5},... | collective-permute-start | bytes 221192 | tf_op jit(solution)/shard_map/ppermute | solution.py:33
  45.1 1.6 %collective-permute-done.19.refs_1_.refs_2_ = f32[104,256]{1,0:T(8,128)S(1)} collective-permute-done((f32[104,256]{1,0:T(8,128)S(1)}, f32[104,256]{1,0:T(8,128)S(1)}, u32[]{:S(2)}, u32[]{:S(2)}) %collective-permute-start.19) | collective-permute-done | bytes 106528 | tf_op jit(solution)/shard_map/ppermute | solution.py:33
  46.8 1.2 %collective-permute-start.20 = (f32[176,256]{1,0:T(8,128)S(1)}, f32[176,256]{1,0:T(8,128)S(1)}, u32[]{:S(2)}, u32[]{:S(2)}) collective-permute-start(f32[176,256]{1,0:T(8,128)S(1)} %shard_map.118.refs_0_.refs_1_), channel_id=1, source_target_pairs={{0,2},{1,3},{2,0},{3,1},{4,6},{5,7},{6,4},{7,5},{8,10},{9,11},{10,... | collective-permute-start | bytes 540680 | tf_op jit(solution)/shard_map/ppermute | solution.py:33
  48.0 2.8 %collective-permute-done.21.refs_0_ = f32[72,256]{1,0:T(8,128)S(1)} collective-permute-done((f32[72,256]{1,0:T(8,128)S(1)}, f32[72,256]{1,0:T(8,128)S(1)}, u32[]{:S(2)}, u32[]{:S(2)}) %collective-permute-start.21) | collective-permute-done | bytes 73760 | tf_op jit(solution)/shard_map/ppermute | solution.py:33
  50.8 1.4 %collective-permute-start.26 = (f32[144,256]{1,0:T(8,128)S(1)}, f32[144,256]{1,0:T(8,128)S(1)}, u32[]{:S(2)}, u32[]{:S(2)}) collective-permute-start(f32[144,256]{1,0:T(8,128)S(1)} %shard_map.120.refs_2_), channel_id=1, source_target_pairs={{0,2},{1,3},{2,0},{3,1},{4,6},{5,7},{6,4},{7,5},{8,10},{9,11},{10,... | collective-permute-start | bytes 442376 | tf_op jit(solution)/shard_map/ppermute | solution.py:33
  52.9 3.1 %collective-permute-done.26.refs_0_ = f32[144,256]{1,0:T(8,128)S(1)} collective-permute-done((f32[144,256]{1,0:T(8,128)S(1)}, f32[144,256]{1,0:T(8,128)S(1)}, u32[]{:S(2)}, u32[]{:S(2)}) %collective-permute-start.26) | collective-permute-done | bytes 147488 | tf_op jit(solution)/shard_map/ppermute | solution.py:33
  57.5 1.6 %shard_map.123 = (f32[16,1,128]{2,1,0:T(1,128)S(1)}, f32[32,256]{1,0:T(8,128)S(1)}, f32[32,256]{1,0:T(8,128)S(1)}, f32[16,128]{1,0:T(8,128)S(1)}, f32[16,128]{1,0:T(8,128)S(1)}) custom-call(s32[4,16]{1,0:T(4,128)S(1)} %bitcast.5, s32[1]{0:T(128)} %bitcast.1.me, f32[16,4,128,256]{3,2,1,0:T(8,128)S(1)} %get-tuple-element.22.tiles, ...), custom_call_target="tpu_custom_call" | custom-call | flops 8388608 | bytes 8388608 | tf_op jit(solution)/shard_map/pallas_call | solution.py:427
  59.1 10.5 %all_to_all.5.sums = f32[16,1,128]{2,1,0:T(1,128)S(1)} all-to-all(f32[16,1,128]{2,1,0:T(1,128)S(1)} %get-tuple-element.37), channel_id=1, replica_groups=mesh['groups'=2,'obs'=16] {'obs'}, dimensions={0} | all-to-all | bytes 16384 | tf_op jit(solution)/shard_map/all_to_all | solution.py:434
  (56 shorter events, 9.9 us)
Async XLA Ops:
  1.6 9.8 %collective-permute-start = (f32[104,256]{1,0:T(8,128)S(1)}, f32[104,256]{1,0:T(8,128)S(1)}, u32[]{:S(2)}, u32[]{:S(2)}) collective-permute-start(f32[104,256]{1,0:T(8,128)S(1)} %get-tuple-element.25.refs_0_.bundle), channel_id=1, source_target_pairs={{0,4},{1,5},{2,6},{3,7},{4,0},{5,1},{6,2},{7,3},{8,12},{9,13},{10,... | collective-permute-start | bytes 319496 | tf_op jit(solution)/shard_map/ppermute | solution.py:33
  4.7 8.7 %collective-permute-start.2 = (f32[104,256]{1,0:T(8,128)S(1)}, f32[104,256]{1,0:T(8,128)S(1)}, u32[]{:S(2)}, u32[]{:S(2)}) collective-permute-start(f32[104,256]{1,0:T(8,128)S(1)} %get-tuple-element.25.refs_0_.bundle), channel_id=1, source_target_pairs={{0,8},{1,9},{2,10},{3,11},{4,12},{5,13},{6,14},{7,15},{8,0},{9,1},... | collective-permute-start | bytes 319496 | tf_op jit(solution)/shard_map/ppermute | solution.py:33
  7.3 6.0 %collective-permute-start.3 = (f32[32,256]{1,0:T(8,128)}, f32[32,256]{1,0:T(8,128)S(1)}, u32[]{:S(2)}, u32[]{:S(2)}) collective-permute-start(f32[32,256]{1,0:T(8,128)} %flux.1), channel_id=1, source_target_pairs={{0,12},{1,13},{2,14},{3,15},{4,8},{5,9},{6,10},{7,11},{8,4},{9,5},... | collective-permute-start | bytes 98312 | tf_op jit(solution)/shard_map/ppermute | solution.py:33
  11.5 4.9 %collective-permute-start.1 = (f32[64,256]{1,0:T(8,128)S(1)}, f32[64,256]{1,0:T(8,128)S(1)}, u32[]{:S(2)}, u32[]{:S(2)}) collective-permute-start(f32[64,256]{1,0:T(8,128)S(1)} %shard_map.106.refs_0_), channel_id=1, source_target_pairs={{0,2},{1,3},{2,0},{3,1},{4,6},{5,7},{6,4},{7,5},{8,10},{9,11},{10,... | collective-permute-start | bytes 196616 | tf_op jit(solution)/shard_map/ppermute | solution.py:33
  13.4 5.0 %collective-permute-start.4 = (f32[64,256]{1,0:T(8,128)S(1)}, f32[64,256]{1,0:T(8,128)S(1)}, u32[]{:S(2)}, u32[]{:S(2)}) collective-permute-start(f32[64,256]{1,0:T(8,128)S(1)} %shard_map.107.refs_2_.refs_3_), channel_id=1, source_target_pairs={{0,2},{1,3},{2,0},{3,1},{4,6},{5,7},{6,4},{7,5},{8,10},{9,11},{10,... | collective-permute-start | bytes 196616 | tf_op jit(solution)/shard_map/ppermute | solution.py:33
  14.9 11.3 %collective-permute-start.10 = (f32[216,256]{1,0:T(8,128)S(1)}, f32[216,256]{1,0:T(8,128)S(1)}, u32[]{:S(2)}, u32[]{:S(2)}) collective-permute-start(f32[216,256]{1,0:T(8,128)S(1)} %shard_map.110.refs_1_), channel_id=1, source_target_pairs={{0,2},{1,3},{2,0},{3,1},{4,6},{5,7},{6,4},{7,5},{8,10},{9,11},{10,... | collective-permute-start | bytes 663560 | tf_op jit(solution)/shard_map/ppermute | solution.py:33
  15.5 2.9 %collective-permute-start.5 = (f32[64,256]{1,0:T(8,128)S(1)}, f32[64,256]{1,0:T(8,128)S(1)}, u32[]{:S(2)}, u32[]{:S(2)}) collective-permute-start(f32[64,256]{1,0:T(8,128)S(1)} %shard_map.106.refs_0_), channel_id=1, source_target_pairs={{0,1},{1,0},{2,3},{3,2},{4,5},{5,4},{6,7},{7,6},{8,9},{9,8},{10,11... | collective-permute-start | bytes 196616 | tf_op jit(solution)/shard_map/ppermute | solution.py:33
  15.5 2.9 %collective-permute-start.7 = (f32[64,256]{1,0:T(8,128)S(1)}, f32[64,256]{1,0:T(8,128)S(1)}, u32[]{:S(2)}, u32[]{:S(2)}) collective-permute-start(f32[64,256]{1,0:T(8,128)S(1)} %shard_map.107.refs_2_.refs_3_), channel_id=1, source_target_pairs={{0,1},{1,0},{2,3},{3,2},{4,5},{5,4},{6,7},{7,6},{8,9},{9,8},{10,11... | collective-permute-start | bytes 196616 | tf_op jit(solution)/shard_map/ppermute | solution.py:33
  21.8 6.3 %collective-permute-start.9 = (f32[104,256]{1,0:T(8,128)S(1)}, f32[104,256]{1,0:T(8,128)S(1)}, u32[]{:S(2)}, u32[]{:S(2)}) collective-permute-start(f32[104,256]{1,0:T(8,128)S(1)} %shard_map.109), channel_id=1, source_target_pairs={{0,4},{1,5},{2,6},{3,7},{4,0},{5,1},{6,2},{7,3},{8,12},{9,13},{10,... | collective-permute-start | bytes 319496 | tf_op jit(solution)/shard_map/ppermute | solution.py:33
  22.8 6.8 %collective-permute-start.12 = (f32[64,256]{1,0:T(8,128)S(1)}, f32[64,256]{1,0:T(8,128)S(1)}, u32[]{:S(2)}, u32[]{:S(2)}) collective-permute-start(f32[64,256]{1,0:T(8,128)S(1)} %get-tuple-element.27.refs_0_.refs_2_.refs_3_), channel_id=1, source_target_pairs={{0,8},{1,9},{2,10},{3,11},{4,12},{5,13},{6,14},{7,15},{8,0},{9,1},... | collective-permute-start | bytes 196616 | tf_op jit(solution)/shard_map/ppermute | solution.py:33
  26.0 6.1 %collective-permute-start.13 = (f32[64,256]{1,0:T(8,128)S(1)}, f32[64,256]{1,0:T(8,128)S(1)}, u32[]{:S(2)}, u32[]{:S(2)}) collective-permute-start(f32[64,256]{1,0:T(8,128)S(1)} %get-tuple-element.27.refs_0_.refs_2_.refs_3_), channel_id=1, source_target_pairs={{0,12},{1,13},{2,14},{3,15},{4,8},{5,9},{6,10},{7,11},{8,4},{9,5},... | collective-permute-start | bytes 196616 | tf_op jit(solution)/shard_map/ppermute | solution.py:33
  28.0 6.0 %collective-permute-start.11 = (f32[168,256]{1,0:T(8,128)S(1)}, f32[168,256]{1,0:T(8,128)S(1)}, u32[]{:S(2)}, u32[]{:S(2)}) collective-permute-start(f32[168,256]{1,0:T(8,128)S(1)} %shard_map.111.refs_0_.refs_1_), channel_id=1, source_target_pairs={{0,2},{1,3},{2,0},{3,1},{4,6},{5,7},{6,4},{7,5},{8,10},{9,11},{10,... | collective-permute-start | bytes 516104 | tf_op jit(solution)/shard_map/ppermute | solution.py:33
  32.1 5.0 %collective-permute-start.17 = (f32[128,256]{1,0:T(8,128)S(1)}, f32[128,256]{1,0:T(8,128)S(1)}, u32[]{:S(2)}, u32[]{:S(2)}) collective-permute-start(f32[128,256]{1,0:T(8,128)S(1)} %shard_map.113.refs_2_), channel_id=1, source_target_pairs={{0,2},{1,3},{2,0},{3,1},{4,6},{5,7},{6,4},{7,5},{8,10},{9,11},{10,... | collective-permute-start | bytes 393224 | tf_op jit(solution)/shard_map/ppermute | solution.py:33
  33.4 3.8 %collective-permute-start.16 = (f32[128,256]{1,0:T(8,128)S(1)}, f32[128,256]{1,0:T(8,128)S(1)}, u32[]{:S(2)}, u32[]{:S(2)}) collective-permute-start(f32[128,256]{1,0:T(8,128)S(1)} %shard_map.113.refs_2_), channel_id=1, source_target_pairs={{0,1},{1,0},{2,3},{3,2},{4,5},{5,4},{6,7},{7,6},{8,9},{9,8},{10,11... | collective-permute-start | bytes 393224 | tf_op jit(solution)/shard_map/ppermute | solution.py:33
  33.4 3.8 %collective-permute-start.14 = (f32[408,256]{1,0:T(8,128)S(1)}, f32[408,256]{1,0:T(8,128)S(1)}, u32[]{:S(2)}, u32[]{:S(2)}) collective-permute-start(f32[408,256]{1,0:T(8,128)S(1)} %shard_map.112.refs_0_), channel_id=1, source_target_pairs={{0,1},{1,0},{2,3},{3,2},{4,5},{5,4},{6,7},{7,6},{8,9},{9,8},{10,11... | collective-permute-start | bytes 1253384 | tf_op jit(solution)/shard_map/ppermute | solution.py:33
  34.0 3.2 %collective-permute-start.15 = (f32[168,256]{1,0:T(8,128)S(1)}, f32[168,256]{1,0:T(8,128)S(1)}, u32[]{:S(2)}, u32[]{:S(2)}) collective-permute-start(f32[168,256]{1,0:T(8,128)S(1)} %collective-permute-done.11.refs_1_), channel_id=1, source_target_pairs={{0,1},{1,0},{2,3},{3,2},{4,5},{5,4},{6,7},{7,6},{8,9},{9,8},{10,11... | collective-permute-start | bytes 516104 | tf_op jit(solution)/shard_map/ppermute | solution.py:33
  40.7 6.1 %collective-permute-start.19 = (f32[104,256]{1,0:T(8,128)S(1)}, f32[104,256]{1,0:T(8,128)S(1)}, u32[]{:S(2)}, u32[]{:S(2)}) collective-permute-start(f32[104,256]{1,0:T(8,128)S(1)} %shard_map.117), channel_id=1, source_target_pairs={{0,4},{1,5},{2,6},{3,7},{4,0},{5,1},{6,2},{7,3},{8,12},{9,13},{10,... | collective-permute-start | bytes 319496 | tf_op jit(solution)/shard_map/ppermute | solution.py:33
  41.7 9.2 %collective-permute-start.21 = (f32[72,256]{1,0:T(8,128)S(1)}, f32[72,256]{1,0:T(8,128)S(1)}, u32[]{:S(2)}, u32[]{:S(2)}) collective-permute-start(f32[72,256]{1,0:T(8,128)S(1)} %get-tuple-element.31.refs_0_.refs_2_.refs_3_), channel_id=1, source_target_pairs={{0,8},{1,9},{2,10},{3,11},{4,12},{5,13},{6,14},{7,15},{8,0},{9,1},... | collective-permute-start | bytes 221192 | tf_op jit(solution)/shard_map/ppermute | solution.py:33
  44.0 6.8 %collective-permute-start.22 = (f32[72,256]{1,0:T(8,128)S(1)}, f32[72,256]{1,0:T(8,128)S(1)}, u32[]{:S(2)}, u32[]{:S(2)}) collective-permute-start(f32[72,256]{1,0:T(8,128)S(1)} %get-tuple-element.31.refs_0_.refs_2_.refs_3_), channel_id=1, source_target_pairs={{0,12},{1,13},{2,14},{3,15},{4,8},{5,9},{6,10},{7,11},{8,4},{9,5},... | collective-permute-start | bytes 221192 | tf_op jit(solution)/shard_map/ppermute | solution.py:33
  46.8 6.1 %collective-permute-start.20 = (f32[176,256]{1,0:T(8,128)S(1)}, f32[176,256]{1,0:T(8,128)S(1)}, u32[]{:S(2)}, u32[]{:S(2)}) collective-permute-start(f32[176,256]{1,0:T(8,128)S(1)} %shard_map.118.refs_0_.refs_1_), channel_id=1, source_target_pairs={{0,2},{1,3},{2,0},{3,1},{4,6},{5,7},{6,4},{7,5},{8,10},{9,11},{10,... | collective-permute-start | bytes 540680 | tf_op jit(solution)/shard_map/ppermute | solution.py:33
  50.8 5.2 %collective-permute-start.26 = (f32[144,256]{1,0:T(8,128)S(1)}, f32[144,256]{1,0:T(8,128)S(1)}, u32[]{:S(2)}, u32[]{:S(2)}) collective-permute-start(f32[144,256]{1,0:T(8,128)S(1)} %shard_map.120.refs_2_), channel_id=1, source_target_pairs={{0,2},{1,3},{2,0},{3,1},{4,6},{5,7},{6,4},{7,5},{8,10},{9,11},{10,... | collective-permute-start | bytes 442376 | tf_op jit(solution)/shard_map/ppermute | solution.py:33
  52.2 3.9 %collective-permute-start.25 = (f32[144,256]{1,0:T(8,128)S(1)}, f32[144,256]{1,0:T(8,128)S(1)}, u32[]{:S(2)}, u32[]{:S(2)}) collective-permute-start(f32[144,256]{1,0:T(8,128)S(1)} %shard_map.120.refs_2_), channel_id=1, source_target_pairs={{0,1},{1,0},{2,3},{3,2},{4,5},{5,4},{6,7},{7,6},{8,9},{9,8},{10,11... | collective-permute-start | bytes 442376 | tf_op jit(solution)/shard_map/ppermute | solution.py:33
  52.3 3.9 %collective-permute-start.23 = (f32[368,256]{1,0:T(8,128)S(1)}, f32[368,256]{1,0:T(8,128)S(1)}, u32[]{:S(2)}, u32[]{:S(2)}) collective-permute-start(f32[368,256]{1,0:T(8,128)S(1)} %shard_map.119.refs_0_), channel_id=1, source_target_pairs={{0,1},{1,0},{2,3},{3,2},{4,5},{5,4},{6,7},{7,6},{8,9},{9,8},{10,11... | collective-permute-start | bytes 1130504 | tf_op jit(solution)/shard_map/ppermute | solution.py:33
  52.8 3.3 %collective-permute-start.24 = (f32[176,256]{1,0:T(8,128)S(1)}, f32[176,256]{1,0:T(8,128)S(1)}, u32[]{:S(2)}, u32[]{:S(2)}) collective-permute-start(f32[176,256]{1,0:T(8,128)S(1)} %collective-permute-done.20.refs_1_), channel_id=1, source_target_pairs={{0,1},{1,0},{2,3},{3,2},{4,5},{5,4},{6,7},{7,6},{8,9},{9,8},{10,11... | collective-permute-start | bytes 540680 | tf_op jit(solution)/shard_map/ppermute | solution.py:33
  (5 other events, 25.2 us)
